TPU v7x, 256 devices: a whole 4x4x8 slice. The times are simulated.
256 devices in a mesh: section: 16 (over z, x_lo), sp: 16 (over x_hi, y, core).
Axes of the slice: x: 4 (x_hi: 2, x_lo: 2; x = x_hi * 2 + x_lo), y: 4, z: 8, core: 2. Of those that a mesh axis runs over, the one named last changes fastest.
Arguments:
- slots: bfloat16 [16, 256, 3072], P('section', 'sp'), may hold values from -6 to 6
- patch_of_slot: int32 [16], replicated, may hold values from 0 to 15, each once
- step_of_slot: int32 [16], replicated, may hold values from 0 to 26
- modulation: bfloat16 [16, 28, 3, 3072], P('section'), may hold values from -4 to 4
- w_qkv: bfloat16 [16, 3072, 3, 2048], P('section', None, None, 'sp'), may hold values from -0.109375 to 0.109375
- qk_scale: bfloat16 [16, 2, 128], P('section'), may hold values from 0.25 to 4
- w_mlp_in: bfloat16 [16, 3072, 6144], P('section', None, 'sp'), may hold values from -0.109375 to 0.109375
- w_attn_out: bfloat16 [16, 2048, 3072], P('section', 'sp'), may hold values from -0.125 to 0.125
- w_mlp_out: bfloat16 [16, 6144, 3072], P('section', 'sp'), may hold values from -0.078125 to 0.078125
- kv_cache: bfloat16 [16, 2, 4096, 2048], P('section', None, None, 'sp'), may hold values from -130 to 130
Outputs:
- slots_out: bfloat16 [16, 256, 3072], P('section', 'sp')
- kv_cache_out: bfloat16 [16, 2, 4096, 2048], P('section', None, None, 'sp')
Inputs may be any that keep to these rules, and one draw needn't show every extreme that they name: `patch_of_slot`: each patch id names exactly one slot.
All inputs are finite; a program needn't handle non-finite values.
Results may differ from a plain program's by a relative error of at most 0.012.
The roundings to bfloat16 on the way count: a program that leaves them out, or rounds other values in their place, can miss the bound.
Values may be sent and summed in bfloat16 or wider, within the bound.
No kernel may reach another device: no remote copies, remote signals or barrier semaphores. Data moves between devices by JAX's collectives and lax.ppermute only.
A program may use at most 128 MiB of HBM per device.

v0:
```python
import math

import jax
import jax.numpy as jnp
from jax import lax
from jax.sharding import PartitionSpec as P

HD = 128
ROUNDS = 2


def shifted_2(x, axis, by):
    length = lax.axis_size(axis)
    return lax.ppermute(x, axis, [(i, (i + by) % length) for i in range(length)])


def slot_labels(patch_of_slot, step_of_slot, section_id, sections, round_id):
    anchor = section_id - round_id
    wrapped = (anchor < 0).astype(jnp.int32)
    anchor = anchor + wrapped * sections
    patch_id = lax.dynamic_index_in_dim(patch_of_slot, anchor, 0, keepdims=False)
    timestep = lax.dynamic_index_in_dim(step_of_slot, anchor, 0, keepdims=False) + wrapped
    return (patch_id, timestep)


def modulate(slot, table, timestep):
    factors = lax.dynamic_index_in_dim(table, timestep, 0, keepdims=False).astype(jnp.float32)
    wide = slot.astype(jnp.float32)
    center = wide - jnp.mean(wide, axis=-1, keepdims=True)
    spread = jnp.mean(center * center, axis=-1, keepdims=True)
    normed = (center * lax.rsqrt(spread + 1e-06) * (1.0 + factors[1]) + factors[0]).astype(
        jnp.bfloat16
    )
    return (normed, factors[2])


def head_norm(part, gain):
    rows = part.shape[0]
    wide = part.astype(jnp.float32).reshape(rows, -1, HD)
    power = jnp.mean(wide * wide, axis=-1, keepdims=True)
    normed = wide * lax.rsqrt(power + 1e-06) * gain.astype(jnp.float32)
    return normed.astype(jnp.bfloat16).reshape(rows, -1)


def mix(normed, patch_id, keys, values, qkv_weight, norm_gain, inner_weight):
    patch_rows = normed.shape[0]
    projected = jnp.einsum(
        "rd,dce->rce", normed, qkv_weight, preferred_element_type=jnp.float32
    ).astype(jnp.bfloat16)
    query_normed = head_norm(projected[:, 0], norm_gain[0])
    key_normed = head_norm(projected[:, 1], norm_gain[1])
    first_row = patch_id * patch_rows
    keys = lax.dynamic_update_slice_in_dim(keys, key_normed, first_row, 0)
    values = lax.dynamic_update_slice_in_dim(values, projected[:, 2], first_row, 0)
    local_heads = qkv_weight.shape[2] // HD
    queries = query_normed.reshape(patch_rows, local_heads, HD)
    key_heads = keys.reshape(keys.shape[0], local_heads, HD)
    value_heads = values.reshape(values.shape[0], local_heads, HD)
    scores = jnp.einsum(
        "rhd,thd->hrt", queries, key_heads, preferred_element_type=jnp.float32
    ) / math.sqrt(HD)
    shifted = jnp.exp(scores - jnp.max(scores, axis=-1, keepdims=True))
    weights = (shifted / jnp.sum(shifted, axis=-1, keepdims=True)).astype(jnp.bfloat16)
    attention = jnp.einsum(
        "hrt,thd->rhd", weights, value_heads, preferred_element_type=jnp.float32
    ).astype(jnp.bfloat16)
    attention = attention.reshape(patch_rows, local_heads * HD)
    activity = jax.nn.gelu(
        jnp.dot(normed, inner_weight, preferred_element_type=jnp.float32), approximate=True
    ).astype(jnp.bfloat16)
    return (attention, activity, keys, values)


def shards(
    slots,
    patch_of_slot,
    step_of_slot,
    modulation,
    w_qkv,
    qk_scale,
    w_mlp_in,
    w_attn_out,
    w_mlp_out,
    kv_cache,
):
    sections = lax.axis_size("section")
    section_id = lax.axis_index("section")
    table = modulation[0]
    qkv_weight = w_qkv[0]
    norm_gain = qk_scale[0]
    inner_weight = w_mlp_in[0]
    attention_weight = w_attn_out[0]
    outer_weight = w_mlp_out[0]
    keys = kv_cache[0, 0]
    values = kv_cache[0, 1]
    current = slots[0]
    for round_id in range(ROUNDS):
        patch_id, timestep = slot_labels(
            patch_of_slot, step_of_slot, section_id, sections, round_id
        )
        normed, gate = modulate(current, table, timestep)
        gathered = lax.all_gather(normed, "sp", axis=0, tiled=True)
        attention, activity, keys, values = mix(
            gathered, patch_id, keys, values, qkv_weight, norm_gain, inner_weight
        )
        summed = lax.psum_scatter(
            jnp.dot(attention, attention_weight, preferred_element_type=jnp.float32)
            + jnp.dot(activity, outer_weight, preferred_element_type=jnp.float32),
            "sp",
            scatter_dimension=0,
            tiled=True,
        )
        current = (current.astype(jnp.float32) + gate * summed).astype(jnp.bfloat16)
        current = shifted_2(current, "section", 1)
    return (current[None], jnp.stack([keys, values])[None])


def solution(mesh):
    return jax.shard_map(
        shards,
        mesh=mesh,
        in_specs=(
            P("section", "sp", None),
            P(),
            P(),
            P("section", None, None, None),
            P("section", None, None, "sp"),
            P("section", None, None),
            P("section", None, "sp"),
            P("section", "sp", None),
            P("section", "sp", None),
            P("section", None, None, "sp"),
        ),
        out_specs=(P("section", "sp", None), P("section", None, None, "sp")),
        check_vma=False,
    )
```

profile of v0, /device:TPU:8, one launch (start us, length us, event | category | flops | bytes accessed | tf_op | source)
XLA Modules:
  0.0 358.9 jit_solution(12189687350472921491)
XLA Ops:
  7.2 0.0 copy-start
  7.2 0.0 all-gather.3.cloned.1.call-start
  7.2 1.4 fusion.105
  10.0 1.0 convert_reduce_fusion.1
  11.0 1.1 fusion.56
  12.1 1.7 dynamic-slice_convert_fusion
  13.8 1.6 fusion.59
  15.4 0.0 all-gather.3.cloned.1.call-update
  15.5 0.0 reduce-scatter.3.cloned.1.call-start
  15.5 1.3 fusion.104
  17.5 0.0 copy-start.11
  17.5 4.4 %copy.12 = bf16[3072,3,128]{0,2,1:T(8,128)(2,1)} copy(bf16[3072,3,128]{2,0,1:T(8,128)(2,1)} %bitcast.123) | data formatting | bytes 4718592 | tf_op jit(solution)/shard_map/squeeze | solution.py:89
  21.9 0.0 copy-done.11
  21.9 0.6 bitcast_convert_fusion.1
  22.4 2.6 slice_bitcast_fusion
  25.1 44.4 %all-gather.3.cloned.1.call-done = bf16[256,3072]{1,0:T(8,128)(2,1)} async-done(((bf16[16,3072]{1,0:T(8,128)(2,1)}), bf16[256,3072]{1,0:T(8,128)(2,1)}) %all-gather.3.cloned.1.call-update) | async-done | bytes 1572880 | tf_op jit(solution)/shard_map/all_gather | solution.py:102
  69.5 3.0 fusion.108
  72.5 0.0 copy-start.4
  72.6 0.6 add_rsqrt_fusion.3
  73.2 0.0 copy-done.4
  73.2 0.0 copy-done.9
  73.2 0.1 fusion.85
  73.3 0.7 copy.14
  74.0 0.1 copy.13
  74.1 1.5 constant_dynamic-update-slice_fusion.2
  75.6 0.0 copy-done.7
  75.6 1.7 fusion.106
  77.3 1.9 copy-done.1
  79.3 0.7 fusion
  80.0 6.6 %fusion.13 = f32[256,3072]{1,0:T(8,128)} fusion(bf16[4096,128]{1,0:T(8,128)(2,1)} %get-tuple-element.27, f32[256,4096]{1,0:T(8,128)} %copy-done.1, f32[256]{0:T(256)S(1)} %fusion, f32[256]{0:T(256)S(1)} %get-tuple-element.22, bf16[1,128,3072]{2,1,0:T(8,128)(2,1)} %param.17), kind=kOutput, calls=%fused_computation.22 | convolution fusion | flops 472940544 | bytes 9177088 | tf_op jit(solution)/shard_map/dot_general | solution.py:107
  86.6 0.0 copy-done
  86.6 6.7 %convolution_add_fusion.1 = f32[256,3072]{1,0:T(8,128)} fusion(f32[256,3072]{1,0:T(8,128)} %fusion.13, bf16[1,384,3072]{2,1,0:T(8,128)(2,1)S(1)} %copy-done, bf16[256,3072]{1,0:T(8,128)(2,1)} %all-gather.3.cloned.1.call-done, bf16[1,3072,384]{2,1,0:T(8,128)(2,1)} %param.16), kind=kOutput, calls=%fused_computation.7 | convolution fusion | flops 1209630720 | bytes 12582912 | tf_op jit(solution)/shard_map/dot_general | solution.py:108
  93.3 0.0 reduce-scatter.3.cloned.1.call-update
  93.3 0.0 all-gather.5.cloned.1.call-start
  93.3 82.0 %reduce-scatter.3.cloned.1.call-done = f32[16,3072]{1,0:T(8,128)} async-done(((f32[256,3072]{1,0:T(8,128)}), f32[16,3072]{1,0:T(8,128)}) %reduce-scatter.3.cloned.1.call-update) | async-done | bytes 196624 | tf_op jit(solution)/shard_map/reduce_scatter | solution.py:106
  175.3 1.0 fusion.60
  176.3 0.6 collective-permute-start
  176.9 6.2 %collective-permute-done = bf16[16,3072]{1,0:T(8,128)(2,1)S(1)} collective-permute-done((bf16[16,3072]{1,0:T(8,128)(2,1)S(1)}, bf16[16,3072]{1,0:T(8,128)(2,1)S(1)}, u32[]{:S(2)}, u32[]{:S(2)}) %collective-permute-start) | collective-permute-done | bytes 98336 | tf_op jit(solution)/shard_map/ppermute | solution.py:14
  183.1 0.1 convert_reduce_fusion
  183.2 0.2 fusion.52
  183.5 0.8 fusion.55
  184.2 0.0 all-gather.5.cloned.1.call-update
  184.2 0.2 reduce-scatter.5.cloned.1.call-start
  185.1 49.3 %all-gather.5.cloned.1.call-done = bf16[256,3072]{1,0:T(8,128)(2,1)} async-done(((bf16[16,3072]{1,0:T(8,128)(2,1)}), bf16[256,3072]{1,0:T(8,128)(2,1)}) %all-gather.5.cloned.1.call-update) | async-done | bytes 1572880 | tf_op jit(solution)/shard_map/all_gather | solution.py:102
  234.4 3.0 fusion.109
  237.4 0.0 copy-start.5
  237.4 0.6 slice_bitcast_fusion.2
  238.1 0.7 fusion.82
  238.8 1.6 copy.17
  240.4 1.6 copy.16
  241.9 0.9 constant_dynamic-update-slice_fusion
  242.8 1.5 constant_dynamic-update-slice_fusion.1
  244.3 1.7 fusion.107
  246.0 1.9 copy-done.2
  247.9 0.7 fusion.1
  248.6 6.6 %fusion.15 = f32[256,3072]{1,0:T(8,128)} fusion(bf16[4096,128]{1,0:T(8,128)(2,1)} %constant_dynamic-update-slice_fusion.1, f32[256,4096]{1,0:T(8,128)} %copy-done.2, f32[256]{0:T(256)S(1)} %fusion.1, f32[256]{0:T(256)S(1)} %get-tuple-element.24, bf16[1,128,3072]{2,1,0:T(8,128)(2,1)} %param.17), kind=kOutput, calls=%fused_computation.24 | convolution fusion | flops 472940544 | bytes 9177088 | tf_op jit(solution)/shard_map/dot_general | solution.py:107
  255.2 6.7 %convolution_add_fusion = f32[256,3072]{1,0:T(8,128)} fusion(f32[256,3072]{1,0:T(8,128)} %fusion.15, bf16[1,384,3072]{2,1,0:T(8,128)(2,1)S(1)} %copy-done, bf16[256,3072]{1,0:T(8,128)(2,1)} %all-gather.5.cloned.1.call-done, bf16[1,3072,384]{2,1,0:T(8,128)(2,1)} %param.16), kind=kOutput, calls=%fused_computation.6 | convolution fusion | flops 1209630720 | bytes 12582912 | tf_op jit(solution)/shard_map/dot_general | solution.py:108
  261.9 0.0 reduce-scatter.5.cloned.1.call-update
  261.9 82.0 %reduce-scatter.5.cloned.1.call-done = f32[16,3072]{1,0:T(8,128)} async-done(((f32[256,3072]{1,0:T(8,128)}), f32[16,3072]{1,0:T(8,128)}) %reduce-scatter.5.cloned.1.call-update) | async-done | bytes 196624 | tf_op jit(solution)/shard_map/reduce_scatter | solution.py:106
  344.0 1.0 fusion.61
  344.9 0.6 collective-permute-start.1
  345.5 2.7 maximum_bitcast_fusion
  348.3 3.5 collective-permute-done.1
  351.7 0.6 copy.23
  (27 shorter events, 0.2 us)
Async XLA Ops:
  7.2 79.4 %copy-start = (bf16[1,384,3072]{2,1,0:T(8,128)(2,1)S(1)}, bf16[1,384,3072]{2,1,0:T(8,128)(2,1)}, u32[]{:S(2)}) copy-start(bf16[1,384,3072]{2,1,0:T(8,128)(2,1)} %param.18) | copy-start | bytes 7077892
  7.2 62.3 %all-gather.3.cloned.1.call-start = ((), (), s32[]{:S(2)}) async-start(), calls=%async_computation.2 | async-start | bytes 1671168 | tf_op jit(solution)/shard_map/all_gather | solution.py:102
  15.5 159.9 %reduce-scatter.3.cloned.1.call-start = ((), (), s32[]{:S(2)}) async-start(), calls=%async_computation.3 | async-start | bytes 3342336 | tf_op jit(solution)/shard_map/reduce_scatter | solution.py:106
  17.5 4.4 %copy-start.11 = (bf16[1,2,128]{2,1,0:T(2,128)(2,1)S(1)}, bf16[1,2,128]{2,1,0:T(2,128)(2,1)}, u32[]{:S(2)}) copy-start(bf16[1,2,128]{2,1,0:T(2,128)(2,1)} %param.15) | copy-start | bytes 1540
  22.4 53.2 %copy-start.7 = (f32[128]{0:T(128)}, f32[128]{0:T(128)S(1)}, u32[]{:S(2)}) copy-start(f32[128]{0:T(128)S(1)} %get-tuple-element.20) | copy-start | bytes 1540
  69.5 3.7 %copy-start.9 = (f32[128]{0:T(128)S(1)}, f32[128]{0:T(128)}, u32[]{:S(2)}) copy-start(f32[128]{0:T(128)} %get-tuple-element.21) | copy-start | bytes 1540
  72.5 0.7 copy-start.4
  77.3 1.9 copy-start.1
  93.3 82.1 %copy-start.3 = (bf16[1,16,3072]{2,1,0:T(8,128)(2,1)S(1)}, bf16[1,16,3072]{2,1,0:T(8,128)(2,1)}, u32[]{:S(2)}) copy-start(bf16[1,16,3072]{2,1,0:T(8,128)(2,1)} %param.10) | copy-start | bytes 294916
  93.3 83.6 %copy-start.6 = (f32[1,1,3,3072]{3,1,2,0:T(1,128)S(1)}, f32[1,1,3,3072]{3,1,2,0:T(1,128)}, u32[]{:S(2)}) copy-start(f32[1,1,3,3072]{3,1,2,0:T(1,128)} %get-tuple-element.8) | copy-start | bytes 110596
  93.3 141.1 %all-gather.5.cloned.1.call-start = ((), (), s32[]{:S(2)}) async-start(), calls=%async_computation.4 | async-start | bytes 1671168 | tf_op jit(solution)/shard_map/all_gather | solution.py:102
  176.3 6.8 %collective-permute-start = (bf16[16,3072]{1,0:T(8,128)(2,1)S(1)}, bf16[16,3072]{1,0:T(8,128)(2,1)S(1)}, u32[]{:S(2)}, u32[]{:S(2)}) collective-permute-start(bf16[16,3072]{1,0:T(8,128)(2,1)S(1)} %fusion.60), channel_id=1, source_target_pairs={{0,16},{16,32},{32,48},{48,64},{64,80},{80,96},{96,112},{112,128},... | collective-permute-start | bytes 294920 | tf_op jit(solution)/shard_map/ppermute | solution.py:14
  184.2 159.7 %reduce-scatter.5.cloned.1.call-start = ((), (), s32[]{:S(2)}) async-start(), calls=%async_computation.5 | async-start | bytes 3342336 | tf_op jit(solution)/shard_map/reduce_scatter | solution.py:106
  185.0 53.1 %copy-start.10 = (f32[128]{0:T(128)S(1)}, f32[128]{0:T(128)}, u32[]{:S(2)}) copy-start(f32[128]{0:T(128)} %get-tuple-element.21) | copy-start | bytes 1540
  185.0 59.2 %copy-start.8 = (f32[128]{0:T(128)S(1)}, f32[128]{0:T(128)}, u32[]{:S(2)}) copy-start(f32[128]{0:T(128)} %copy-done.7) | copy-start | bytes 1540
  237.4 0.7 copy-start.5
  246.0 1.9 copy-start.2
  344.9 6.8 %collective-permute-start.1 = (bf16[16,3072]{1,0:T(8,128)(2,1)S(1)}, bf16[16,3072]{1,0:T(8,128)(2,1)S(1)}, u32[]{:S(2)}, u32[]{:S(2)}) collective-permute-start(bf16[16,3072]{1,0:T(8,128)(2,1)S(1)} %fusion.61), channel_id=1, source_target_pairs={{0,16},{16,32},{32,48},{48,64},{64,80},{80,96},{96,112},{112,128},... | collective-permute-start | bytes 294920 | tf_op jit(solution)/shard_map/ppermute | solution.py:14
Sparse Core Ops, SparseCore 0:
  15.6 53.8 all-gather.2
  93.4 81.8 reduce-scatter.2
  184.4 49.9 all-gather.4
  262.1 81.8 reduce-scatter.4
where the time goes:
time: 360 us; the launch traced here: 359 us
  waiting for transfers between devices  267 us (74%)
  matrix products  36 us (10%)
  local copies, waits for them, and re-layouts  22.7 us (6%)
  between operations  16.5 us (5%)
  other arithmetic  14.8 us (4%)
    reduce_scatter x2, waiting for transfers between devices, shards(): lax.psum_scatter(jnp.dot(attention, attention_weight, preferred_element_t...  164 us
    all_gather x2, waiting for transfers between devices, shards(): gathered = lax.all_gather(normed, 'sp', axis=0, tiled=True)  93.7 us
    dot_general x2, matrix products, shards(): jnp.dot(activity, outer_weight, preferred_element_type=jnp.float32)  13.4 us
    dot_general x2, matrix products, shards(): jnp.dot(attention, attention_weight, preferred_element_type=jnp.float32)  13.2 us
    ppermute x2, waiting for transfers between devices, shifted_2(): lax.ppermute(x, axis, [(i, (i + by) % length) for i in range(length)])  9.66 us
  transfers between devices with their start and end apart: 6, of which 6 were waited for; matrix products, arithmetic and copies ran while one was open for 3% of the time, Pallas kernels for 0%

commit v1 on v0

v1 whole, which is shorter than its diff:
```python
import math

import jax
import jax.numpy as jnp
from jax import lax
from jax.experimental import pallas as pl
from jax.experimental.pallas import tpu as pltpu
from jax.sharding import PartitionSpec as P

HD = 128
D = 3072
ROWS = 256
TOKENS = 4096
HIDDEN = 384
PIECE = 16
PAIR = 32
HALF = 128
SECTIONS = 16
SPAN = 16
BF = jnp.bfloat16
F32 = jnp.float32
MIB = 1 << 20


def send_core(x):
    return lax.ppermute(x, "sp", [(i, i ^ 1) for i in range(SPAN)])


def send_y(x, by):
    return lax.ppermute(
        x, "sp", [(i, (i & 9) | ((((i >> 1) & 3) + by) % 4) << 1) for i in range(SPAN)]
    )


def send_x(x):
    return lax.ppermute(x, "sp", [(i, i ^ 8) for i in range(SPAN)])


def send_on(x, flip):
    pairs = []
    for s in range(SECTIONS):
        for i in range(SPAN):
            pairs.append((s * SPAN + i, ((s + 1) % SECTIONS) * SPAN + (i ^ flip)))
    return lax.ppermute(x, ("section", "sp"), pairs)


def in_vmem(x):
    return pltpu.with_memory_space_constraint(x, pltpu.VMEM)


def local_call(body, outs, args, scratch=(), limit=16, flops=0, moved=0, name=None, aliases=None):
    specs = []
    given = []
    for kind, arg in args:
        if kind == "smem":
            specs.append(pl.BlockSpec(memory_space=pltpu.SMEM))
            given.append(arg)
        elif kind == "any":
            specs.append(pl.BlockSpec(memory_space=pl.ANY))
            given.append(arg)
        else:
            specs.append(pl.BlockSpec(memory_space=pltpu.VMEM))
            given.append(in_vmem(arg))
    out_specs = []
    out_shape = []
    for kind, shape, dtype in outs:
        if kind == "any":
            out_specs.append(pl.BlockSpec(memory_space=pl.ANY))
            out_shape.append(jax.ShapeDtypeStruct(shape, dtype))
        else:
            out_specs.append(pl.BlockSpec(memory_space=pltpu.VMEM))
            out_shape.append(pltpu.VMEM(shape, dtype))
    return pl.pallas_call(
        body,
        out_shape=out_shape,
        in_specs=specs,
        out_specs=out_specs,
        scratch_shapes=list(scratch),
        input_output_aliases=aliases or {},
        compiler_params=pltpu.CompilerParams(vmem_limit_bytes=limit * MIB),
        cost_estimate=pl.CostEstimate(flops=flops, bytes_accessed=moved, transcendentals=0),
        name=name,
    )(*given)


def layer_norm(wide, factors):
    center = wide - jnp.mean(wide, axis=-1, keepdims=True)
    spread = jnp.mean(center * center, axis=-1, keepdims=True)
    shift = factors[0:1, :].astype(F32)
    scale = factors[1:2, :].astype(F32)
    return (center * lax.rsqrt(spread + 1e-06) * (1.0 + scale) + shift).astype(BF)


def start_body(where, own, other, factors, normed, kept):
    xh = where[1]
    mine = pl.multiple_of(xh * PIECE, PIECE)
    theirs = pl.multiple_of((1 - xh) * PIECE, PIECE)
    kept[pl.ds(mine, PIECE), :] = own[...]
    kept[pl.ds(theirs, PIECE), :] = other[...]
    table = factors[...]
    normed[pl.ds(mine, PIECE), :] = layer_norm(own[...].astype(F32), table)
    normed[pl.ds(theirs, PIECE), :] = layer_norm(other[...].astype(F32), table)


def head_norm(part, gain):
    wide = part.astype(F32)
    power = jnp.mean(wide * wide, axis=-1, keepdims=True)
    return (wide * lax.rsqrt(power + 1e-06) * gain.astype(F32)).astype(BF)


def gelu(x):
    return jax.nn.gelu(x, approximate=True)


def block_body(
    where, n0, n1, n2, n3, s0, s1, s2, s3, w1, w2, gains, cache, new_cache, joined, partial,
    rows, kv, scores, sems,
):
    patch = pl.multiple_of(where[0] * ROWS, ROWS)
    xh, y, core = where[1], where[2], where[3]
    reads = [
        pltpu.make_async_copy(cache.at[i], kv.at[i], sems.at[i]) for i in range(2)
    ]
    for r in reads:
        r.start()
    for i, piece in enumerate((n0, n1, n2, n3, s0, s1, s2, s3)):
        rows[i * PAIR:(i + 1) * PAIR, :] = piece[...]
    h = rows[...]
    qk = jnp.dot(h, w1[:, 0:256], preferred_element_type=F32).astype(BF)
    vm = jnp.dot(h, w1[:, 256:512], preferred_element_type=F32)
    mm = jnp.dot(h, w1[:, 512:768], preferred_element_type=F32)
    query = head_norm(qk[:, :HD], gains[0:1, :])
    key = head_norm(qk[:, HD:], gains[1:2, :])
    value = vm[:, :HD].astype(BF)
    joined[:, HD:2 * HD] = gelu(vm[:, HD:]).astype(BF)
    joined[:, 2 * HD:] = gelu(mm).astype(BF)
    for r in reads:
        r.wait()
    for dc in range(2):
        for dy in range(4):
            for x in range(2):
                at = (dc * 4 + dy) * PAIR + x * PIECE
                row = x * HALF + lax.rem(y + dy, 4) * PAIR + jnp.where(core == dc, 0, PIECE)
                to = pl.multiple_of(patch + row, PIECE)
                kv[0, pl.ds(to, PIECE), :] = key[at:at + PIECE, :]
                kv[1, pl.ds(to, PIECE), :] = value[at:at + PIECE, :]
    writes = [
        pltpu.make_async_copy(
            kv.at[i, pl.ds(patch, ROWS)], new_cache.at[i, pl.ds(patch, ROWS)], sems.at[2 + i]
        )
        for i in range(2)
    ]
    for w in writes:
        w.start()
    step = 512
    top = None
    for j in range(TOKENS // step):
        s = lax.dot_general(
            query, kv[0, j * step:(j + 1) * step, :], (((1,), (1,)), ((), ())),
            preferred_element_type=F32,
        ) * (1.0 / math.sqrt(HD))
        scores[:, j * step:(j + 1) * step] = s
        best = jnp.max(s, axis=-1, keepdims=True)
        top = best if top is None else jnp.maximum(top, best)
    total = None
    mixed = None
    for j in range(TOKENS // step):
        e = jnp.exp(scores[:, j * step:(j + 1) * step] - top)
        t = jnp.sum(e, axis=-1, keepdims=True)
        m = jnp.dot(
            e.astype(BF), kv[1, j * step:(j + 1) * step, :], preferred_element_type=F32
        )
        total = t if total is None else total + t
        mixed = m if mixed is None else mixed + m
    joined[:, 0:HD] = (mixed / total).astype(BF)
    theirs = joined[HALF:, :]
    for j in range(D // 256):
        partial[:, j * 256:(j + 1) * 256] = jnp.dot(
            theirs, w2[:, j * 256:(j + 1) * 256], preferred_element_type=F32
        ).astype(BF)
    for w in writes:
        w.wait()


def own_body(joined, w2, partial):
    mine = joined[:HALF, :]
    for j in range(D // 256):
        partial[:, j * 256:(j + 1) * 256] = jnp.dot(
            mine, w2[:, j * 256:(j + 1) * 256], preferred_element_type=F32
        )


def pair_body(mine, came, o0, o1, o2, o3):
    o0[...] = mine[0:PAIR, :] + came[0:PAIR, :].astype(F32)
    for i, o in ((1, o1), (2, o2), (3, o3)):
        a, b = i * PAIR, (i + 1) * PAIR
        o[...] = (mine[a:b, :] + came[a:b, :].astype(F32)).astype(BF)


def column_body(mine, r1, r2, r3, factors, out):
    total = mine[...] + r1[...].astype(F32) + (r2[...].astype(F32) + r3[...].astype(F32))
    out[...] = (factors[2:3, :].astype(F32) * total).astype(BF)


def last_column_body(where, mine, r1, r2, r3, factors, here, there):
    xh = where[1]
    gate = factors[2:3, :].astype(F32)
    for out, at in ((here, xh), (there, 1 - xh)):
        rows = pl.ds(pl.multiple_of(at * PIECE, PIECE), PIECE)
        total = mine[rows, :] + r1[rows, :].astype(F32)
        total = total + (r2[rows, :].astype(F32) + r3[rows, :].astype(F32))
        out[...] = (gate * total).astype(BF)


def next_body(where, kept, p0, p1, factors, normed, own):
    xh = where[1]
    new = (kept[...].astype(F32) + (p0[...].astype(F32) + p1[...].astype(F32))).astype(BF)
    wide = new.astype(F32)
    normed[...] = layer_norm(wide, factors[...])
    own[...] = jnp.where(xh == 0, new[:PIECE, :], new[PIECE:, :])


def final_body(kept, p0, p1, out):
    out[...] = (kept[...].astype(F32) + (p0[...].astype(F32) + p1[...].astype(F32))).astype(BF)


def block(normed, where, w1, w2, gains, cache):
    core_parts = [send_core(normed)]
    parts = [normed] + [send_y(normed, -dy) for dy in (1, 2, 3)]
    core_parts += [send_core(p) for p in parts[1:]]
    new_cache, joined, partial = local_call(
        block_body,
        [("any", cache.shape, BF), ("vmem", (ROWS, 4 * HD), BF), ("vmem", (HALF, D), BF)],
        [("smem", where)] + [("vmem", p) for p in parts + core_parts]
        + [("vmem", w1), ("vmem", w2), ("vmem", gains), ("any", cache)],
        scratch=[
            pltpu.VMEM((ROWS, D), BF),
            pltpu.VMEM((2, TOKENS, HD), BF),
            pltpu.VMEM((ROWS, TOKENS), F32),
            pltpu.SemaphoreType.DMA((4,)),
        ],
        limit=24,
        flops=2_200_000_000,
        moved=12_000_000,
        name="block",
        aliases={12: 0},
    )
    came = send_core(partial)
    (mine,) = local_call(
        own_body,
        [("vmem", (HALF, D), F32)],
        [("vmem", joined), ("vmem", w2)],
        flops=400_000_000,
        moved=4_700_000,
        name="own_half",
    )
    o0, o1, o2, o3 = local_call(
        pair_body,
        [("vmem", (PAIR, D), F32)] + [("vmem", (PAIR, D), BF)] * 3,
        [("vmem", mine), ("vmem", came)],
        flops=400_000,
        moved=3_000_000,
        name="pair_sum",
    )
    return (o0, send_y(o1, 1), send_y(o2, 2), send_y(o3, 3)), new_cache


def labels(patch_of_slot, step_of_slot, section_id, round_id):
    anchor = section_id - round_id
    wrapped = (anchor < 0).astype(jnp.int32)
    anchor = anchor + wrapped * SECTIONS
    patch_id = lax.dynamic_index_in_dim(patch_of_slot, anchor, 0, keepdims=False)
    timestep = lax.dynamic_index_in_dim(step_of_slot, anchor, 0, keepdims=False) + wrapped
    return patch_id, timestep


def shards(
    slots,
    patch_of_slot,
    step_of_slot,
    modulation,
    w_qkv,
    qk_scale,
    w_mlp_in,
    w_attn_out,
    w_mlp_out,
    kv_cache,
):
    section_id = lax.axis_index("section")
    place = lax.axis_index("sp")
    xh, y, core = place // 8, (place // 2) % 4, place % 2
    own = slots[0]
    other = send_x(own)
    where, factors = [], []
    for r in range(2):
        patch, step = labels(patch_of_slot, step_of_slot, section_id, r)
        where.append(jnp.stack([patch, xh, y, core]).astype(jnp.int32))
        factors.append(lax.dynamic_index_in_dim(modulation[0], step, 0, keepdims=False))
    w1 = jnp.concatenate([w_qkv[0].reshape(D, 3 * HD), w_mlp_in[0]], axis=1)
    w2 = jnp.concatenate([w_attn_out[0], w_mlp_out[0]], axis=0)
    gains = qk_scale[0]
    cache = kv_cache[0]

    normed, kept = local_call(
        start_body,
        [("vmem", (PAIR, D), BF)] * 2,
        [("smem", where[0]), ("vmem", own), ("vmem", other), ("vmem", factors[0])],
        flops=1_000_000,
        moved=400_000,
        name="norm_first",
    )
    kept = send_on(kept, 0)
    sums, cache = block(normed, where[0], w1, w2, gains, cache)
    (out,) = local_call(
        column_body,
        [("vmem", (PAIR, D), BF)],
        [("vmem", a) for a in sums] + [("vmem", factors[0])],
        flops=400_000,
        moved=1_200_000,
        name="column_sum",
    )
    p0, p1 = send_on(out, 0), send_on(out, 8)
    normed, kept = local_call(
        next_body,
        [("vmem", (PAIR, D), BF), ("vmem", (PIECE, D), BF)],
        [("smem", where[1])] + [("vmem", a) for a in (kept, p0, p1, factors[1])],
        flops=1_000_000,
        moved=800_000,
        name="norm_next",
    )
    kept = send_on(kept, 0)
    sums, cache = block(normed, where[1], w1, w2, gains, cache)
    here, there = local_call(
        last_column_body,
        [("vmem", (PIECE, D), BF)] * 2,
        [("smem", where[1])] + [("vmem", a) for a in sums] + [("vmem", factors[1])],
        flops=400_000,
        moved=1_200_000,
        name="column_last",
    )
    p0, p1 = send_on(here, 0), send_on(there, 8)
    (out,) = local_call(
        final_body,
        [("vmem", (PIECE, D), BF)],
        [("vmem", a) for a in (kept, p0, p1)],
        flops=400_000,
        moved=400_000,
        name="residual_last",
    )
    return out[None], cache[None]


def solution(mesh):
    return jax.shard_map(
        shards,
        mesh=mesh,
        in_specs=(
            P("section", "sp", None),
            P(),
            P(),
            P("section", None, None, None),
            P("section", None, None, "sp"),
            P("section", None, None),
            P("section", None, "sp"),
            P("section", "sp", None),
            P("section", "sp", None),
            P("section", None, None, "sp"),
        ),
        out_specs=(P("section", "sp", None), P("section", None, None, "sp")),
        check_vma=False,
    )
```

time: 360 us -> 117 us (0.33)
  waiting for transfers between devices: 267 us -> 55.7 us
  matrix products: 36 us -> 0 us
  starting transfers between devices: 1.53 us -> 26.6 us
  Pallas kernels: 0 us -> 16 us
  between operations: 16.5 us -> 2.16 us
  local copies, waits for them, and re-layouts: 22.7 us -> 10.8 us
  other arithmetic: 14.8 us -> 4.5 us
    reduce_scatter x2 -> x0, waiting for transfers between devices: 164 us -> none  [shards(): lax.psum_scatter(jnp.dot(attention, attention_weight, preferred_element_t...]
    all_gather x2 -> x0, waiting for transfers between devices: 93.7 us -> none  [shards(): gathered = lax.all_gather(normed, 'sp', axis=0, tiled=True)]
    ppermute x2 -> x29, waiting for transfers between devices: 9.66 us -> 55.7 us  [the longest x12 28.9 us: send_y(): lax.ppermute(x, 'sp', [(i, i & 9 | ((i >> 1 & 3) + by) % 4 << 1) for i in...]
    dot_general x6 -> x0, matrix products: 30.1 us -> none  [the longest x2 13.4 us: shards(): jnp.dot(activity, outer_weight, preferred_element_type=jnp.float32)]
    ppermute x2 -> x29, starting transfers between devices: 1.19 us -> 26.6 us  [the longest x12 18.8 us: send_y(): lax.ppermute(x, 'sp', [(i, i & 9 | ((i >> 1 & 3) + by) % 4 << 1) for i in...]
    pallas_call x0 -> x11, Pallas kernels: none -> 16 us  [local_call(): pl.pallas_call(body, out_shape=out_shape, in_specs=specs, out_specs=out_s...]
    squeeze x6 -> x0, local copies, waits for them, and re-layouts: 9.31 us -> none  [the longest x1 4.35 us: shards(): qkv_weight = w_qkv[0]]
    convert_element_type x7 -> x0, other arithmetic: 6.01 us -> none  [the longest x2 2.4 us: modulate(): (center * lax.rsqrt(spread + 1e-06) * (1.0 + factors[1]) + factors[0]).as...]
  transfers between devices with their start and end apart: 6 -> 29, of which waited for: 6 -> 19; matrix products, arithmetic and copies ran while one was open for 3% -> 10% of each run, Pallas kernels for 0% -> 2%
where the time goes in v1:
time: 117 us; the launch traced here: 116 us
  waiting for transfers between devices  55.7 us (48%)
  starting transfers between devices  26.6 us (23%)
  Pallas kernels  16 us (14%)
  local copies, waits for them, and re-layouts  10.8 us (9%)
  other arithmetic  4.5 us (4%)
  between operations  2.16 us (2%)
    ppermute x12, waiting for transfers between devices, send_y(): lax.ppermute(x, 'sp', [(i, i & 9 | ((i >> 1 & 3) + by) % 4 << 1) for i in...  28.9 us
    ppermute x6, waiting for transfers between devices, send_on(): return lax.ppermute(x, ('section', 'sp'), pairs)  21.1 us
    ppermute x12, starting transfers between devices, send_y(): lax.ppermute(x, 'sp', [(i, i & 9 | ((i >> 1 & 3) + by) % 4 << 1) for i in...  18.8 us
    pallas_call x11, Pallas kernels, local_call(): pl.pallas_call(body, out_shape=out_shape, in_specs=specs, out_specs=out_s...  16 us
    unnamed x17, local copies, waits for them, and re-layouts  6.63 us
    ppermute x10, waiting for transfers between devices, send_core(): return lax.ppermute(x, 'sp', [(i, i ^ 1) for i in range(SPAN)])  5.69 us
    ppermute x6, starting transfers between devices, send_on(): return lax.ppermute(x, ('section', 'sp'), pairs)  3.59 us
    ppermute x1, starting transfers between devices, send_x(): return lax.ppermute(x, 'sp', [(i, i ^ 8) for i in range(SPAN)])  3.02 us
  transfers between devices with their start and end apart: 29, of which 19 were waited for; matrix products, arithmetic and copies ran while one was open for 10% of the time, Pallas kernels for 2%

profile of v1, /device:TPU:8, one launch (start us, length us, event | category | flops | bytes accessed | tf_op | source)
XLA Modules:
  0.0 115.8 jit_solution(10393646930092453031)
XLA Ops:
  0.7 3.1 %copy.27 = bf16[1,2,4096,128]{3,2,1,0:T(8,128)(2,1)} copy(bf16[1,2,4096,128]{3,2,1,0:T(8,128)(2,1)} %param.19) | data formatting | bytes 4194304
  3.8 3.0 %collective-permute-start = (bf16[16,3072]{1,0:T(8,128)(2,1)S(1)}, bf16[16,3072]{1,0:T(8,128)(2,1)S(1)}, u32[]{:S(2)}, u32[]{:S(2)}) collective-permute-start(bf16[16,3072]{1,0:T(8,128)(2,1)S(1)} %bitcast.25), channel_id=1, source_target_pairs={{0,8},{1,9},{2,10},{3,11},{4,12},{5,13},{6,14},{7,15},{8,0},{9,1},... | collective-permute-start | bytes 294920 | tf_op jit(solution)/shard_map/ppermute | solution.py:36
  6.8 0.7 fusion
  8.8 1.1 constant_dynamic-slice_fusion
  9.9 2.8 %copy.15 = bf16[1,3072,3,128]{1,3,2,0:T(8,128)(2,1)S(1)} copy(bf16[1,3072,3,128]{3,1,2,0:T(8,128)(2,1)} %param.14) | data formatting | bytes 4718592 | tf_op args[4]
  12.7 2.5 %copy.16 = bf16[3072,384]{1,0:T(8,128)(2,1)} copy(bf16[3072,384]{0,1:T(8,128)(2,1)S(1)} %bitcast.31) | data formatting | bytes 4718592 | tf_op jit(solution)/shard_map/reshape;squeeze | solution.py:299
  15.2 0.7 add_add_fusion.1.where
  15.9 0.0 collective-permute-done.other
  15.9 0.8 norm_first.1
  16.7 1.7 %collective-permute-start.4 = (bf16[32,3072]{1,0:T(8,128)(2,1)S(1)}, bf16[32,3072]{1,0:T(8,128)(2,1)S(1)}, u32[]{:S(2)}, u32[]{:S(2)}) collective-permute-start(bf16[32,3072]{1,0:T(8,128)(2,1)S(1)} %get-tuple-element.23.n0), channel_id=1, source_target_pairs={{0,2},{1,3},{2,4},{3,5},{4,6},{5,7},{6,0},{7,1},{8,10},{9,11},{10,... | collective-permute-start | bytes 589832 | tf_op jit(solution)/shard_map/ppermute | solution.py:30
  18.4 0.9 collective-permute-start.3
  19.3 2.4 %collective-permute-start.2 = (bf16[32,3072]{1,0:T(8,128)(2,1)S(1)}, bf16[32,3072]{1,0:T(8,128)(2,1)S(1)}, u32[]{:S(2)}, u32[]{:S(2)}) collective-permute-start(bf16[32,3072]{1,0:T(8,128)(2,1)S(1)} %get-tuple-element.23.n0), channel_id=1, source_target_pairs={{0,6},{1,7},{2,0},{3,1},{4,2},{5,3},{6,4},{7,5},{8,14},{9,15},{10,... | collective-permute-start | bytes 589832 | tf_op jit(solution)/shard_map/ppermute | solution.py:30
  21.8 2.9 %pad_maximum_fusion.w1 = bf16[3072,768]{1,0:T(8,128)(2,1)S(1)} fusion(bf16[3072,384]{1,0:T(8,128)(2,1)} %bitcast.33, bf16[3072,384]{1,0:T(8,128)(2,1)} %copy.16), kind=kLoop, calls=%fused_computation | loop fusion | flops 9437184 | bytes 9437184 | tf_op jit(solution)/shard_map/concatenate | solution.py:299
  24.7 0.1 collective-permute-start.5
  24.8 0.5 collective-permute-start.8
  25.3 2.5 %collective-permute-done.3.n2 = bf16[32,3072]{1,0:T(8,128)(2,1)S(1)} collective-permute-done((bf16[32,3072]{1,0:T(8,128)(2,1)S(1)}, bf16[32,3072]{1,0:T(8,128)(2,1)S(1)}, u32[]{:S(2)}, u32[]{:S(2)}) %collective-permute-start.3) | collective-permute-done | bytes 196640 | tf_op jit(solution)/shard_map/ppermute | solution.py:30
  27.7 1.8 %collective-permute-done.2.n1 = bf16[32,3072]{1,0:T(8,128)(2,1)S(1)} collective-permute-done((bf16[32,3072]{1,0:T(8,128)(2,1)S(1)}, bf16[32,3072]{1,0:T(8,128)(2,1)S(1)}, u32[]{:S(2)}, u32[]{:S(2)}) %collective-permute-start.2) | collective-permute-done | bytes 196640 | tf_op jit(solution)/shard_map/ppermute | solution.py:30
  29.5 0.0 copy-start.1
  29.5 0.2 pad_maximum_fusion.1.w2
  29.8 1.2 %collective-permute-done.6.s1 = bf16[32,3072]{1,0:T(8,128)(2,1)S(1)} collective-permute-done((bf16[32,3072]{1,0:T(8,128)(2,1)S(1)}, bf16[32,3072]{1,0:T(8,128)(2,1)S(1)}, u32[]{:S(2)}, u32[]{:S(2)}) %collective-permute-start.6) | collective-permute-done | bytes 196640 | tf_op jit(solution)/shard_map/ppermute | solution.py:26
  31.0 6.0 %block.2 = (bf16[2,4096,128]{2,1,0:T(8,128)(2,1)}, bf16[256,512]{1,0:T(8,128)(2,1)S(1)}, bf16[128,3072]{1,0:T(8,128)(2,1)S(1)}) custom-call(s32[4]{0:T(128)S(1)} %add_add_fusion.1.where, bf16[32,3072]{1,0:T(8,128)(2,1)S(1)} %get-tuple-element.23.n0, bf16[32,3072]{1,0:T(8,128)(2,1)S(1)} %collective-permute-done.2.n1, ...), custom_call_target="tpu_custom_call", output_to_operand_aliasing={{0}: (12, {})} | custom-call | flops 2200000000 | bytes 12000000 | tf_op jit(solution)/shard_map/block/pallas_call | solution.py:73
  37.0 0.4 collective-permute-start.9
  37.4 0.6 own_half.2.mine
  38.0 1.5 %collective-permute-done.9.came = bf16[128,3072]{1,0:T(8,128)(2,1)S(1)} collective-permute-done((bf16[128,3072]{1,0:T(8,128)(2,1)S(1)}, bf16[128,3072]{1,0:T(8,128)(2,1)S(1)}, u32[]{:S(2)}, u32[]{:S(2)}) %collective-permute-start.9) | collective-permute-done | bytes 786464 | tf_op jit(solution)/shard_map/ppermute | solution.py:26
  39.5 0.1 pair_sum.2
  39.6 1.4 %collective-permute-start.10 = (bf16[32,3072]{1,0:T(8,128)(2,1)S(1)}, bf16[32,3072]{1,0:T(8,128)(2,1)S(1)}, u32[]{:S(2)}, u32[]{:S(2)}) collective-permute-start(bf16[32,3072]{1,0:T(8,128)(2,1)S(1)} %get-tuple-element.27), channel_id=1, source_target_pairs={{0,2},{1,3},{2,4},{3,5},{4,6},{5,7},{6,0},{7,1},{8,10},{9,11},{10,... | collective-permute-start | bytes 589832 | tf_op jit(solution)/shard_map/ppermute | solution.py:30
  41.0 1.8 %collective-permute-start.11 = (bf16[32,3072]{1,0:T(8,128)(2,1)S(1)}, bf16[32,3072]{1,0:T(8,128)(2,1)S(1)}, u32[]{:S(2)}, u32[]{:S(2)}) collective-permute-start(bf16[32,3072]{1,0:T(8,128)(2,1)S(1)} %get-tuple-element.28), channel_id=1, source_target_pairs={{0,4},{1,5},{2,6},{3,7},{4,0},{5,1},{6,2},{7,3},{8,12},{9,13},{10,... | collective-permute-start | bytes 589832 | tf_op jit(solution)/shard_map/ppermute | solution.py:30
  42.9 1.3 %collective-permute-start.12 = (bf16[32,3072]{1,0:T(8,128)(2,1)S(1)}, bf16[32,3072]{1,0:T(8,128)(2,1)S(1)}, u32[]{:S(2)}, u32[]{:S(2)}) collective-permute-start(bf16[32,3072]{1,0:T(8,128)(2,1)S(1)} %get-tuple-element.29), channel_id=1, source_target_pairs={{0,6},{1,7},{2,0},{3,1},{4,2},{5,3},{6,4},{7,5},{8,14},{9,15},{10,... | collective-permute-start | bytes 589832 | tf_op jit(solution)/shard_map/ppermute | solution.py:30
  44.1 0.6 collective-permute-start.1
  44.7 2.7 %collective-permute-done.10.r1 = bf16[32,3072]{1,0:T(8,128)(2,1)S(1)} collective-permute-done((bf16[32,3072]{1,0:T(8,128)(2,1)S(1)}, bf16[32,3072]{1,0:T(8,128)(2,1)S(1)}, u32[]{:S(2)}, u32[]{:S(2)}) %collective-permute-start.10) | collective-permute-done | bytes 196640 | tf_op jit(solution)/shard_map/ppermute | solution.py:30
  47.5 2.9 %collective-permute-done.11.r2 = bf16[32,3072]{1,0:T(8,128)(2,1)S(1)} collective-permute-done((bf16[32,3072]{1,0:T(8,128)(2,1)S(1)}, bf16[32,3072]{1,0:T(8,128)(2,1)S(1)}, u32[]{:S(2)}, u32[]{:S(2)}) %collective-permute-start.11) | collective-permute-done | bytes 196640 | tf_op jit(solution)/shard_map/ppermute | solution.py:30
  50.3 3.0 %collective-permute-done.12.r3 = bf16[32,3072]{1,0:T(8,128)(2,1)S(1)} collective-permute-done((bf16[32,3072]{1,0:T(8,128)(2,1)S(1)}, bf16[32,3072]{1,0:T(8,128)(2,1)S(1)}, u32[]{:S(2)}, u32[]{:S(2)}) %collective-permute-start.12) | collective-permute-done | bytes 196640 | tf_op jit(solution)/shard_map/ppermute | solution.py:30
  53.4 0.1 column_sum.1
  53.5 1.2 %collective-permute-start.14 = (bf16[32,3072]{1,0:T(8,128)(2,1)S(1)}, bf16[32,3072]{1,0:T(8,128)(2,1)S(1)}, u32[]{:S(2)}, u32[]{:S(2)}) collective-permute-start(bf16[32,3072]{1,0:T(8,128)(2,1)S(1)} %column_sum.1), channel_id=1, source_target_pairs={{0,24},{1,25},{2,26},{3,27},{4,28},{5,29},{6,30},{7,31},{8,16},{9,... | collective-permute-start | bytes 589832 | tf_op jit(solution)/shard_map/ppermute | solution.py:44
  54.7 0.7 collective-permute-start.13
  55.4 0.6 add_add_fusion.where
  56.1 9.6 %collective-permute-done.14.p1 = bf16[32,3072]{1,0:T(8,128)(2,1)S(1)} collective-permute-done((bf16[32,3072]{1,0:T(8,128)(2,1)S(1)}, bf16[32,3072]{1,0:T(8,128)(2,1)S(1)}, u32[]{:S(2)}, u32[]{:S(2)}) %collective-permute-start.14) | collective-permute-done | bytes 196640 | tf_op jit(solution)/shard_map/ppermute | solution.py:44
  65.7 3.0 %collective-permute-done.13.p0 = bf16[32,3072]{1,0:T(8,128)(2,1)S(1)} collective-permute-done((bf16[32,3072]{1,0:T(8,128)(2,1)S(1)}, bf16[32,3072]{1,0:T(8,128)(2,1)S(1)}, u32[]{:S(2)}, u32[]{:S(2)}) %collective-permute-start.13) | collective-permute-done | bytes 196640 | tf_op jit(solution)/shard_map/ppermute | solution.py:44
  68.8 0.9 norm_next.1
  69.7 0.1 collective-permute-start.18
  69.8 2.0 %collective-permute-start.17 = (bf16[32,3072]{1,0:T(8,128)(2,1)S(1)}, bf16[32,3072]{1,0:T(8,128)(2,1)S(1)}, u32[]{:S(2)}, u32[]{:S(2)}) collective-permute-start(bf16[32,3072]{1,0:T(8,128)(2,1)S(1)} %get-tuple-element.31.n0), channel_id=1, source_target_pairs={{0,4},{1,5},{2,6},{3,7},{4,0},{5,1},{6,2},{7,3},{8,12},{9,13},{10,... | collective-permute-start | bytes 589832 | tf_op jit(solution)/shard_map/ppermute | solution.py:30
  71.8 2.5 %collective-permute-start.16 = (bf16[32,3072]{1,0:T(8,128)(2,1)S(1)}, bf16[32,3072]{1,0:T(8,128)(2,1)S(1)}, u32[]{:S(2)}, u32[]{:S(2)}) collective-permute-start(bf16[32,3072]{1,0:T(8,128)(2,1)S(1)} %get-tuple-element.31.n0), channel_id=1, source_target_pairs={{0,6},{1,7},{2,0},{3,1},{4,2},{5,3},{6,4},{7,5},{8,14},{9,15},{10,... | collective-permute-start | bytes 589832 | tf_op jit(solution)/shard_map/ppermute | solution.py:30
  74.3 3.3 %collective-permute-done.18.n3 = bf16[32,3072]{1,0:T(8,128)(2,1)S(1)} collective-permute-done((bf16[32,3072]{1,0:T(8,128)(2,1)S(1)}, bf16[32,3072]{1,0:T(8,128)(2,1)S(1)}, u32[]{:S(2)}, u32[]{:S(2)}) %collective-permute-start.18) | collective-permute-done | bytes 196640 | tf_op jit(solution)/shard_map/ppermute | solution.py:30
  77.6 1.6 %collective-permute-done.17.n2 = bf16[32,3072]{1,0:T(8,128)(2,1)S(1)} collective-permute-done((bf16[32,3072]{1,0:T(8,128)(2,1)S(1)}, bf16[32,3072]{1,0:T(8,128)(2,1)S(1)}, u32[]{:S(2)}, u32[]{:S(2)}) %collective-permute-start.17) | collective-permute-done | bytes 196640 | tf_op jit(solution)/shard_map/ppermute | solution.py:30
  79.3 2.6 %collective-permute-done.16.n1 = bf16[32,3072]{1,0:T(8,128)(2,1)S(1)} collective-permute-done((bf16[32,3072]{1,0:T(8,128)(2,1)S(1)}, bf16[32,3072]{1,0:T(8,128)(2,1)S(1)}, u32[]{:S(2)}, u32[]{:S(2)}) %collective-permute-start.16) | collective-permute-done | bytes 196640 | tf_op jit(solution)/shard_map/ppermute | solution.py:30
  81.9 0.0 collective-permute-start.20
  81.9 1.4 %collective-permute-done.20.s1 = bf16[32,3072]{1,0:T(8,128)(2,1)S(1)} collective-permute-done((bf16[32,3072]{1,0:T(8,128)(2,1)S(1)}, bf16[32,3072]{1,0:T(8,128)(2,1)S(1)}, u32[]{:S(2)}, u32[]{:S(2)}) %collective-permute-start.20) | collective-permute-done | bytes 196640 | tf_op jit(solution)/shard_map/ppermute | solution.py:26
  83.3 6.0 %block.3 = (bf16[2,4096,128]{2,1,0:T(8,128)(2,1)}, bf16[256,512]{1,0:T(8,128)(2,1)S(1)}, bf16[128,3072]{1,0:T(8,128)(2,1)S(1)}) custom-call(s32[4]{0:T(128)S(1)} %add_add_fusion.where, bf16[32,3072]{1,0:T(8,128)(2,1)S(1)} %get-tuple-element.31.n0, bf16[32,3072]{1,0:T(8,128)(2,1)S(1)} %collective-permute-done.16.n1, ...), custom_call_target="tpu_custom_call", output_to_operand_aliasing={{0}: (12, {})} | custom-call | flops 2200000000 | bytes 12000000 | tf_op jit(solution)/shard_map/block/pallas_call | solution.py:73
  89.3 0.2 collective-permute-start.23
  89.5 0.6 own_half.3.mine
  90.1 1.6 %collective-permute-done.23.came = bf16[128,3072]{1,0:T(8,128)(2,1)S(1)} collective-permute-done((bf16[128,3072]{1,0:T(8,128)(2,1)S(1)}, bf16[128,3072]{1,0:T(8,128)(2,1)S(1)}, u32[]{:S(2)}, u32[]{:S(2)}) %collective-permute-start.23) | collective-permute-done | bytes 786464 | tf_op jit(solution)/shard_map/ppermute | solution.py:26
  91.7 0.1 pair_sum.3
  91.8 0.7 collective-permute-start.24
  92.5 2.7 %collective-permute-start.25 = (bf16[32,3072]{1,0:T(8,128)(2,1)S(1)}, bf16[32,3072]{1,0:T(8,128)(2,1)S(1)}, u32[]{:S(2)}, u32[]{:S(2)}) collective-permute-start(bf16[32,3072]{1,0:T(8,128)(2,1)S(1)} %get-tuple-element.37), channel_id=1, source_target_pairs={{0,4},{1,5},{2,6},{3,7},{4,0},{5,1},{6,2},{7,3},{8,12},{9,13},{10,... | collective-permute-start | bytes 589832 | tf_op jit(solution)/shard_map/ppermute | solution.py:30
  95.2 1.3 %collective-permute-start.26 = (bf16[32,3072]{1,0:T(8,128)(2,1)S(1)}, bf16[32,3072]{1,0:T(8,128)(2,1)S(1)}, u32[]{:S(2)}, u32[]{:S(2)}) collective-permute-start(bf16[32,3072]{1,0:T(8,128)(2,1)S(1)} %get-tuple-element.38), channel_id=1, source_target_pairs={{0,6},{1,7},{2,0},{3,1},{4,2},{5,3},{6,4},{7,5},{8,14},{9,15},{10,... | collective-permute-start | bytes 589832 | tf_op jit(solution)/shard_map/ppermute | solution.py:30
  96.5 3.2 %collective-permute-done.24.r1 = bf16[32,3072]{1,0:T(8,128)(2,1)S(1)} collective-permute-done((bf16[32,3072]{1,0:T(8,128)(2,1)S(1)}, bf16[32,3072]{1,0:T(8,128)(2,1)S(1)}, u32[]{:S(2)}, u32[]{:S(2)}) %collective-permute-start.24) | collective-permute-done | bytes 196640 | tf_op jit(solution)/shard_map/ppermute | solution.py:30
  99.6 2.2 %collective-permute-done.25.r2 = bf16[32,3072]{1,0:T(8,128)(2,1)S(1)} collective-permute-done((bf16[32,3072]{1,0:T(8,128)(2,1)S(1)}, bf16[32,3072]{1,0:T(8,128)(2,1)S(1)}, u32[]{:S(2)}, u32[]{:S(2)}) %collective-permute-start.25) | collective-permute-done | bytes 196640 | tf_op jit(solution)/shard_map/ppermute | solution.py:30
  101.8 3.0 %collective-permute-done.26.r3 = bf16[32,3072]{1,0:T(8,128)(2,1)S(1)} collective-permute-done((bf16[32,3072]{1,0:T(8,128)(2,1)S(1)}, bf16[32,3072]{1,0:T(8,128)(2,1)S(1)}, u32[]{:S(2)}, u32[]{:S(2)}) %collective-permute-start.26) | collective-permute-done | bytes 196640 | tf_op jit(solution)/shard_map/ppermute | solution.py:30
  104.9 0.6 column_last.1
  105.5 0.1 collective-permute-start.27
  105.6 1.0 collective-permute-start.28
  106.6 6.7 %collective-permute-done.27.p0 = bf16[16,3072]{1,0:T(8,128)(2,1)S(1)} collective-permute-done((bf16[16,3072]{1,0:T(8,128)(2,1)S(1)}, bf16[16,3072]{1,0:T(8,128)(2,1)S(1)}, u32[]{:S(2)}, u32[]{:S(2)}) %collective-permute-start.27) | collective-permute-done | bytes 98336 | tf_op jit(solution)/shard_map/ppermute | solution.py:44
  113.4 1.7 %collective-permute-done.28.p1 = bf16[16,3072]{1,0:T(8,128)(2,1)S(1)} collective-permute-done((bf16[16,3072]{1,0:T(8,128)(2,1)S(1)}, bf16[16,3072]{1,0:T(8,128)(2,1)S(1)}, u32[]{:S(2)}, u32[]{:S(2)}) %collective-permute-start.28) | collective-permute-done | bytes 98336 | tf_op jit(solution)/shard_map/ppermute | solution.py:44
  115.1 0.6 copy.26
  (29 shorter events, 0.1 us)
Async XLA Ops:
  0.6 3.1 %copy-start = (bf16[1,16,3072]{2,1,0:T(8,128)(2,1)S(1)}, bf16[1,16,3072]{2,1,0:T(8,128)(2,1)}, u32[]{:S(2)}) copy-start(bf16[1,16,3072]{2,1,0:T(8,128)(2,1)} %param.10) | copy-start | bytes 294916
  0.6 6.1 %copy-start.5 = (s32[16]{0:T(128)S(1)}, s32[16]{0:T(128)}, u32[]{:S(2)}) copy-start(s32[16]{0:T(128)} %param.11) | copy-start | bytes 196
  0.7 6.1 %copy-start.4 = (s32[16]{0:T(128)S(1)}, s32[16]{0:T(128)}, u32[]{:S(2)}) copy-start(s32[16]{0:T(128)} %param.12) | copy-start | bytes 196
  3.8 12.2 %collective-permute-start = (bf16[16,3072]{1,0:T(8,128)(2,1)S(1)}, bf16[16,3072]{1,0:T(8,128)(2,1)S(1)}, u32[]{:S(2)}, u32[]{:S(2)}) collective-permute-start(bf16[16,3072]{1,0:T(8,128)(2,1)S(1)} %bitcast.25), channel_id=1, source_target_pairs={{0,8},{1,9},{2,10},{3,11},{4,12},{5,13},{6,14},{7,15},{8,0},{9,1},... | collective-permute-start | bytes 294920 | tf_op jit(solution)/shard_map/ppermute | solution.py:36
  16.7 8.0 %collective-permute-start.4 = (bf16[32,3072]{1,0:T(8,128)(2,1)S(1)}, bf16[32,3072]{1,0:T(8,128)(2,1)S(1)}, u32[]{:S(2)}, u32[]{:S(2)}) collective-permute-start(bf16[32,3072]{1,0:T(8,128)(2,1)S(1)} %get-tuple-element.23.n0), channel_id=1, source_target_pairs={{0,2},{1,3},{2,4},{3,5},{4,6},{5,7},{6,0},{7,1},{8,10},{9,11},{10,... | collective-permute-start | bytes 589832 | tf_op jit(solution)/shard_map/ppermute | solution.py:30
  18.4 9.3 %collective-permute-start.3 = (bf16[32,3072]{1,0:T(8,128)(2,1)S(1)}, bf16[32,3072]{1,0:T(8,128)(2,1)S(1)}, u32[]{:S(2)}, u32[]{:S(2)}) collective-permute-start(bf16[32,3072]{1,0:T(8,128)(2,1)S(1)} %get-tuple-element.23.n0), channel_id=1, source_target_pairs={{0,4},{1,5},{2,6},{3,7},{4,0},{5,1},{6,2},{7,3},{8,12},{9,13},{10,... | collective-permute-start | bytes 589832 | tf_op jit(solution)/shard_map/ppermute | solution.py:30
  19.3 10.2 %collective-permute-start.2 = (bf16[32,3072]{1,0:T(8,128)(2,1)S(1)}, bf16[32,3072]{1,0:T(8,128)(2,1)S(1)}, u32[]{:S(2)}, u32[]{:S(2)}) collective-permute-start(bf16[32,3072]{1,0:T(8,128)(2,1)S(1)} %get-tuple-element.23.n0), channel_id=1, source_target_pairs={{0,6},{1,7},{2,0},{3,1},{4,2},{5,3},{6,4},{7,5},{8,14},{9,15},{10,... | collective-permute-start | bytes 589832 | tf_op jit(solution)/shard_map/ppermute | solution.py:30
  21.7 7.8 %copy-start.2 = (bf16[1,384,3072]{2,1,0:T(8,128)(2,1)S(1)}, bf16[1,384,3072]{2,1,0:T(8,128)(2,1)}, u32[]{:S(2)}) copy-start(bf16[1,384,3072]{2,1,0:T(8,128)(2,1)} %param.18) | copy-start | bytes 7077892
  21.8 7.8 %copy-start.3 = (bf16[1,128,3072]{2,1,0:T(8,128)(2,1)S(1)}, bf16[1,128,3072]{2,1,0:T(8,128)(2,1)}, u32[]{:S(2)}) copy-start(bf16[1,128,3072]{2,1,0:T(8,128)(2,1)} %param.17) | copy-start | bytes 2359300
  24.7 5.1 %collective-permute-start.5 = (bf16[32,3072]{1,0:T(8,128)(2,1)S(1)}, bf16[32,3072]{1,0:T(8,128)(2,1)S(1)}, u32[]{:S(2)}, u32[]{:S(2)}) collective-permute-start(bf16[32,3072]{1,0:T(8,128)(2,1)S(1)} %get-tuple-element.23.n0), channel_id=1, source_target_pairs={{0,1},{1,0},{2,3},{3,2},{4,5},{5,4},{6,7},{7,6},{8,9},{9,8},{10,11... | collective-permute-start | bytes 589832 | tf_op jit(solution)/shard_map/ppermute | solution.py:26
  24.8 5.0 %collective-permute-start.8 = (bf16[32,3072]{1,0:T(8,128)(2,1)S(1)}, bf16[32,3072]{1,0:T(8,128)(2,1)S(1)}, u32[]{:S(2)}, u32[]{:S(2)}) collective-permute-start(bf16[32,3072]{1,0:T(8,128)(2,1)S(1)} %collective-permute-done.4.n3), channel_id=1, source_target_pairs={{0,1},{1,0},{2,3},{3,2},{4,5},{5,4},{6,7},{7,6},{8,9},{9,8},{10,11... | collective-permute-start | bytes 589832 | tf_op jit(solution)/shard_map/ppermute | solution.py:26
  27.7 2.0 %collective-permute-start.7 = (bf16[32,3072]{1,0:T(8,128)(2,1)S(1)}, bf16[32,3072]{1,0:T(8,128)(2,1)S(1)}, u32[]{:S(2)}, u32[]{:S(2)}) collective-permute-start(bf16[32,3072]{1,0:T(8,128)(2,1)S(1)} %collective-permute-done.3.n2), channel_id=1, source_target_pairs={{0,1},{1,0},{2,3},{3,2},{4,5},{5,4},{6,7},{7,6},{8,9},{9,8},{10,11... | collective-permute-start | bytes 589832 | tf_op jit(solution)/shard_map/ppermute | solution.py:26
  29.5 1.4 %collective-permute-start.6 = (bf16[32,3072]{1,0:T(8,128)(2,1)S(1)}, bf16[32,3072]{1,0:T(8,128)(2,1)S(1)}, u32[]{:S(2)}, u32[]{:S(2)}) collective-permute-start(bf16[32,3072]{1,0:T(8,128)(2,1)S(1)} %collective-permute-done.2.n1), channel_id=1, source_target_pairs={{0,1},{1,0},{2,3},{3,2},{4,5},{5,4},{6,7},{7,6},{8,9},{9,8},{10,11... | collective-permute-start | bytes 589832 | tf_op jit(solution)/shard_map/ppermute | solution.py:26
  29.5 1.4 %copy-start.1 = (bf16[1,2,128]{2,1,0:T(2,128)(2,1)S(1)}, bf16[1,2,128]{2,1,0:T(2,128)(2,1)}, u32[]{:S(2)}) copy-start(bf16[1,2,128]{2,1,0:T(2,128)(2,1)} %param.15) | copy-start | bytes 1540
  37.0 2.6 %collective-permute-start.9 = (bf16[128,3072]{1,0:T(8,128)(2,1)S(1)}, bf16[128,3072]{1,0:T(8,128)(2,1)S(1)}, u32[]{:S(2)}, u32[]{:S(2)}) collective-permute-start(bf16[128,3072]{1,0:T(8,128)(2,1)S(1)} %get-tuple-element.25), channel_id=1, source_target_pairs={{0,1},{1,0},{2,3},{3,2},{4,5},{5,4},{6,7},{7,6},{8,9},{9,8},{10,11... | collective-permute-start | bytes 2359304 | tf_op jit(solution)/shard_map/ppermute | solution.py:26
  39.6 7.8 %collective-permute-start.10 = (bf16[32,3072]{1,0:T(8,128)(2,1)S(1)}, bf16[32,3072]{1,0:T(8,128)(2,1)S(1)}, u32[]{:S(2)}, u32[]{:S(2)}) collective-permute-start(bf16[32,3072]{1,0:T(8,128)(2,1)S(1)} %get-tuple-element.27), channel_id=1, source_target_pairs={{0,2},{1,3},{2,4},{3,5},{4,6},{5,7},{6,0},{7,1},{8,10},{9,11},{10,... | collective-permute-start | bytes 589832 | tf_op jit(solution)/shard_map/ppermute | solution.py:30
  41.0 9.3 %collective-permute-start.11 = (bf16[32,3072]{1,0:T(8,128)(2,1)S(1)}, bf16[32,3072]{1,0:T(8,128)(2,1)S(1)}, u32[]{:S(2)}, u32[]{:S(2)}) collective-permute-start(bf16[32,3072]{1,0:T(8,128)(2,1)S(1)} %get-tuple-element.28), channel_id=1, source_target_pairs={{0,4},{1,5},{2,6},{3,7},{4,0},{5,1},{6,2},{7,3},{8,12},{9,13},{10,... | collective-permute-start | bytes 589832 | tf_op jit(solution)/shard_map/ppermute | solution.py:30
  42.9 10.5 %collective-permute-start.12 = (bf16[32,3072]{1,0:T(8,128)(2,1)S(1)}, bf16[32,3072]{1,0:T(8,128)(2,1)S(1)}, u32[]{:S(2)}, u32[]{:S(2)}) collective-permute-start(bf16[32,3072]{1,0:T(8,128)(2,1)S(1)} %get-tuple-element.29), channel_id=1, source_target_pairs={{0,6},{1,7},{2,0},{3,1},{4,2},{5,3},{6,4},{7,5},{8,14},{9,15},{10,... | collective-permute-start | bytes 589832 | tf_op jit(solution)/shard_map/ppermute | solution.py:30
  44.1 11.9 %collective-permute-start.1 = (bf16[32,3072]{1,0:T(8,128)(2,1)S(1)}, bf16[32,3072]{1,0:T(8,128)(2,1)S(1)}, u32[]{:S(2)}, u32[]{:S(2)}) collective-permute-start(bf16[32,3072]{1,0:T(8,128)(2,1)S(1)} %get-tuple-element.22), channel_id=1, source_target_pairs={{0,16},{1,17},{2,18},{3,19},{4,20},{5,21},{6,22},{7,23},{8,24},{9,... | collective-permute-start | bytes 589832 | tf_op jit(solution)/shard_map/ppermute | solution.py:44
  53.5 12.2 %collective-permute-start.14 = (bf16[32,3072]{1,0:T(8,128)(2,1)S(1)}, bf16[32,3072]{1,0:T(8,128)(2,1)S(1)}, u32[]{:S(2)}, u32[]{:S(2)}) collective-permute-start(bf16[32,3072]{1,0:T(8,128)(2,1)S(1)} %column_sum.1), channel_id=1, source_target_pairs={{0,24},{1,25},{2,26},{3,27},{4,28},{5,29},{6,30},{7,31},{8,16},{9,... | collective-permute-start | bytes 589832 | tf_op jit(solution)/shard_map/ppermute | solution.py:44
  54.7 14.0 %collective-permute-start.13 = (bf16[32,3072]{1,0:T(8,128)(2,1)S(1)}, bf16[32,3072]{1,0:T(8,128)(2,1)S(1)}, u32[]{:S(2)}, u32[]{:S(2)}) collective-permute-start(bf16[32,3072]{1,0:T(8,128)(2,1)S(1)} %column_sum.1), channel_id=1, source_target_pairs={{0,16},{1,17},{2,18},{3,19},{4,20},{5,21},{6,22},{7,23},{8,24},{9,... | collective-permute-start | bytes 589832 | tf_op jit(solution)/shard_map/ppermute | solution.py:44
  69.7 7.9 %collective-permute-start.18 = (bf16[32,3072]{1,0:T(8,128)(2,1)S(1)}, bf16[32,3072]{1,0:T(8,128)(2,1)S(1)}, u32[]{:S(2)}, u32[]{:S(2)}) collective-permute-start(bf16[32,3072]{1,0:T(8,128)(2,1)S(1)} %get-tuple-element.31.n0), channel_id=1, source_target_pairs={{0,2},{1,3},{2,4},{3,5},{4,6},{5,7},{6,0},{7,1},{8,10},{9,11},{10,... | collective-permute-start | bytes 589832 | tf_op jit(solution)/shard_map/ppermute | solution.py:30
  69.8 9.5 %collective-permute-start.17 = (bf16[32,3072]{1,0:T(8,128)(2,1)S(1)}, bf16[32,3072]{1,0:T(8,128)(2,1)S(1)}, u32[]{:S(2)}, u32[]{:S(2)}) collective-permute-start(bf16[32,3072]{1,0:T(8,128)(2,1)S(1)} %get-tuple-element.31.n0), channel_id=1, source_target_pairs={{0,4},{1,5},{2,6},{3,7},{4,0},{5,1},{6,2},{7,3},{8,12},{9,13},{10,... | collective-permute-start | bytes 589832 | tf_op jit(solution)/shard_map/ppermute | solution.py:30
  71.8 10.1 %collective-permute-start.16 = (bf16[32,3072]{1,0:T(8,128)(2,1)S(1)}, bf16[32,3072]{1,0:T(8,128)(2,1)S(1)}, u32[]{:S(2)}, u32[]{:S(2)}) collective-permute-start(bf16[32,3072]{1,0:T(8,128)(2,1)S(1)} %get-tuple-element.31.n0), channel_id=1, source_target_pairs={{0,6},{1,7},{2,0},{3,1},{4,2},{5,3},{6,4},{7,5},{8,14},{9,15},{10,... | collective-permute-start | bytes 589832 | tf_op jit(solution)/shard_map/ppermute | solution.py:30
  74.3 7.6 %collective-permute-start.19 = (bf16[32,3072]{1,0:T(8,128)(2,1)S(1)}, bf16[32,3072]{1,0:T(8,128)(2,1)S(1)}, u32[]{:S(2)}, u32[]{:S(2)}) collective-permute-start(bf16[32,3072]{1,0:T(8,128)(2,1)S(1)} %get-tuple-element.31.n0), channel_id=1, source_target_pairs={{0,1},{1,0},{2,3},{3,2},{4,5},{5,4},{6,7},{7,6},{8,9},{9,8},{10,11... | collective-permute-start | bytes 589832 | tf_op jit(solution)/shard_map/ppermute | solution.py:26
  77.6 4.3 %collective-permute-start.22 = (bf16[32,3072]{1,0:T(8,128)(2,1)S(1)}, bf16[32,3072]{1,0:T(8,128)(2,1)S(1)}, u32[]{:S(2)}, u32[]{:S(2)}) collective-permute-start(bf16[32,3072]{1,0:T(8,128)(2,1)S(1)} %collective-permute-done.18.n3), channel_id=1, source_target_pairs={{0,1},{1,0},{2,3},{3,2},{4,5},{5,4},{6,7},{7,6},{8,9},{9,8},{10,11... | collective-permute-start | bytes 589832 | tf_op jit(solution)/shard_map/ppermute | solution.py:26
  79.3 2.7 %collective-permute-start.21 = (bf16[32,3072]{1,0:T(8,128)(2,1)S(1)}, bf16[32,3072]{1,0:T(8,128)(2,1)S(1)}, u32[]{:S(2)}, u32[]{:S(2)}) collective-permute-start(bf16[32,3072]{1,0:T(8,128)(2,1)S(1)} %collective-permute-done.17.n2), channel_id=1, source_target_pairs={{0,1},{1,0},{2,3},{3,2},{4,5},{5,4},{6,7},{7,6},{8,9},{9,8},{10,11... | collective-permute-start | bytes 589832 | tf_op jit(solution)/shard_map/ppermute | solution.py:26
  81.9 1.4 %collective-permute-start.20 = (bf16[32,3072]{1,0:T(8,128)(2,1)S(1)}, bf16[32,3072]{1,0:T(8,128)(2,1)S(1)}, u32[]{:S(2)}, u32[]{:S(2)}) collective-permute-start(bf16[32,3072]{1,0:T(8,128)(2,1)S(1)} %collective-permute-done.16.n1), channel_id=1, source_target_pairs={{0,1},{1,0},{2,3},{3,2},{4,5},{5,4},{6,7},{7,6},{8,9},{9,8},{10,11... | collective-permute-start | bytes 589832 | tf_op jit(solution)/shard_map/ppermute | solution.py:26
  89.3 2.4 %collective-permute-start.23 = (bf16[128,3072]{1,0:T(8,128)(2,1)S(1)}, bf16[128,3072]{1,0:T(8,128)(2,1)S(1)}, u32[]{:S(2)}, u32[]{:S(2)}) collective-permute-start(bf16[128,3072]{1,0:T(8,128)(2,1)S(1)} %get-tuple-element.34), channel_id=1, source_target_pairs={{0,1},{1,0},{2,3},{3,2},{4,5},{5,4},{6,7},{7,6},{8,9},{9,8},{10,11... | collective-permute-start | bytes 2359304 | tf_op jit(solution)/shard_map/ppermute | solution.py:26
  91.8 7.8 %collective-permute-start.24 = (bf16[32,3072]{1,0:T(8,128)(2,1)S(1)}, bf16[32,3072]{1,0:T(8,128)(2,1)S(1)}, u32[]{:S(2)}, u32[]{:S(2)}) collective-permute-start(bf16[32,3072]{1,0:T(8,128)(2,1)S(1)} %get-tuple-element.36), channel_id=1, source_target_pairs={{0,2},{1,3},{2,4},{3,5},{4,6},{5,7},{6,0},{7,1},{8,10},{9,11},{10,... | collective-permute-start | bytes 589832 | tf_op jit(solution)/shard_map/ppermute | solution.py:30
  92.5 9.3 %collective-permute-start.25 = (bf16[32,3072]{1,0:T(8,128)(2,1)S(1)}, bf16[32,3072]{1,0:T(8,128)(2,1)S(1)}, u32[]{:S(2)}, u32[]{:S(2)}) collective-permute-start(bf16[32,3072]{1,0:T(8,128)(2,1)S(1)} %get-tuple-element.37), channel_id=1, source_target_pairs={{0,4},{1,5},{2,6},{3,7},{4,0},{5,1},{6,2},{7,3},{8,12},{9,13},{10,... | collective-permute-start | bytes 589832 | tf_op jit(solution)/shard_map/ppermute | solution.py:30
  95.2 9.7 %collective-permute-start.26 = (bf16[32,3072]{1,0:T(8,128)(2,1)S(1)}, bf16[32,3072]{1,0:T(8,128)(2,1)S(1)}, u32[]{:S(2)}, u32[]{:S(2)}) collective-permute-start(bf16[32,3072]{1,0:T(8,128)(2,1)S(1)} %get-tuple-element.38), channel_id=1, source_target_pairs={{0,6},{1,7},{2,0},{3,1},{4,2},{5,3},{6,4},{7,5},{8,14},{9,15},{10,... | collective-permute-start | bytes 589832 | tf_op jit(solution)/shard_map/ppermute | solution.py:30
  96.5 10.2 %collective-permute-start.15 = (bf16[16,3072]{1,0:T(8,128)(2,1)S(1)}, bf16[16,3072]{1,0:T(8,128)(2,1)S(1)}, u32[]{:S(2)}, u32[]{:S(2)}) collective-permute-start(bf16[16,3072]{1,0:T(8,128)(2,1)S(1)} %get-tuple-element.30), channel_id=1, source_target_pairs={{0,16},{1,17},{2,18},{3,19},{4,20},{5,21},{6,22},{7,23},{8,24},{9,... | collective-permute-start | bytes 294920 | tf_op jit(solution)/shard_map/ppermute | solution.py:44
  105.5 7.8 %collective-permute-start.27 = (bf16[16,3072]{1,0:T(8,128)(2,1)S(1)}, bf16[16,3072]{1,0:T(8,128)(2,1)S(1)}, u32[]{:S(2)}, u32[]{:S(2)}) collective-permute-start(bf16[16,3072]{1,0:T(8,128)(2,1)S(1)} %get-tuple-element.39), channel_id=1, source_target_pairs={{0,16},{1,17},{2,18},{3,19},{4,20},{5,21},{6,22},{7,23},{8,24},{9,... | collective-permute-start | bytes 294920 | tf_op jit(solution)/shard_map/ppermute | solution.py:44
  105.6 9.5 %collective-permute-start.28 = (bf16[16,3072]{1,0:T(8,128)(2,1)S(1)}, bf16[16,3072]{1,0:T(8,128)(2,1)S(1)}, u32[]{:S(2)}, u32[]{:S(2)}) collective-permute-start(bf16[16,3072]{1,0:T(8,128)(2,1)S(1)} %get-tuple-element.40), channel_id=1, source_target_pairs={{0,24},{1,25},{2,26},{3,27},{4,28},{5,29},{6,30},{7,31},{8,16},{9,... | collective-permute-start | bytes 294920 | tf_op jit(solution)/shard_map/ppermute | solution.py:44

commit v2 on v1

--- a/solution.py
+++ b/solution.py
@@ -1,3 +1,4 @@
+import functools
 import math
 
 import jax
@@ -58,14 +59,18 @@
         elif kind == "any":
             specs.append(pl.BlockSpec(memory_space=pl.ANY))
             given.append(arg)
+        elif kind == "hbm":
+            specs.append(pl.BlockSpec(memory_space=pltpu.HBM))
+            given.append(pltpu.with_memory_space_constraint(arg, pltpu.HBM))
         else:
             specs.append(pl.BlockSpec(memory_space=pltpu.VMEM))
             given.append(in_vmem(arg))
     out_specs = []
     out_shape = []
     for kind, shape, dtype in outs:
-        if kind == "any":
-            out_specs.append(pl.BlockSpec(memory_space=pl.ANY))
+        if kind in ("any", "hbm"):
+            space = pl.ANY if kind == "any" else pltpu.VMEM
+            out_specs.append(pl.BlockSpec(memory_space=space))
             out_shape.append(jax.ShapeDtypeStruct(shape, dtype))
         else:
             out_specs.append(pl.BlockSpec(memory_space=pltpu.VMEM))
@@ -91,7 +96,7 @@
     return (center * lax.rsqrt(spread + 1e-06) * (1.0 + scale) + shift).astype(BF)
 
 
-def start_body(where, own, other, factors, normed, kept):
+def start_body(where, own, other, factors, fetched, normed, kept):
     xh = where[1]
     mine = pl.multiple_of(xh * PIECE, PIECE)
     theirs = pl.multiple_of((1 - xh) * PIECE, PIECE)
@@ -102,6 +107,17 @@
     normed[pl.ds(theirs, PIECE), :] = layer_norm(other[...].astype(F32), table)
 
 
+def fetch_body(w_qkv, w_mlp_in, w_attn_out, w_mlp_out, cache, w1, w2, kv, sems):
+    pairs = [(w_qkv.at[i], w1.at[:, i * HD:(i + 1) * HD]) for i in range(3)]
+    pairs += [(w_mlp_in, w1.at[:, 3 * HD:]), (w_attn_out, w2.at[:HD, :]), (w_mlp_out, w2.at[HD:, :])]
+    pairs += [(cache.at[i], kv.at[i]) for i in range(2)]
+    copies = [pltpu.make_async_copy(a, b, sems.at[i]) for i, (a, b) in enumerate(pairs)]
+    for c in copies:
+        c.start()
+    for c in copies:
+        c.wait()
+
+
 def head_norm(part, gain):
     wide = part.astype(F32)
     power = jnp.mean(wide * wide, axis=-1, keepdims=True)
@@ -113,16 +129,14 @@
 
 
 def block_body(
-    where, n0, n1, n2, n3, s0, s1, s2, s3, w1, w2, gains, cache, new_cache, joined, partial,
-    rows, kv, scores, sems,
+    last, where, n0, n2, n1, n3, s0, s2, s1, s3, w1, w2, gains, old, *rest,
 ):
-    patch = pl.multiple_of(where[0] * ROWS, ROWS)
-    xh, y, core = where[1], where[2], where[3]
-    reads = [
-        pltpu.make_async_copy(cache.at[i], kv.at[i], sems.at[i]) for i in range(2)
-    ]
-    for r in reads:
-        r.start()
+    if last:
+        kv, joined, partial, new_cache, rows, scores, sems = rest
+    else:
+        passing, kv, joined, partial, rows, scores = rest
+    patch = pl.multiple_of(where[4 if last else 0] * ROWS, ROWS)
+    y, core = where[2], where[3]
     for i, piece in enumerate((n0, n1, n2, n3, s0, s1, s2, s3)):
         rows[i * PAIR:(i + 1) * PAIR, :] = piece[...]
     h = rows[...]
@@ -134,8 +148,6 @@
     value = vm[:, :HD].astype(BF)
     joined[:, HD:2 * HD] = gelu(vm[:, HD:]).astype(BF)
     joined[:, 2 * HD:] = gelu(mm).astype(BF)
-    for r in reads:
-        r.wait()
     for dc in range(2):
         for dy in range(4):
             for x in range(2):
@@ -144,12 +156,9 @@
                 to = pl.multiple_of(patch + row, PIECE)
                 kv[0, pl.ds(to, PIECE), :] = key[at:at + PIECE, :]
                 kv[1, pl.ds(to, PIECE), :] = value[at:at + PIECE, :]
-    writes = [
-        pltpu.make_async_copy(
-            kv.at[i, pl.ds(patch, ROWS)], new_cache.at[i, pl.ds(patch, ROWS)], sems.at[2 + i]
-        )
-        for i in range(2)
-    ]
+    writes = []
+    if last:
+        writes = [pltpu.make_async_copy(kv.at[i], new_cache.at[i], sems.at[i]) for i in range(2)]
     for w in writes:
         w.start()
     step = 512
@@ -197,12 +206,12 @@
         o[...] = (mine[a:b, :] + came[a:b, :].astype(F32)).astype(BF)
 
 
-def column_body(mine, r1, r2, r3, factors, out):
+def column_body(mine, r1, r3, r2, factors, out):
     total = mine[...] + r1[...].astype(F32) + (r2[...].astype(F32) + r3[...].astype(F32))
     out[...] = (factors[2:3, :].astype(F32) * total).astype(BF)
 
 
-def last_column_body(where, mine, r1, r2, r3, factors, here, there):
+def last_column_body(where, mine, r1, r3, r2, factors, here, there):
     xh = where[1]
     gate = factors[2:3, :].astype(F32)
     for out, at in ((here, xh), (there, 1 - xh)):
@@ -224,21 +233,24 @@
     out[...] = (kept[...].astype(F32) + (p0[...].astype(F32) + p1[...].astype(F32))).astype(BF)
 
 
-def block(normed, where, w1, w2, gains, cache):
+def block(last, normed, passing, where, w1, w2, gains, kv):
     core_parts = [send_core(normed)]
-    parts = [normed] + [send_y(normed, -dy) for dy in (1, 2, 3)]
-    core_parts += [send_core(p) for p in parts[1:]]
-    new_cache, joined, partial = local_call(
-        block_body,
-        [("any", cache.shape, BF), ("vmem", (ROWS, 4 * HD), BF), ("vmem", (HALF, D), BF)],
-        [("smem", where)] + [("vmem", p) for p in parts + core_parts]
-        + [("vmem", w1), ("vmem", w2), ("vmem", gains), ("any", cache)],
-        scratch=[
-            pltpu.VMEM((ROWS, D), BF),
-            pltpu.VMEM((2, TOKENS, HD), BF),
-            pltpu.VMEM((ROWS, TOKENS), F32),
-            pltpu.SemaphoreType.DMA((4,)),
-        ],
+    n2 = send_y(normed, 2)
+    n3 = send_y(normed, 1)
+    n1 = send_y(normed, 3)
+    core_parts += [send_core(p) for p in (n2, n1, n3)]
+    outs = [("vmem", kv.shape, BF), ("vmem", (ROWS, 4 * HD), BF), ("vmem", (HALF, D), BF)]
+    scratch = [pltpu.VMEM((ROWS, D), BF), pltpu.VMEM((ROWS, TOKENS), F32)]
+    if last:
+        outs.append(("any", kv.shape, BF))
+        scratch.append(pltpu.SemaphoreType.DMA((2,)))
+    kv, joined, partial, *cache = local_call(
+        functools.partial(block_body, last),
+        outs,
+        [("smem", where)] + [("vmem", p) for p in [normed, n2, n1, n3] + core_parts]
+        + [("vmem", w1), ("vmem", w2), ("vmem", gains), ("vmem", kv)]
+        + ([] if last else [("any", passing)]),
+        scratch=scratch,
         limit=24,
         flops=2_200_000_000,
         moved=12_000_000,
@@ -262,7 +274,10 @@
         moved=3_000_000,
         name="pair_sum",
     )
-    return (o0, send_y(o1, 1), send_y(o2, 2), send_y(o3, 3)), new_cache
+    r2 = send_y(o2, 2)
+    r1 = send_y(o1, 1)
+    r3 = send_y(o3, 3)
+    return (o0, r1, r3, r2), kv, cache
 
 
 def labels(patch_of_slot, step_of_slot, section_id, round_id):
@@ -291,26 +306,39 @@
     xh, y, core = place // 8, (place // 2) % 4, place % 2
     own = slots[0]
     other = send_x(own)
-    where, factors = [], []
-    for r in range(2):
-        patch, step = labels(patch_of_slot, step_of_slot, section_id, r)
-        where.append(jnp.stack([patch, xh, y, core]).astype(jnp.int32))
-        factors.append(lax.dynamic_index_in_dim(modulation[0], step, 0, keepdims=False))
-    w1 = jnp.concatenate([w_qkv[0].reshape(D, 3 * HD), w_mlp_in[0]], axis=1)
-    w2 = jnp.concatenate([w_attn_out[0], w_mlp_out[0]], axis=0)
+    labelled = [labels(patch_of_slot, step_of_slot, section_id, r) for r in range(2)]
+    where = jnp.stack([labelled[0][0], xh, y, core, labelled[1][0]]).astype(jnp.int32)
+    factors = [
+        lax.dynamic_index_in_dim(modulation[0], step, 0, keepdims=False) for _, step in labelled
+    ]
     gains = qk_scale[0]
-    cache = kv_cache[0]
+    w1, w2, kv = local_call(
+        fetch_body,
+        [("vmem", (D, 6 * HD), BF), ("vmem", (4 * HD, D), BF), ("vmem", (2, TOKENS, HD), BF)],
+        [
+            ("hbm", jnp.transpose(w_qkv[0], (1, 0, 2))),
+            ("hbm", w_mlp_in[0]),
+            ("hbm", w_attn_out[0]),
+            ("hbm", w_mlp_out[0]),
+            ("hbm", kv_cache[0]),
+        ],
+        scratch=[pltpu.SemaphoreType.DMA((8,))],
+        flops=0,
+        moved=10_000_000,
+        name="fetch",
+    )
 
     normed, kept = local_call(
         start_body,
         [("vmem", (PAIR, D), BF)] * 2,
-        [("smem", where[0]), ("vmem", own), ("vmem", other), ("vmem", factors[0])],
+        [("smem", where), ("vmem", own), ("vmem", other), ("vmem", factors[0])]
+        + [("any", w1)],
         flops=1_000_000,
         moved=400_000,
         name="norm_first",
     )
     kept = send_on(kept, 0)
-    sums, cache = block(normed, where[0], w1, w2, gains, cache)
+    sums, kv, _ = block(False, normed, kept, where, w1, w2, gains, kv)
     (out,) = local_call(
         column_body,
         [("vmem", (PAIR, D), BF)],
@@ -323,17 +351,17 @@
     normed, kept = local_call(
         next_body,
         [("vmem", (PAIR, D), BF), ("vmem", (PIECE, D), BF)],
-        [("smem", where[1])] + [("vmem", a) for a in (kept, p0, p1, factors[1])],
+        [("smem", where)] + [("vmem", a) for a in (kept, p0, p1, factors[1])],
         flops=1_000_000,
         moved=800_000,
         name="norm_next",
     )
     kept = send_on(kept, 0)
-    sums, cache = block(normed, where[1], w1, w2, gains, cache)
+    sums, kv, (cache,) = block(True, normed, kept, where, w1, w2, gains, kv)
     here, there = local_call(
         last_column_body,
         [("vmem", (PIECE, D), BF)] * 2,
-        [("smem", where[1])] + [("vmem", a) for a in sums] + [("vmem", factors[1])],
+        [("smem", where)] + [("vmem", a) for a in sums] + [("vmem", factors[1])],
         flops=400_000,
         moved=1_200_000,
         name="column_last",
@@ -341,7 +369,7 @@
     p0, p1 = send_on(here, 0), send_on(there, 8)
     (out,) = local_call(
         final_body,
-        [("vmem", (PIECE, D), BF)],
+        [("hbm", (PIECE, D), BF)],
         [("vmem", a) for a in (kept, p0, p1)],
         flops=400_000,
         moved=400_000,

time: 117 us -> 108 us (0.923)
  local copies, waits for them, and re-layouts: 10.8 us -> 3.82 us
  other arithmetic: 4.5 us -> 0 us
  waiting for transfers between devices: 55.7 us -> 60.2 us
  starting transfers between devices: 26.6 us -> 23.1 us
  Pallas kernels: 16 us -> 17.9 us
    unnamed x17 -> x6, local copies, waits for them, and re-layouts: 6.63 us -> 0.04 us
    ppermute x12, waiting for transfers between devices: 28.9 us -> 32.7 us  [send_y(): lax.ppermute(x, 'sp', [(i, i & 9 | ((i >> 1 & 3) + by) % 4 << 1) for i in...]
    concatenate x2 -> x0, other arithmetic: 3.1 us -> none  [the longest x1 2.9 us: shards(): w1 = jnp.concatenate([w_qkv[0].reshape(D, 3 * HD), w_mlp_in[0]], axis=1)]
    pallas_call x11 -> x12, Pallas kernels: 16 us -> 17.9 us  [local_call(): pl.pallas_call(body, out_shape=out_shape, in_specs=specs, out_specs=out_s...]
    ppermute x12, starting transfers between devices: 18.8 us -> 17.1 us  [send_y(): lax.ppermute(x, 'sp', [(i, i & 9 | ((i >> 1 & 3) + by) % 4 << 1) for i in...]
    ppermute x6, waiting for transfers between devices: 21.1 us -> 22.8 us  [send_on(): return lax.ppermute(x, ('section', 'sp'), pairs)]
    ppermute x6, starting transfers between devices: 3.59 us -> 2.09 us  [send_on(): return lax.ppermute(x, ('section', 'sp'), pairs)]
    another operation x2 -> x0, other arithmetic: 1.4 us -> none  [shards(): where.append(jnp.stack([patch, xh, y, core]).astype(jnp.int32))]
  transfers between devices with their start and end apart: 29 -> 29, of which waited for: 19 -> 18; matrix products, arithmetic and copies ran while one was open for 10% -> 4% of each run, Pallas kernels for 2% -> 5%
where the time goes in v2:
time: 108 us; the launch traced here: 107 us
  waiting for transfers between devices  60.2 us (56%)
  starting transfers between devices  23.1 us (21%)
  Pallas kernels  17.9 us (17%)
  local copies, waits for them, and re-layouts  3.82 us (4%)
  between operations  2.18 us (2%)
    ppermute x12, waiting for transfers between devices, send_y(): lax.ppermute(x, 'sp', [(i, i & 9 | ((i >> 1 & 3) + by) % 4 << 1) for i in...  32.7 us
    ppermute x6, waiting for transfers between devices, send_on(): return lax.ppermute(x, ('section', 'sp'), pairs)  22.8 us
    pallas_call x12, Pallas kernels, local_call(): pl.pallas_call(body, out_shape=out_shape, in_specs=specs, out_specs=out_s...  17.9 us
    ppermute x12, starting transfers between devices, send_y(): lax.ppermute(x, 'sp', [(i, i & 9 | ((i >> 1 & 3) + by) % 4 << 1) for i in...  17.1 us
    ppermute x10, waiting for transfers between devices, send_core(): return lax.ppermute(x, 'sp', [(i, i ^ 1) for i in range(SPAN)])  4.68 us
    ppermute x1, starting transfers between devices, send_x(): return lax.ppermute(x, 'sp', [(i, i ^ 8) for i in range(SPAN)])  3.11 us
  transfers between devices with their start and end apart: 29, of which 18 were waited for; matrix products, arithmetic and copies ran while one was open for 4% of the time, Pallas kernels for 5%

profile of v2, /device:TPU:8, one launch (start us, length us, event | category | flops | bytes accessed | tf_op | source)
XLA Modules:
  0.0 107.3 jit_solution(7944254349578421751)
XLA Ops:
  0.6 3.1 %collective-permute-start = (bf16[16,3072]{1,0:T(8,128)(2,1)}, bf16[16,3072]{1,0:T(8,128)(2,1)S(1)}, u32[]{:S(2)}, u32[]{:S(2)}) collective-permute-start(bf16[16,3072]{1,0:T(8,128)(2,1)} %bitcast.26), channel_id=1, source_target_pairs={{0,8},{1,9},{2,10},{3,11},{4,12},{5,13},{6,14},{7,15},{8,0},{9,1},... | collective-permute-start | bytes 294920 | tf_op jit(solution)/shard_map/ppermute | solution.py:37
  3.7 1.4 %fusion = (s32[1]{0:T(128)}, s32[1]{0:T(128)}, s32[1]{0:T(128)}, s32[1]{0:T(128)}) fusion(s32[16]{0:T(128)} %param.12, s32[]{:T(128)S(6)} %select_n.39, s32[]{:T(128)S(6)} %select_n.34, s32[16]{0:T(128)} %param.11), kind=kLoop, calls=%fused_computation.4 | loop fusion | bytes 40 | tf_op jit(solution)/shard_map/jit(dynamic_index_in_dim)/dynamic_slice | solution.py:288
  6.4 1.1 constant_dynamic-slice_fusion
  7.6 1.3 %stack.17.where = s32[5]{0:T(128)S(1)} concatenate(s32[1]{0:T(128)} %get-tuple-element.54, s32[1]{0:T(128)} %bitcast, s32[1]{0:T(128)} %bitcast.1, s32[1]{0:T(128)} %bitcast.2, s32[1]{0:T(128)} %get-tuple-element.55), dimensions={0} | concatenate | bytes 40 | tf_op jit(solution)/shard_map/stack | solution.py:310
  8.9 3.9 %fetch.1 = (bf16[3072,768]{1,0:T(8,128)(2,1)S(1)}, bf16[512,3072]{1,0:T(8,128)(2,1)S(1)}, bf16[2,4096,128]{2,1,0:T(8,128)(2,1)S(1)}) custom-call(bf16[3,3072,128]{2,1,0:T(8,128)(2,1)} %bitcast.30, bf16[3072,384]{1,0:T(8,128)(2,1)} %bitcast.31, bf16[128,3072]{1,0:T(8,128)(2,1)} %bitcast.34, bf16[384,3072]{1,0:T(8,128)(2,1)} %bitcast.32, ...), custom_call_target="tpu_custom_call" | custom-call | bytes 10000000 | tf_op jit(solution)/shard_map/fetch/pallas_call | solution.py:78
  12.9 0.0 collective-permute-done.other
  12.9 0.0 copy-start.1
  12.9 0.8 norm_first.1
  13.7 1.7 %collective-permute-start.4 = (bf16[32,3072]{1,0:T(8,128)(2,1)S(1)}, bf16[32,3072]{1,0:T(8,128)(2,1)S(1)}, u32[]{:S(2)}, u32[]{:S(2)}) collective-permute-start(bf16[32,3072]{1,0:T(8,128)(2,1)S(1)} %get-tuple-element.27.n0), channel_id=1, source_target_pairs={{0,2},{1,3},{2,4},{3,5},{4,6},{5,7},{6,0},{7,1},{8,10},{9,11},{10,... | collective-permute-start | bytes 589832 | tf_op jit(solution)/shard_map/ppermute | solution.py:31
  15.4 0.4 collective-permute-start.3
  15.8 2.3 %collective-permute-start.2 = (bf16[32,3072]{1,0:T(8,128)(2,1)S(1)}, bf16[32,3072]{1,0:T(8,128)(2,1)S(1)}, u32[]{:S(2)}, u32[]{:S(2)}) collective-permute-start(bf16[32,3072]{1,0:T(8,128)(2,1)S(1)} %get-tuple-element.27.n0), channel_id=1, source_target_pairs={{0,4},{1,5},{2,6},{3,7},{4,0},{5,1},{6,2},{7,3},{8,12},{9,13},{10,... | collective-permute-start | bytes 589832 | tf_op jit(solution)/shard_map/ppermute | solution.py:31
  18.1 0.0 collective-permute-start.5
  18.1 0.6 collective-permute-start.1
  18.7 2.5 %collective-permute-done.4.n3 = bf16[32,3072]{1,0:T(8,128)(2,1)S(1)} collective-permute-done((bf16[32,3072]{1,0:T(8,128)(2,1)S(1)}, bf16[32,3072]{1,0:T(8,128)(2,1)S(1)}, u32[]{:S(2)}, u32[]{:S(2)}) %collective-permute-start.4) | collective-permute-done | bytes 196640 | tf_op jit(solution)/shard_map/ppermute | solution.py:31
  21.2 0.0 collective-permute-start.8
  21.2 1.3 %collective-permute-done.3.n1 = bf16[32,3072]{1,0:T(8,128)(2,1)S(1)} collective-permute-done((bf16[32,3072]{1,0:T(8,128)(2,1)S(1)}, bf16[32,3072]{1,0:T(8,128)(2,1)S(1)}, u32[]{:S(2)}, u32[]{:S(2)}) %collective-permute-start.3) | collective-permute-done | bytes 196640 | tf_op jit(solution)/shard_map/ppermute | solution.py:31
  22.5 0.0 collective-permute-start.7
  22.5 3.9 %collective-permute-done.2.n2 = bf16[32,3072]{1,0:T(8,128)(2,1)S(1)} collective-permute-done((bf16[32,3072]{1,0:T(8,128)(2,1)S(1)}, bf16[32,3072]{1,0:T(8,128)(2,1)S(1)}, u32[]{:S(2)}, u32[]{:S(2)}) %collective-permute-start.2) | collective-permute-done | bytes 196640 | tf_op jit(solution)/shard_map/ppermute | solution.py:31
  26.4 3.2 %collective-permute-done.1.rest_0_.kept = bf16[32,3072]{1,0:T(8,128)(2,1)S(1)} collective-permute-done((bf16[32,3072]{1,0:T(8,128)(2,1)S(1)}, bf16[32,3072]{1,0:T(8,128)(2,1)S(1)}, u32[]{:S(2)}, u32[]{:S(2)}) %collective-permute-start.1) | collective-permute-done | bytes 196640 | tf_op jit(solution)/shard_map/ppermute | solution.py:45
  29.6 0.0 collective-permute-done.5.s0
  29.6 4.7 %block.2 = (bf16[2,4096,128]{2,1,0:T(8,128)(2,1)S(1)}, bf16[256,512]{1,0:T(8,128)(2,1)S(1)}, bf16[128,3072]{1,0:T(8,128)(2,1)S(1)}) custom-call(s32[5]{0:T(128)S(1)} %stack.17.where, bf16[32,3072]{1,0:T(8,128)(2,1)S(1)} %get-tuple-element.27.n0, bf16[32,3072]{1,0:T(8,128)(2,1)S(1)} %collective-permute-done.2.n2, ...), custom_call_target="tpu_custom_call", output_to_operand_aliasing={{0}: (12, {})} | custom-call | flops 2200000000 | bytes 12000000 | tf_op jit(solution)/shard_map/block/pallas_call | solution.py:78
  34.3 0.1 collective-permute-start.9
  34.4 0.6 own_half.2.mine
  35.0 1.7 %collective-permute-done.9.came = bf16[128,3072]{1,0:T(8,128)(2,1)S(1)} collective-permute-done((bf16[128,3072]{1,0:T(8,128)(2,1)S(1)}, bf16[128,3072]{1,0:T(8,128)(2,1)S(1)}, u32[]{:S(2)}, u32[]{:S(2)}) %collective-permute-start.9) | collective-permute-done | bytes 786464 | tf_op jit(solution)/shard_map/ppermute | solution.py:27
  36.7 0.1 pair_sum.2
  36.8 0.9 collective-permute-start.10
  37.7 1.2 %collective-permute-start.11 = (bf16[32,3072]{1,0:T(8,128)(2,1)S(1)}, bf16[32,3072]{1,0:T(8,128)(2,1)S(1)}, u32[]{:S(2)}, u32[]{:S(2)}) collective-permute-start(bf16[32,3072]{1,0:T(8,128)(2,1)S(1)} %get-tuple-element.34), channel_id=1, source_target_pairs={{0,6},{1,7},{2,0},{3,1},{4,2},{5,3},{6,4},{7,5},{8,14},{9,15},{10,... | collective-permute-start | bytes 589832 | tf_op jit(solution)/shard_map/ppermute | solution.py:31
  38.9 1.4 %collective-permute-start.12 = (bf16[32,3072]{1,0:T(8,128)(2,1)S(1)}, bf16[32,3072]{1,0:T(8,128)(2,1)S(1)}, u32[]{:S(2)}, u32[]{:S(2)}) collective-permute-start(bf16[32,3072]{1,0:T(8,128)(2,1)S(1)} %get-tuple-element.35), channel_id=1, source_target_pairs={{0,4},{1,5},{2,6},{3,7},{4,0},{5,1},{6,2},{7,3},{8,12},{9,13},{10,... | collective-permute-start | bytes 589832 | tf_op jit(solution)/shard_map/ppermute | solution.py:31
  40.3 4.3 %collective-permute-done.10.r1 = bf16[32,3072]{1,0:T(8,128)(2,1)S(1)} collective-permute-done((bf16[32,3072]{1,0:T(8,128)(2,1)S(1)}, bf16[32,3072]{1,0:T(8,128)(2,1)S(1)}, u32[]{:S(2)}, u32[]{:S(2)}) %collective-permute-start.10) | collective-permute-done | bytes 196640 | tf_op jit(solution)/shard_map/ppermute | solution.py:31
  44.6 0.0 collective-permute-done.11.r3
  44.6 4.8 %collective-permute-done.12.r2 = bf16[32,3072]{1,0:T(8,128)(2,1)S(1)} collective-permute-done((bf16[32,3072]{1,0:T(8,128)(2,1)S(1)}, bf16[32,3072]{1,0:T(8,128)(2,1)S(1)}, u32[]{:S(2)}, u32[]{:S(2)}) %collective-permute-start.12) | collective-permute-done | bytes 196640 | tf_op jit(solution)/shard_map/ppermute | solution.py:31
  49.4 0.1 column_sum.1
  49.5 0.1 collective-permute-start.14
  49.6 0.3 collective-permute-start.13
  49.9 10.8 %collective-permute-done.14.p1 = bf16[32,3072]{1,0:T(8,128)(2,1)S(1)} collective-permute-done((bf16[32,3072]{1,0:T(8,128)(2,1)S(1)}, bf16[32,3072]{1,0:T(8,128)(2,1)S(1)}, u32[]{:S(2)}, u32[]{:S(2)}) %collective-permute-start.14) | collective-permute-done | bytes 196640 | tf_op jit(solution)/shard_map/ppermute | solution.py:45
  60.8 1.6 %collective-permute-done.13.p0 = bf16[32,3072]{1,0:T(8,128)(2,1)S(1)} collective-permute-done((bf16[32,3072]{1,0:T(8,128)(2,1)S(1)}, bf16[32,3072]{1,0:T(8,128)(2,1)S(1)}, u32[]{:S(2)}, u32[]{:S(2)}) %collective-permute-start.13) | collective-permute-done | bytes 196640 | tf_op jit(solution)/shard_map/ppermute | solution.py:45
  62.4 0.9 norm_next.1
  63.3 0.1 collective-permute-start.18
  63.4 2.0 %collective-permute-start.17 = (bf16[32,3072]{1,0:T(8,128)(2,1)S(1)}, bf16[32,3072]{1,0:T(8,128)(2,1)S(1)}, u32[]{:S(2)}, u32[]{:S(2)}) collective-permute-start(bf16[32,3072]{1,0:T(8,128)(2,1)S(1)} %get-tuple-element.37.n0), channel_id=1, source_target_pairs={{0,6},{1,7},{2,0},{3,1},{4,2},{5,3},{6,4},{7,5},{8,14},{9,15},{10,... | collective-permute-start | bytes 589832 | tf_op jit(solution)/shard_map/ppermute | solution.py:31
  65.4 1.5 %collective-permute-start.16 = (bf16[32,3072]{1,0:T(8,128)(2,1)S(1)}, bf16[32,3072]{1,0:T(8,128)(2,1)S(1)}, u32[]{:S(2)}, u32[]{:S(2)}) collective-permute-start(bf16[32,3072]{1,0:T(8,128)(2,1)S(1)} %get-tuple-element.37.n0), channel_id=1, source_target_pairs={{0,4},{1,5},{2,6},{3,7},{4,0},{5,1},{6,2},{7,3},{8,12},{9,13},{10,... | collective-permute-start | bytes 589832 | tf_op jit(solution)/shard_map/ppermute | solution.py:31
  66.9 0.0 collective-permute-start.19
  66.9 4.2 %collective-permute-done.18.n3 = bf16[32,3072]{1,0:T(8,128)(2,1)S(1)} collective-permute-done((bf16[32,3072]{1,0:T(8,128)(2,1)S(1)}, bf16[32,3072]{1,0:T(8,128)(2,1)S(1)}, u32[]{:S(2)}, u32[]{:S(2)}) %collective-permute-start.18) | collective-permute-done | bytes 196640 | tf_op jit(solution)/shard_map/ppermute | solution.py:31
  71.1 0.0 collective-permute-start.22
  71.1 0.0 collective-permute-done.17.n1
  71.1 0.5 collective-permute-start.21
  71.6 2.8 %collective-permute-done.16.n2 = bf16[32,3072]{1,0:T(8,128)(2,1)S(1)} collective-permute-done((bf16[32,3072]{1,0:T(8,128)(2,1)S(1)}, bf16[32,3072]{1,0:T(8,128)(2,1)S(1)}, u32[]{:S(2)}, u32[]{:S(2)}) %collective-permute-start.16) | collective-permute-done | bytes 196640 | tf_op jit(solution)/shard_map/ppermute | solution.py:31
  74.5 1.4 %collective-permute-done.20.s2 = bf16[32,3072]{1,0:T(8,128)(2,1)S(1)} collective-permute-done((bf16[32,3072]{1,0:T(8,128)(2,1)S(1)}, bf16[32,3072]{1,0:T(8,128)(2,1)S(1)}, u32[]{:S(2)}, u32[]{:S(2)}) %collective-permute-start.20) | collective-permute-done | bytes 196640 | tf_op jit(solution)/shard_map/ppermute | solution.py:27
  75.9 4.7 %block.3 = (bf16[2,4096,128]{2,1,0:T(8,128)(2,1)S(1)}, bf16[256,512]{1,0:T(8,128)(2,1)S(1)}, bf16[128,3072]{1,0:T(8,128)(2,1)S(1)}, bf16[2,4096,128]{2,1,0:T(8,128)(2,1)}) custom-call(s32[5]{0:T(128)S(1)} %stack.17.where, bf16[32,3072]{1,0:T(8,128)(2,1)S(1)} %get-tuple-element.37.n0, ...), custom_call_target="tpu_custom_call", output_to_operand_aliasing={{0}: (12, {})} | custom-call | flops 2200000000 | bytes 12000000 | tf_op jit(solution)/shard_map/block/pallas_call | solution.py:78
  80.6 0.2 collective-permute-start.23
  80.8 0.6 own_half.3.mine
  81.4 1.6 %collective-permute-done.23.came = bf16[128,3072]{1,0:T(8,128)(2,1)S(1)} collective-permute-done((bf16[128,3072]{1,0:T(8,128)(2,1)S(1)}, bf16[128,3072]{1,0:T(8,128)(2,1)S(1)}, u32[]{:S(2)}, u32[]{:S(2)}) %collective-permute-start.23) | collective-permute-done | bytes 786464 | tf_op jit(solution)/shard_map/ppermute | solution.py:27
  82.9 0.1 pair_sum.3
  83.1 0.5 collective-permute-start.24
  83.6 1.8 %collective-permute-start.25 = (bf16[32,3072]{1,0:T(8,128)(2,1)S(1)}, bf16[32,3072]{1,0:T(8,128)(2,1)S(1)}, u32[]{:S(2)}, u32[]{:S(2)}) collective-permute-start(bf16[32,3072]{1,0:T(8,128)(2,1)S(1)} %get-tuple-element.43), channel_id=1, source_target_pairs={{0,6},{1,7},{2,0},{3,1},{4,2},{5,3},{6,4},{7,5},{8,14},{9,15},{10,... | collective-permute-start | bytes 589832 | tf_op jit(solution)/shard_map/ppermute | solution.py:31
  85.4 3.2 %collective-permute-start.26 = (bf16[32,3072]{1,0:T(8,128)(2,1)S(1)}, bf16[32,3072]{1,0:T(8,128)(2,1)S(1)}, u32[]{:S(2)}, u32[]{:S(2)}) collective-permute-start(bf16[32,3072]{1,0:T(8,128)(2,1)S(1)} %get-tuple-element.44), channel_id=1, source_target_pairs={{0,4},{1,5},{2,6},{3,7},{4,0},{5,1},{6,2},{7,3},{8,12},{9,13},{10,... | collective-permute-start | bytes 589832 | tf_op jit(solution)/shard_map/ppermute | solution.py:31
  88.6 2.5 %collective-permute-done.24.r1 = bf16[32,3072]{1,0:T(8,128)(2,1)S(1)} collective-permute-done((bf16[32,3072]{1,0:T(8,128)(2,1)S(1)}, bf16[32,3072]{1,0:T(8,128)(2,1)S(1)}, u32[]{:S(2)}, u32[]{:S(2)}) %collective-permute-start.24) | collective-permute-done | bytes 196640 | tf_op jit(solution)/shard_map/ppermute | solution.py:31
  91.1 1.1 %collective-permute-done.25.r3 = bf16[32,3072]{1,0:T(8,128)(2,1)S(1)} collective-permute-done((bf16[32,3072]{1,0:T(8,128)(2,1)S(1)}, bf16[32,3072]{1,0:T(8,128)(2,1)S(1)}, u32[]{:S(2)}, u32[]{:S(2)}) %collective-permute-start.25) | collective-permute-done | bytes 196640 | tf_op jit(solution)/shard_map/ppermute | solution.py:31
  92.2 5.4 %collective-permute-done.26.r2 = bf16[32,3072]{1,0:T(8,128)(2,1)S(1)} collective-permute-done((bf16[32,3072]{1,0:T(8,128)(2,1)S(1)}, bf16[32,3072]{1,0:T(8,128)(2,1)S(1)}, u32[]{:S(2)}, u32[]{:S(2)}) %collective-permute-start.26) | collective-permute-done | bytes 196640 | tf_op jit(solution)/shard_map/ppermute | solution.py:31
  97.6 0.7 column_last.1
  98.2 0.1 collective-permute-start.27
  98.3 1.0 collective-permute-start.28
  99.4 5.9 %collective-permute-done.27.p0 = bf16[16,3072]{1,0:T(8,128)(2,1)S(1)} collective-permute-done((bf16[16,3072]{1,0:T(8,128)(2,1)S(1)}, bf16[16,3072]{1,0:T(8,128)(2,1)S(1)}, u32[]{:S(2)}, u32[]{:S(2)}) %collective-permute-start.27) | collective-permute-done | bytes 98336 | tf_op jit(solution)/shard_map/ppermute | solution.py:45
  105.3 1.3 %collective-permute-done.28.p1 = bf16[16,3072]{1,0:T(8,128)(2,1)S(1)} collective-permute-done((bf16[16,3072]{1,0:T(8,128)(2,1)S(1)}, bf16[16,3072]{1,0:T(8,128)(2,1)S(1)}, u32[]{:S(2)}, u32[]{:S(2)}) %collective-permute-start.28) | collective-permute-done | bytes 98336 | tf_op jit(solution)/shard_map/ppermute | solution.py:45
  106.6 0.7 residual_last.1
  (15 shorter events, 0.1 us)
Async XLA Ops:
  0.6 12.3 %collective-permute-start = (bf16[16,3072]{1,0:T(8,128)(2,1)}, bf16[16,3072]{1,0:T(8,128)(2,1)S(1)}, u32[]{:S(2)}, u32[]{:S(2)}) collective-permute-start(bf16[16,3072]{1,0:T(8,128)(2,1)} %bitcast.26), channel_id=1, source_target_pairs={{0,8},{1,9},{2,10},{3,11},{4,12},{5,13},{6,14},{7,15},{8,0},{9,1},... | collective-permute-start | bytes 294920 | tf_op jit(solution)/shard_map/ppermute | solution.py:37
  8.9 4.0 %copy-start = (bf16[1,16,3072]{2,1,0:T(8,128)(2,1)S(1)}, bf16[1,16,3072]{2,1,0:T(8,128)(2,1)}, u32[]{:S(2)}) copy-start(bf16[1,16,3072]{2,1,0:T(8,128)(2,1)} %param.10) | copy-start | bytes 294916
  12.9 16.7 %copy-start.1 = (bf16[1,2,128]{2,1,0:T(2,128)(2,1)S(1)}, bf16[1,2,128]{2,1,0:T(2,128)(2,1)}, u32[]{:S(2)}) copy-start(bf16[1,2,128]{2,1,0:T(2,128)(2,1)} %param.15) | copy-start | bytes 1540
  13.7 7.5 %collective-permute-start.4 = (bf16[32,3072]{1,0:T(8,128)(2,1)S(1)}, bf16[32,3072]{1,0:T(8,128)(2,1)S(1)}, u32[]{:S(2)}, u32[]{:S(2)}) collective-permute-start(bf16[32,3072]{1,0:T(8,128)(2,1)S(1)} %get-tuple-element.27.n0), channel_id=1, source_target_pairs={{0,2},{1,3},{2,4},{3,5},{4,6},{5,7},{6,0},{7,1},{8,10},{9,11},{10,... | collective-permute-start | bytes 589832 | tf_op jit(solution)/shard_map/ppermute | solution.py:31
  15.4 7.1 %collective-permute-start.3 = (bf16[32,3072]{1,0:T(8,128)(2,1)S(1)}, bf16[32,3072]{1,0:T(8,128)(2,1)S(1)}, u32[]{:S(2)}, u32[]{:S(2)}) collective-permute-start(bf16[32,3072]{1,0:T(8,128)(2,1)S(1)} %get-tuple-element.27.n0), channel_id=1, source_target_pairs={{0,6},{1,7},{2,0},{3,1},{4,2},{5,3},{6,4},{7,5},{8,14},{9,15},{10,... | collective-permute-start | bytes 589832 | tf_op jit(solution)/shard_map/ppermute | solution.py:31
  15.8 10.6 %collective-permute-start.2 = (bf16[32,3072]{1,0:T(8,128)(2,1)S(1)}, bf16[32,3072]{1,0:T(8,128)(2,1)S(1)}, u32[]{:S(2)}, u32[]{:S(2)}) collective-permute-start(bf16[32,3072]{1,0:T(8,128)(2,1)S(1)} %get-tuple-element.27.n0), channel_id=1, source_target_pairs={{0,4},{1,5},{2,6},{3,7},{4,0},{5,1},{6,2},{7,3},{8,12},{9,13},{10,... | collective-permute-start | bytes 589832 | tf_op jit(solution)/shard_map/ppermute | solution.py:31
  18.1 11.5 %collective-permute-start.5 = (bf16[32,3072]{1,0:T(8,128)(2,1)S(1)}, bf16[32,3072]{1,0:T(8,128)(2,1)S(1)}, u32[]{:S(2)}, u32[]{:S(2)}) collective-permute-start(bf16[32,3072]{1,0:T(8,128)(2,1)S(1)} %get-tuple-element.27.n0), channel_id=1, source_target_pairs={{0,1},{1,0},{2,3},{3,2},{4,5},{5,4},{6,7},{7,6},{8,9},{9,8},{10,11... | collective-permute-start | bytes 589832 | tf_op jit(solution)/shard_map/ppermute | solution.py:27
  18.1 11.5 %collective-permute-start.1 = (bf16[32,3072]{1,0:T(8,128)(2,1)S(1)}, bf16[32,3072]{1,0:T(8,128)(2,1)S(1)}, u32[]{:S(2)}, u32[]{:S(2)}) collective-permute-start(bf16[32,3072]{1,0:T(8,128)(2,1)S(1)} %get-tuple-element.26), channel_id=1, source_target_pairs={{0,16},{1,17},{2,18},{3,19},{4,20},{5,21},{6,22},{7,23},{8,24},{9,... | collective-permute-start | bytes 589832 | tf_op jit(solution)/shard_map/ppermute | solution.py:45
  21.2 8.4 %collective-permute-start.8 = (bf16[32,3072]{1,0:T(8,128)(2,1)S(1)}, bf16[32,3072]{1,0:T(8,128)(2,1)S(1)}, u32[]{:S(2)}, u32[]{:S(2)}) collective-permute-start(bf16[32,3072]{1,0:T(8,128)(2,1)S(1)} %collective-permute-done.4.n3), channel_id=1, source_target_pairs={{0,1},{1,0},{2,3},{3,2},{4,5},{5,4},{6,7},{7,6},{8,9},{9,8},{10,11... | collective-permute-start | bytes 589832 | tf_op jit(solution)/shard_map/ppermute | solution.py:27
  22.5 7.1 %collective-permute-start.7 = (bf16[32,3072]{1,0:T(8,128)(2,1)S(1)}, bf16[32,3072]{1,0:T(8,128)(2,1)S(1)}, u32[]{:S(2)}, u32[]{:S(2)}) collective-permute-start(bf16[32,3072]{1,0:T(8,128)(2,1)S(1)} %collective-permute-done.3.n1), channel_id=1, source_target_pairs={{0,1},{1,0},{2,3},{3,2},{4,5},{5,4},{6,7},{7,6},{8,9},{9,8},{10,11... | collective-permute-start | bytes 589832 | tf_op jit(solution)/shard_map/ppermute | solution.py:27
  26.4 3.2 %collective-permute-start.6 = (bf16[32,3072]{1,0:T(8,128)(2,1)S(1)}, bf16[32,3072]{1,0:T(8,128)(2,1)S(1)}, u32[]{:S(2)}, u32[]{:S(2)}) collective-permute-start(bf16[32,3072]{1,0:T(8,128)(2,1)S(1)} %collective-permute-done.2.n2), channel_id=1, source_target_pairs={{0,1},{1,0},{2,3},{3,2},{4,5},{5,4},{6,7},{7,6},{8,9},{9,8},{10,11... | collective-permute-start | bytes 589832 | tf_op jit(solution)/shard_map/ppermute | solution.py:27
  34.3 2.4 %collective-permute-start.9 = (bf16[128,3072]{1,0:T(8,128)(2,1)S(1)}, bf16[128,3072]{1,0:T(8,128)(2,1)S(1)}, u32[]{:S(2)}, u32[]{:S(2)}) collective-permute-start(bf16[128,3072]{1,0:T(8,128)(2,1)S(1)} %get-tuple-element.31), channel_id=1, source_target_pairs={{0,1},{1,0},{2,3},{3,2},{4,5},{5,4},{6,7},{7,6},{8,9},{9,8},{10,11... | collective-permute-start | bytes 2359304 | tf_op jit(solution)/shard_map/ppermute | solution.py:27
  36.8 7.8 %collective-permute-start.10 = (bf16[32,3072]{1,0:T(8,128)(2,1)S(1)}, bf16[32,3072]{1,0:T(8,128)(2,1)S(1)}, u32[]{:S(2)}, u32[]{:S(2)}) collective-permute-start(bf16[32,3072]{1,0:T(8,128)(2,1)S(1)} %get-tuple-element.33), channel_id=1, source_target_pairs={{0,2},{1,3},{2,4},{3,5},{4,6},{5,7},{6,0},{7,1},{8,10},{9,11},{10,... | collective-permute-start | bytes 589832 | tf_op jit(solution)/shard_map/ppermute | solution.py:31
  37.7 6.9 %collective-permute-start.11 = (bf16[32,3072]{1,0:T(8,128)(2,1)S(1)}, bf16[32,3072]{1,0:T(8,128)(2,1)S(1)}, u32[]{:S(2)}, u32[]{:S(2)}) collective-permute-start(bf16[32,3072]{1,0:T(8,128)(2,1)S(1)} %get-tuple-element.34), channel_id=1, source_target_pairs={{0,6},{1,7},{2,0},{3,1},{4,2},{5,3},{6,4},{7,5},{8,14},{9,15},{10,... | collective-permute-start | bytes 589832 | tf_op jit(solution)/shard_map/ppermute | solution.py:31
  38.9 10.5 %collective-permute-start.12 = (bf16[32,3072]{1,0:T(8,128)(2,1)S(1)}, bf16[32,3072]{1,0:T(8,128)(2,1)S(1)}, u32[]{:S(2)}, u32[]{:S(2)}) collective-permute-start(bf16[32,3072]{1,0:T(8,128)(2,1)S(1)} %get-tuple-element.35), channel_id=1, source_target_pairs={{0,4},{1,5},{2,6},{3,7},{4,0},{5,1},{6,2},{7,3},{8,12},{9,13},{10,... | collective-permute-start | bytes 589832 | tf_op jit(solution)/shard_map/ppermute | solution.py:31
  49.5 11.2 %collective-permute-start.14 = (bf16[32,3072]{1,0:T(8,128)(2,1)S(1)}, bf16[32,3072]{1,0:T(8,128)(2,1)S(1)}, u32[]{:S(2)}, u32[]{:S(2)}) collective-permute-start(bf16[32,3072]{1,0:T(8,128)(2,1)S(1)} %column_sum.1), channel_id=1, source_target_pairs={{0,24},{1,25},{2,26},{3,27},{4,28},{5,29},{6,30},{7,31},{8,16},{9,... | collective-permute-start | bytes 589832 | tf_op jit(solution)/shard_map/ppermute | solution.py:45
  49.6 12.7 %collective-permute-start.13 = (bf16[32,3072]{1,0:T(8,128)(2,1)S(1)}, bf16[32,3072]{1,0:T(8,128)(2,1)S(1)}, u32[]{:S(2)}, u32[]{:S(2)}) collective-permute-start(bf16[32,3072]{1,0:T(8,128)(2,1)S(1)} %column_sum.1), channel_id=1, source_target_pairs={{0,16},{1,17},{2,18},{3,19},{4,20},{5,21},{6,22},{7,23},{8,24},{9,... | collective-permute-start | bytes 589832 | tf_op jit(solution)/shard_map/ppermute | solution.py:45
  63.3 7.8 %collective-permute-start.18 = (bf16[32,3072]{1,0:T(8,128)(2,1)S(1)}, bf16[32,3072]{1,0:T(8,128)(2,1)S(1)}, u32[]{:S(2)}, u32[]{:S(2)}) collective-permute-start(bf16[32,3072]{1,0:T(8,128)(2,1)S(1)} %get-tuple-element.37.n0), channel_id=1, source_target_pairs={{0,2},{1,3},{2,4},{3,5},{4,6},{5,7},{6,0},{7,1},{8,10},{9,11},{10,... | collective-permute-start | bytes 589832 | tf_op jit(solution)/shard_map/ppermute | solution.py:31
  63.4 7.7 %collective-permute-start.17 = (bf16[32,3072]{1,0:T(8,128)(2,1)S(1)}, bf16[32,3072]{1,0:T(8,128)(2,1)S(1)}, u32[]{:S(2)}, u32[]{:S(2)}) collective-permute-start(bf16[32,3072]{1,0:T(8,128)(2,1)S(1)} %get-tuple-element.37.n0), channel_id=1, source_target_pairs={{0,6},{1,7},{2,0},{3,1},{4,2},{5,3},{6,4},{7,5},{8,14},{9,15},{10,... | collective-permute-start | bytes 589832 | tf_op jit(solution)/shard_map/ppermute | solution.py:31
  65.4 9.0 %collective-permute-start.16 = (bf16[32,3072]{1,0:T(8,128)(2,1)S(1)}, bf16[32,3072]{1,0:T(8,128)(2,1)S(1)}, u32[]{:S(2)}, u32[]{:S(2)}) collective-permute-start(bf16[32,3072]{1,0:T(8,128)(2,1)S(1)} %get-tuple-element.37.n0), channel_id=1, source_target_pairs={{0,4},{1,5},{2,6},{3,7},{4,0},{5,1},{6,2},{7,3},{8,12},{9,13},{10,... | collective-permute-start | bytes 589832 | tf_op jit(solution)/shard_map/ppermute | solution.py:31
  66.9 7.5 %collective-permute-start.19 = (bf16[32,3072]{1,0:T(8,128)(2,1)S(1)}, bf16[32,3072]{1,0:T(8,128)(2,1)S(1)}, u32[]{:S(2)}, u32[]{:S(2)}) collective-permute-start(bf16[32,3072]{1,0:T(8,128)(2,1)S(1)} %get-tuple-element.37.n0), channel_id=1, source_target_pairs={{0,1},{1,0},{2,3},{3,2},{4,5},{5,4},{6,7},{7,6},{8,9},{9,8},{10,11... | collective-permute-start | bytes 589832 | tf_op jit(solution)/shard_map/ppermute | solution.py:27
  71.1 3.3 %collective-permute-start.22 = (bf16[32,3072]{1,0:T(8,128)(2,1)S(1)}, bf16[32,3072]{1,0:T(8,128)(2,1)S(1)}, u32[]{:S(2)}, u32[]{:S(2)}) collective-permute-start(bf16[32,3072]{1,0:T(8,128)(2,1)S(1)} %collective-permute-done.18.n3), channel_id=1, source_target_pairs={{0,1},{1,0},{2,3},{3,2},{4,5},{5,4},{6,7},{7,6},{8,9},{9,8},{10,11... | collective-permute-start | bytes 589832 | tf_op jit(solution)/shard_map/ppermute | solution.py:27
  71.1 3.3 %collective-permute-start.21 = (bf16[32,3072]{1,0:T(8,128)(2,1)S(1)}, bf16[32,3072]{1,0:T(8,128)(2,1)S(1)}, u32[]{:S(2)}, u32[]{:S(2)}) collective-permute-start(bf16[32,3072]{1,0:T(8,128)(2,1)S(1)} %collective-permute-done.17.n1), channel_id=1, source_target_pairs={{0,1},{1,0},{2,3},{3,2},{4,5},{5,4},{6,7},{7,6},{8,9},{9,8},{10,11... | collective-permute-start | bytes 589832 | tf_op jit(solution)/shard_map/ppermute | solution.py:27
  74.4 1.4 %collective-permute-start.20 = (bf16[32,3072]{1,0:T(8,128)(2,1)S(1)}, bf16[32,3072]{1,0:T(8,128)(2,1)S(1)}, u32[]{:S(2)}, u32[]{:S(2)}) collective-permute-start(bf16[32,3072]{1,0:T(8,128)(2,1)S(1)} %collective-permute-done.16.n2), channel_id=1, source_target_pairs={{0,1},{1,0},{2,3},{3,2},{4,5},{5,4},{6,7},{7,6},{8,9},{9,8},{10,11... | collective-permute-start | bytes 589832 | tf_op jit(solution)/shard_map/ppermute | solution.py:27
  80.6 2.4 %collective-permute-start.23 = (bf16[128,3072]{1,0:T(8,128)(2,1)S(1)}, bf16[128,3072]{1,0:T(8,128)(2,1)S(1)}, u32[]{:S(2)}, u32[]{:S(2)}) collective-permute-start(bf16[128,3072]{1,0:T(8,128)(2,1)S(1)} %get-tuple-element.40), channel_id=1, source_target_pairs={{0,1},{1,0},{2,3},{3,2},{4,5},{5,4},{6,7},{7,6},{8,9},{9,8},{10,11... | collective-permute-start | bytes 2359304 | tf_op jit(solution)/shard_map/ppermute | solution.py:27
  83.1 8.0 %collective-permute-start.24 = (bf16[32,3072]{1,0:T(8,128)(2,1)S(1)}, bf16[32,3072]{1,0:T(8,128)(2,1)S(1)}, u32[]{:S(2)}, u32[]{:S(2)}) collective-permute-start(bf16[32,3072]{1,0:T(8,128)(2,1)S(1)} %get-tuple-element.42), channel_id=1, source_target_pairs={{0,2},{1,3},{2,4},{3,5},{4,6},{5,7},{6,0},{7,1},{8,10},{9,11},{10,... | collective-permute-start | bytes 589832 | tf_op jit(solution)/shard_map/ppermute | solution.py:31
  83.6 8.6 %collective-permute-start.25 = (bf16[32,3072]{1,0:T(8,128)(2,1)S(1)}, bf16[32,3072]{1,0:T(8,128)(2,1)S(1)}, u32[]{:S(2)}, u32[]{:S(2)}) collective-permute-start(bf16[32,3072]{1,0:T(8,128)(2,1)S(1)} %get-tuple-element.43), channel_id=1, source_target_pairs={{0,6},{1,7},{2,0},{3,1},{4,2},{5,3},{6,4},{7,5},{8,14},{9,15},{10,... | collective-permute-start | bytes 589832 | tf_op jit(solution)/shard_map/ppermute | solution.py:31
  85.4 12.2 %collective-permute-start.26 = (bf16[32,3072]{1,0:T(8,128)(2,1)S(1)}, bf16[32,3072]{1,0:T(8,128)(2,1)S(1)}, u32[]{:S(2)}, u32[]{:S(2)}) collective-permute-start(bf16[32,3072]{1,0:T(8,128)(2,1)S(1)} %get-tuple-element.44), channel_id=1, source_target_pairs={{0,4},{1,5},{2,6},{3,7},{4,0},{5,1},{6,2},{7,3},{8,12},{9,13},{10,... | collective-permute-start | bytes 589832 | tf_op jit(solution)/shard_map/ppermute | solution.py:31
  88.6 10.7 %collective-permute-start.15 = (bf16[16,3072]{1,0:T(8,128)(2,1)S(1)}, bf16[16,3072]{1,0:T(8,128)(2,1)S(1)}, u32[]{:S(2)}, u32[]{:S(2)}) collective-permute-start(bf16[16,3072]{1,0:T(8,128)(2,1)S(1)} %get-tuple-element.36), channel_id=1, source_target_pairs={{0,16},{1,17},{2,18},{3,19},{4,20},{5,21},{6,22},{7,23},{8,24},{9,... | collective-permute-start | bytes 294920 | tf_op jit(solution)/shard_map/ppermute | solution.py:45
  98.2 7.0 %collective-permute-start.27 = (bf16[16,3072]{1,0:T(8,128)(2,1)S(1)}, bf16[16,3072]{1,0:T(8,128)(2,1)S(1)}, u32[]{:S(2)}, u32[]{:S(2)}) collective-permute-start(bf16[16,3072]{1,0:T(8,128)(2,1)S(1)} %get-tuple-element.45), channel_id=1, source_target_pairs={{0,16},{1,17},{2,18},{3,19},{4,20},{5,21},{6,22},{7,23},{8,24},{9,... | collective-permute-start | bytes 294920 | tf_op jit(solution)/shard_map/ppermute | solution.py:45
  98.3 8.3 %collective-permute-start.28 = (bf16[16,3072]{1,0:T(8,128)(2,1)S(1)}, bf16[16,3072]{1,0:T(8,128)(2,1)S(1)}, u32[]{:S(2)}, u32[]{:S(2)}) collective-permute-start(bf16[16,3072]{1,0:T(8,128)(2,1)S(1)} %get-tuple-element.46), channel_id=1, source_target_pairs={{0,24},{1,25},{2,26},{3,27},{4,28},{5,29},{6,30},{7,31},{8,16},{9,... | collective-permute-start | bytes 294920 | tf_op jit(solution)/shard_map/ppermute | solution.py:45

commit v3 on v2

--- a/solution.py
+++ b/solution.py
@@ -21,6 +21,7 @@
 BF = jnp.bfloat16
 F32 = jnp.float32
 MIB = 1 << 20
+EXPONENT = 1.0 / (math.sqrt(HD) * math.log(2.0))
 
 
 def send_core(x):
@@ -91,13 +92,24 @@
 def layer_norm(wide, factors):
     center = wide - jnp.mean(wide, axis=-1, keepdims=True)
     spread = jnp.mean(center * center, axis=-1, keepdims=True)
-    shift = factors[0:1, :].astype(F32)
-    scale = factors[1:2, :].astype(F32)
+    shift = factors[0:1, :]
+    scale = factors[1:2, :]
     return (center * lax.rsqrt(spread + 1e-06) * (1.0 + scale) + shift).astype(BF)
 
 
-def start_body(where, own, other, factors, fetched, normed, kept):
-    xh = where[1]
+def spot():
+    place = lax.axis_index("sp")
+    return lax.div(place, 8), lax.rem(lax.div(place, 2), 4), lax.rem(place, 2)
+
+
+def turn(round_id):
+    section = lax.axis_index("section")
+    anchor = lax.rem(section - round_id + SECTIONS, SECTIONS)
+    return anchor, jnp.where(section < round_id, 1, 0)
+
+
+def start_body(own, other, factors, normed, kept):
+    xh, _, _ = spot()
     mine = pl.multiple_of(xh * PIECE, PIECE)
     theirs = pl.multiple_of((1 - xh) * PIECE, PIECE)
     kept[pl.ds(mine, PIECE), :] = own[...]
@@ -107,14 +119,23 @@
     normed[pl.ds(theirs, PIECE), :] = layer_norm(other[...].astype(F32), table)
 
 
-def fetch_body(w_qkv, w_mlp_in, w_attn_out, w_mlp_out, cache, w1, w2, kv, sems):
-    pairs = [(w_qkv.at[i], w1.at[:, i * HD:(i + 1) * HD]) for i in range(3)]
-    pairs += [(w_mlp_in, w1.at[:, 3 * HD:]), (w_attn_out, w2.at[:HD, :]), (w_mlp_out, w2.at[HD:, :])]
+def fetch_body(steps, modulation, w_qkv, w_mlp_in, cache, w1, first, second, kv, table, sems):
+    pairs = [(modulation, table)]
+    pairs += [(w_qkv.at[i], w1.at[:, i * HD:(i + 1) * HD]) for i in range(3)]
+    pairs += [(w_mlp_in, w1.at[:, 3 * HD:])]
     pairs += [(cache.at[i], kv.at[i]) for i in range(2)]
     copies = [pltpu.make_async_copy(a, b, sems.at[i]) for i, (a, b) in enumerate(pairs)]
     for c in copies:
         c.start()
-    for c in copies:
+    copies[0].wait()
+    for round_id, out in ((0, first), (1, second)):
+        anchor, late = turn(round_id)
+        step = steps[anchor] + late
+        for k in range(3):
+            plane = table[k].astype(F32)
+            hit = lax.broadcasted_iota(jnp.int32, plane.shape, 0) == step
+            out[k:k + 1, :] = jnp.sum(jnp.where(hit, plane, 0.0), axis=0, keepdims=True)
+    for c in copies[1:]:
         c.wait()
 
 
@@ -128,15 +149,44 @@
     return jax.nn.gelu(x, approximate=True)
 
 
-def block_body(
-    last, where, n0, n2, n1, n3, s0, s2, s1, s3, w1, w2, gains, old, *rest,
-):
+def attend(query, kv, scores):
+    rows = query.shape[0]
+    step = 512
+    top = None
+    for j in range(TOKENS // step):
+        s = lax.dot_general(
+            query, kv[0, j * step:(j + 1) * step, :], (((1,), (1,)), ((), ())),
+            preferred_element_type=F32,
+        )
+        scores[0:rows, j * step:(j + 1) * step] = s
+        best = jnp.max(s, axis=-1, keepdims=True)
+        top = best if top is None else jnp.maximum(top, best)
+    total = None
+    mixed = None
+    for j in range(TOKENS // step):
+        e = jnp.exp2((scores[0:rows, j * step:(j + 1) * step] - top) * EXPONENT)
+        t = jnp.sum(e, axis=-1, keepdims=True)
+        m = jnp.dot(
+            e.astype(BF), kv[1, j * step:(j + 1) * step, :], preferred_element_type=F32
+        )
+        total = t if total is None else total + t
+        mixed = m if mixed is None else mixed + m
+    return (mixed / total).astype(BF)
+
+
+def block_body(last, patches, n0, n3, n1, n2, s0, s3, s1, s2, w1, gains, *rest):
     if last:
-        kv, joined, partial, new_cache, rows, scores, sems = rest
+        (old, w2, kv, joined, queries, partial, new_cache, rows, scores, sems) = rest
+        reads = []
     else:
-        passing, kv, joined, partial, rows, scores = rest
-    patch = pl.multiple_of(where[4 if last else 0] * ROWS, ROWS)
-    y, core = where[2], where[3]
+        (old, w_attn_out, w_mlp_out, kv, joined, queries, partial, w2, rows, scores, sems) = rest
+        pairs = [(w_attn_out, w2.at[:HD, :]), (w_mlp_out, w2.at[HD:, :])]
+        reads = [pltpu.make_async_copy(a, b, sems.at[i]) for i, (a, b) in enumerate(pairs)]
+    for r in reads:
+        r.start()
+    anchor, _ = turn(1 if last else 0)
+    patch = pl.multiple_of(patches[anchor] * ROWS, ROWS)
+    _, y, core = spot()
     for i, piece in enumerate((n0, n1, n2, n3, s0, s1, s2, s3)):
         rows[i * PAIR:(i + 1) * PAIR, :] = piece[...]
     h = rows[...]
@@ -161,27 +211,10 @@
         writes = [pltpu.make_async_copy(kv.at[i], new_cache.at[i], sems.at[i]) for i in range(2)]
     for w in writes:
         w.start()
-    step = 512
-    top = None
-    for j in range(TOKENS // step):
-        s = lax.dot_general(
-            query, kv[0, j * step:(j + 1) * step, :], (((1,), (1,)), ((), ())),
-            preferred_element_type=F32,
-        ) * (1.0 / math.sqrt(HD))
-        scores[:, j * step:(j + 1) * step] = s
-        best = jnp.max(s, axis=-1, keepdims=True)
-        top = best if top is None else jnp.maximum(top, best)
-    total = None
-    mixed = None
-    for j in range(TOKENS // step):
-        e = jnp.exp(scores[:, j * step:(j + 1) * step] - top)
-        t = jnp.sum(e, axis=-1, keepdims=True)
-        m = jnp.dot(
-            e.astype(BF), kv[1, j * step:(j + 1) * step, :], preferred_element_type=F32
-        )
-        total = t if total is None else total + t
-        mixed = m if mixed is None else mixed + m
-    joined[:, 0:HD] = (mixed / total).astype(BF)
+    queries[...] = query[:HALF, :]
+    joined[HALF:, 0:HD] = attend(query[HALF:, :], kv, scores)
+    for r in reads:
+        r.wait()
     theirs = joined[HALF:, :]
     for j in range(D // 256):
         partial[:, j * 256:(j + 1) * 256] = jnp.dot(
@@ -191,8 +224,9 @@
         w.wait()
 
 
-def own_body(joined, w2, partial):
-    mine = joined[:HALF, :]
+def own_body(queries, kv, joined, w2, partial, scores):
+    mixed = attend(queries[...], kv, scores)
+    mine = jnp.concatenate([mixed, joined[:HALF, HD:]], axis=1)
     for j in range(D // 256):
         partial[:, j * 256:(j + 1) * 256] = jnp.dot(
             mine, w2[:, j * 256:(j + 1) * 256], preferred_element_type=F32
@@ -206,14 +240,14 @@
         o[...] = (mine[a:b, :] + came[a:b, :].astype(F32)).astype(BF)
 
 
-def column_body(mine, r1, r3, r2, factors, out):
+def column_body(mine, r2, r3, r1, factors, out):
     total = mine[...] + r1[...].astype(F32) + (r2[...].astype(F32) + r3[...].astype(F32))
-    out[...] = (factors[2:3, :].astype(F32) * total).astype(BF)
-
-
-def last_column_body(where, mine, r1, r3, r2, factors, here, there):
-    xh = where[1]
-    gate = factors[2:3, :].astype(F32)
+    out[...] = (factors[2:3, :] * total).astype(BF)
+
+
+def last_column_body(mine, r2, r3, r1, factors, here, there):
+    xh, _, _ = spot()
+    gate = factors[2:3, :]
     for out, at in ((here, xh), (there, 1 - xh)):
         rows = pl.ds(pl.multiple_of(at * PIECE, PIECE), PIECE)
         total = mine[rows, :] + r1[rows, :].astype(F32)
@@ -221,8 +255,8 @@
         out[...] = (gate * total).astype(BF)
 
 
-def next_body(where, kept, p0, p1, factors, normed, own):
-    xh = where[1]
+def next_body(kept, p0, p1, factors, normed, own):
+    xh, _, _ = spot()
     new = (kept[...].astype(F32) + (p0[...].astype(F32) + p1[...].astype(F32))).astype(BF)
     wide = new.astype(F32)
     normed[...] = layer_norm(wide, factors[...])
@@ -233,36 +267,45 @@
     out[...] = (kept[...].astype(F32) + (p0[...].astype(F32) + p1[...].astype(F32))).astype(BF)
 
 
-def block(last, normed, passing, where, w1, w2, gains, kv):
+def block(last, normed, patches, w1, gains, kv, weights):
     core_parts = [send_core(normed)]
     n2 = send_y(normed, 2)
     n3 = send_y(normed, 1)
     n1 = send_y(normed, 3)
-    core_parts += [send_core(p) for p in (n2, n1, n3)]
-    outs = [("vmem", kv.shape, BF), ("vmem", (ROWS, 4 * HD), BF), ("vmem", (HALF, D), BF)]
-    scratch = [pltpu.VMEM((ROWS, D), BF), pltpu.VMEM((ROWS, TOKENS), F32)]
-    if last:
-        outs.append(("any", kv.shape, BF))
-        scratch.append(pltpu.SemaphoreType.DMA((2,)))
-    kv, joined, partial, *cache = local_call(
+    core_parts += [send_core(p) for p in (n3, n1, n2)]
+    cache_shape = (2, TOKENS, HD)
+    outs = [
+        ("vmem", cache_shape, BF),
+        ("vmem", (ROWS, 4 * HD), BF),
+        ("vmem", (HALF, HD), BF),
+        ("vmem", (HALF, D), BF),
+    ]
+    outs.append(("any", cache_shape, BF) if last else ("vmem", (4 * HD, D), BF))
+    kind = "vmem" if last else "hbm"
+    kv, joined, queries, partial, fifth = local_call(
         functools.partial(block_body, last),
         outs,
-        [("smem", where)] + [("vmem", p) for p in [normed, n2, n1, n3] + core_parts]
-        + [("vmem", w1), ("vmem", w2), ("vmem", gains), ("vmem", kv)]
-        + ([] if last else [("any", passing)]),
-        scratch=scratch,
+        [("smem", patches)] + [("vmem", p) for p in [normed, n3, n1, n2] + core_parts]
+        + [("vmem", w1), ("vmem", gains), ("vmem", kv)] + [(kind, a) for a in weights],
+        scratch=[
+            pltpu.VMEM((ROWS, D), BF),
+            pltpu.VMEM((HALF, TOKENS), F32),
+            pltpu.SemaphoreType.DMA((2,)),
+        ],
         limit=24,
         flops=2_200_000_000,
         moved=12_000_000,
         name="block",
-        aliases={12: 0},
-    )
+        aliases={11: 0},
+    )
+    w2 = weights[0] if last else fifth
     came = send_core(partial)
     (mine,) = local_call(
         own_body,
         [("vmem", (HALF, D), F32)],
-        [("vmem", joined), ("vmem", w2)],
-        flops=400_000_000,
+        [("vmem", queries), ("vmem", kv), ("vmem", joined), ("vmem", w2)],
+        scratch=[pltpu.VMEM((HALF, TOKENS), F32)],
+        flops=700_000_000,
         moved=4_700_000,
         name="own_half",
     )
@@ -277,16 +320,7 @@
     r2 = send_y(o2, 2)
     r1 = send_y(o1, 1)
     r3 = send_y(o3, 3)
-    return (o0, r1, r3, r2), kv, cache
-
-
-def labels(patch_of_slot, step_of_slot, section_id, round_id):
-    anchor = section_id - round_id
-    wrapped = (anchor < 0).astype(jnp.int32)
-    anchor = anchor + wrapped * SECTIONS
-    patch_id = lax.dynamic_index_in_dim(patch_of_slot, anchor, 0, keepdims=False)
-    timestep = lax.dynamic_index_in_dim(step_of_slot, anchor, 0, keepdims=False) + wrapped
-    return patch_id, timestep
+    return (o0, r2, r3, r1), kv, fifth
 
 
 def shards(
@@ -301,44 +335,43 @@
     w_mlp_out,
     kv_cache,
 ):
-    section_id = lax.axis_index("section")
-    place = lax.axis_index("sp")
-    xh, y, core = place // 8, (place // 2) % 4, place % 2
     own = slots[0]
     other = send_x(own)
-    labelled = [labels(patch_of_slot, step_of_slot, section_id, r) for r in range(2)]
-    where = jnp.stack([labelled[0][0], xh, y, core, labelled[1][0]]).astype(jnp.int32)
-    factors = [
-        lax.dynamic_index_in_dim(modulation[0], step, 0, keepdims=False) for _, step in labelled
-    ]
     gains = qk_scale[0]
-    w1, w2, kv = local_call(
+    w1, first, second, kv = local_call(
         fetch_body,
-        [("vmem", (D, 6 * HD), BF), ("vmem", (4 * HD, D), BF), ("vmem", (2, TOKENS, HD), BF)],
         [
+            ("vmem", (D, 6 * HD), BF),
+            ("vmem", (3, D), F32),
+            ("vmem", (3, D), F32),
+            ("vmem", (2, TOKENS, HD), BF),
+        ],
+        [
+            ("smem", step_of_slot),
+            ("hbm", jnp.transpose(modulation[0], (1, 0, 2))),
             ("hbm", jnp.transpose(w_qkv[0], (1, 0, 2))),
             ("hbm", w_mlp_in[0]),
-            ("hbm", w_attn_out[0]),
-            ("hbm", w_mlp_out[0]),
             ("hbm", kv_cache[0]),
         ],
-        scratch=[pltpu.SemaphoreType.DMA((8,))],
+        scratch=[pltpu.VMEM((3, modulation.shape[1], D), BF), pltpu.SemaphoreType.DMA((7,))],
         flops=0,
-        moved=10_000_000,
+        moved=7_000_000,
         name="fetch",
     )
+    factors = (first, second)
 
     normed, kept = local_call(
         start_body,
         [("vmem", (PAIR, D), BF)] * 2,
-        [("smem", where), ("vmem", own), ("vmem", other), ("vmem", factors[0])]
-        + [("any", w1)],
+        [("vmem", own), ("vmem", other), ("vmem", factors[0])],
         flops=1_000_000,
         moved=400_000,
         name="norm_first",
     )
     kept = send_on(kept, 0)
-    sums, kv, _ = block(False, normed, kept, where, w1, w2, gains, kv)
+    sums, kv, w2 = block(
+        False, normed, patch_of_slot, w1, gains, kv, (w_attn_out[0], w_mlp_out[0])
+    )
     (out,) = local_call(
         column_body,
         [("vmem", (PAIR, D), BF)],
@@ -351,17 +384,17 @@
     normed, kept = local_call(
         next_body,
         [("vmem", (PAIR, D), BF), ("vmem", (PIECE, D), BF)],
-        [("smem", where)] + [("vmem", a) for a in (kept, p0, p1, factors[1])],
+        [("vmem", a) for a in (kept, p0, p1, factors[1])],
         flops=1_000_000,
         moved=800_000,
         name="norm_next",
     )
     kept = send_on(kept, 0)
-    sums, kv, (cache,) = block(True, normed, kept, where, w1, w2, gains, kv)
+    sums, _, cache = block(True, normed, patch_of_slot, w1, gains, kv, (w2,))
     here, there = local_call(
         last_column_body,
         [("vmem", (PIECE, D), BF)] * 2,
-        [("smem", where)] + [("vmem", a) for a in sums] + [("vmem", factors[1])],
+        [("vmem", a) for a in sums] + [("vmem", factors[1])],
         flops=400_000,
         moved=1_200_000,
         name="column_last",

time: 108 us -> 101 us (0.935)
  waiting for transfers between devices: 60.2 us -> 56.1 us
  starting transfers between devices: 23.1 us -> 26.6 us
  local copies, waits for them, and re-layouts: 3.82 us -> 0.67 us
  between operations: 2.18 us -> 0.76 us
    dynamic_slice x2 -> x0, local copies, waits for them, and re-layouts: 2.45 us -> none  [the longest x1 1.38 us: labels(): lax.dynamic_index_in_dim(step_of_slot, anchor, 0, keepdims=False) + wrapped]
    ppermute x6, starting transfers between devices: 2.09 us -> 4.14 us  [send_on(): return lax.ppermute(x, ('section', 'sp'), pairs)]
    ppermute x10, waiting for transfers between devices: 4.68 us -> 3.01 us  [send_core(): return lax.ppermute(x, 'sp', [(i, i ^ 1) for i in range(SPAN)])]
    ppermute x6, waiting for transfers between devices: 22.8 us -> 21.3 us  [send_on(): return lax.ppermute(x, ('section', 'sp'), pairs)]
    another operation x1 -> x0, local copies, waits for them, and re-layouts: 1.34 us -> none  [shards(): jnp.stack([labelled[0][0], xh, y, core, labelled[1][0]]).astype(jnp.int32)]
  transfers between devices with their start and end apart: 29 -> 29, of which waited for: 18 -> 19; matrix products, arithmetic and copies ran while one was open for 4% -> 0% of each run, Pallas kernels for 5% -> 7%
where the time goes in v3:
time: 101 us
  waiting for transfers between devices  56.1 us (56%)
  starting transfers between devices  26.6 us (26%)
  Pallas kernels  17 us (17%)
    ppermute x12, waiting for transfers between devices, send_y(): lax.ppermute(x, 'sp', [(i, i & 9 | ((i >> 1 & 3) + by) % 4 << 1) for i in...  31.9 us
    ppermute x6, waiting for transfers between devices, send_on(): return lax.ppermute(x, ('section', 'sp'), pairs)  21.3 us
    ppermute x12, starting transfers between devices, send_y(): lax.ppermute(x, 'sp', [(i, i & 9 | ((i >> 1 & 3) + by) % 4 << 1) for i in...  17.6 us
    pallas_call x12, Pallas kernels, local_call(): pl.pallas_call(body, out_shape=out_shape, in_specs=specs, out_specs=out_s...  17 us
    ppermute x6, starting transfers between devices, send_on(): return lax.ppermute(x, ('section', 'sp'), pairs)  4.14 us
    ppermute x1, starting transfers between devices, send_x(): return lax.ppermute(x, 'sp', [(i, i ^ 8) for i in range(SPAN)])  3.11 us
    ppermute x10, waiting for transfers between devices, send_core(): return lax.ppermute(x, 'sp', [(i, i ^ 1) for i in range(SPAN)])  3.01 us
  transfers between devices with their start and end apart: 29, of which 19 were waited for; matrix products, arithmetic and copies ran while one was open for 0% of the time, Pallas kernels for 7%

profile of v3, /device:TPU:8, one launch (start us, length us, event | category | flops | bytes accessed | tf_op | source)
XLA Modules:
  0.0 101.2 jit_solution(4484623964334797947)
XLA Ops:
  0.6 3.1 %collective-permute-start = (bf16[16,3072]{1,0:T(8,128)(2,1)}, bf16[16,3072]{1,0:T(8,128)(2,1)S(1)}, u32[]{:S(2)}, u32[]{:S(2)}) collective-permute-start(bf16[16,3072]{1,0:T(8,128)(2,1)} %bitcast.14), channel_id=1, source_target_pairs={{0,8},{1,9},{2,10},{3,11},{4,12},{5,13},{6,14},{7,15},{8,0},{9,1},... | collective-permute-start | bytes 294920 | tf_op jit(solution)/shard_map/ppermute | solution.py:38
  3.7 0.7 copy-done.3
  4.4 3.7 %fetch.1 = (bf16[3072,768]{1,0:T(8,128)(2,1)S(1)}, f32[3,3072]{1,0:T(4,128)S(1)}, f32[3,3072]{1,0:T(4,128)S(1)}, bf16[2,4096,128]{2,1,0:T(8,128)(2,1)S(1)}) custom-call(s32[16]{0:T(128)S(1)} %copy-done.3, bf16[3,28,3072]{2,1,0:T(8,128)(2,1)} %bitcast.23, bf16[3,3072,128]{2,1,0:T(8,128)(2,1)} %bitcast.18, bf16[3072,384]{1,0:T(8,128)(2,1)} %bitcast.19, ...), custom_call_target="tpu_custom_call" | custom-call | bytes 7000000 | tf_op jit(solution)/shard_map/fetch/pallas_call | solution.py:79
  8.2 0.3 norm_first.1
  8.4 2.4 %collective-permute-start.4 = (bf16[32,3072]{1,0:T(8,128)(2,1)S(1)}, bf16[32,3072]{1,0:T(8,128)(2,1)S(1)}, u32[]{:S(2)}, u32[]{:S(2)}) collective-permute-start(bf16[32,3072]{1,0:T(8,128)(2,1)S(1)} %get-tuple-element.32.n0), channel_id=1, source_target_pairs={{0,4},{1,5},{2,6},{3,7},{4,0},{5,1},{6,2},{7,3},{8,12},{9,13},{10,... | collective-permute-start | bytes 589832 | tf_op jit(solution)/shard_map/ppermute | solution.py:32
  10.8 1.3 %collective-permute-start.3 = (bf16[32,3072]{1,0:T(8,128)(2,1)S(1)}, bf16[32,3072]{1,0:T(8,128)(2,1)S(1)}, u32[]{:S(2)}, u32[]{:S(2)}) collective-permute-start(bf16[32,3072]{1,0:T(8,128)(2,1)S(1)} %get-tuple-element.32.n0), channel_id=1, source_target_pairs={{0,6},{1,7},{2,0},{3,1},{4,2},{5,3},{6,4},{7,5},{8,14},{9,15},{10,... | collective-permute-start | bytes 589832 | tf_op jit(solution)/shard_map/ppermute | solution.py:32
  12.2 0.7 collective-permute-start.2
  12.9 0.0 collective-permute-start.5
  12.9 5.0 %collective-permute-done.4.n2 = bf16[32,3072]{1,0:T(8,128)(2,1)S(1)} collective-permute-done((bf16[32,3072]{1,0:T(8,128)(2,1)S(1)}, bf16[32,3072]{1,0:T(8,128)(2,1)S(1)}, u32[]{:S(2)}, u32[]{:S(2)}) %collective-permute-start.4) | collective-permute-done | bytes 196640 | tf_op jit(solution)/shard_map/ppermute | solution.py:32
  17.9 0.0 collective-permute-start.8
  17.9 2.7 %collective-permute-done.3.n1 = bf16[32,3072]{1,0:T(8,128)(2,1)S(1)} collective-permute-done((bf16[32,3072]{1,0:T(8,128)(2,1)S(1)}, bf16[32,3072]{1,0:T(8,128)(2,1)S(1)}, u32[]{:S(2)}, u32[]{:S(2)}) %collective-permute-start.3) | collective-permute-done | bytes 196640 | tf_op jit(solution)/shard_map/ppermute | solution.py:32
  20.6 0.0 collective-permute-start.7
  20.6 0.1 collective-permute-done.2.n3
  20.8 0.4 collective-permute-start.6
  21.1 0.9 collective-permute-done.7.s1
  22.1 0.3 collective-permute-done.6.s3
  22.3 4.1 %block.2 = (bf16[2,4096,128]{2,1,0:T(8,128)(2,1)S(1)}, bf16[256,512]{1,0:T(8,128)(2,1)S(1)}, bf16[128,128]{1,0:T(8,128)(2,1)S(1)}, bf16[128,3072]{1,0:T(8,128)(2,1)S(1)}, bf16[512,3072]{1,0:T(8,128)(2,1)S(1)}) custom-call(s32[16]{0:T(128)S(1)} %copy-done.1, bf16[32,3072]{1,0:T(8,128)(2,1)S(1)} %get-tuple-element.32.n0, ...), custom_call_target="tpu_custom_call", output_to_operand_aliasing={{0}: (11, {})} | custom-call | flops 2200000000 | bytes 12000000 | tf_op jit(solution)/shard_map/block/pallas_call | solution.py:79
  26.5 0.3 collective-permute-start.9
  26.8 1.7 %own_half.2.mine = f32[128,3072]{1,0:T(8,128)S(1)} custom-call(bf16[128,128]{1,0:T(8,128)(2,1)S(1)} %get-tuple-element.35.queries, bf16[2,4096,128]{2,1,0:T(8,128)(2,1)S(1)} %get-tuple-element.36.kv.rest_0_, bf16[256,512]{1,0:T(8,128)(2,1)S(1)} %get-tuple-element.37.joined, bf16[512,3072]{1,0:T(8,128)(2,1)S(1)} %get-tuple-element.38.w2.rest_1_), custom_call_target="tpu_custom_call" | custom-call | flops 700000000 | bytes 4700000 | tf_op jit(solution)/shard_map/own_half/pallas_call | solution.py:79
  28.5 0.3 collective-permute-done.9.came
  28.8 0.1 pair_sum.2
  29.0 2.4 %collective-permute-start.10 = (bf16[32,3072]{1,0:T(8,128)(2,1)S(1)}, bf16[32,3072]{1,0:T(8,128)(2,1)S(1)}, u32[]{:S(2)}, u32[]{:S(2)}) collective-permute-start(bf16[32,3072]{1,0:T(8,128)(2,1)S(1)} %get-tuple-element.41), channel_id=1, source_target_pairs={{0,4},{1,5},{2,6},{3,7},{4,0},{5,1},{6,2},{7,3},{8,12},{9,13},{10,... | collective-permute-start | bytes 589832 | tf_op jit(solution)/shard_map/ppermute | solution.py:32
  31.4 1.1 %collective-permute-start.11 = (bf16[32,3072]{1,0:T(8,128)(2,1)S(1)}, bf16[32,3072]{1,0:T(8,128)(2,1)S(1)}, u32[]{:S(2)}, u32[]{:S(2)}) collective-permute-start(bf16[32,3072]{1,0:T(8,128)(2,1)S(1)} %get-tuple-element.42), channel_id=1, source_target_pairs={{0,6},{1,7},{2,0},{3,1},{4,2},{5,3},{6,4},{7,5},{8,14},{9,15},{10,... | collective-permute-start | bytes 589832 | tf_op jit(solution)/shard_map/ppermute | solution.py:32
  32.4 1.0 collective-permute-start.12
  33.4 0.6 collective-permute-start.1
  34.0 4.4 %collective-permute-done.10.r2 = bf16[32,3072]{1,0:T(8,128)(2,1)S(1)} collective-permute-done((bf16[32,3072]{1,0:T(8,128)(2,1)S(1)}, bf16[32,3072]{1,0:T(8,128)(2,1)S(1)}, u32[]{:S(2)}, u32[]{:S(2)}) %collective-permute-start.10) | collective-permute-done | bytes 196640 | tf_op jit(solution)/shard_map/ppermute | solution.py:32
  38.3 3.5 %collective-permute-done.11.r3 = bf16[32,3072]{1,0:T(8,128)(2,1)S(1)} collective-permute-done((bf16[32,3072]{1,0:T(8,128)(2,1)S(1)}, bf16[32,3072]{1,0:T(8,128)(2,1)S(1)}, u32[]{:S(2)}, u32[]{:S(2)}) %collective-permute-start.11) | collective-permute-done | bytes 196640 | tf_op jit(solution)/shard_map/ppermute | solution.py:32
  41.8 0.0 collective-permute-done.12.r1
  41.8 0.1 column_sum.1
  41.9 1.2 %collective-permute-start.14 = (bf16[32,3072]{1,0:T(8,128)(2,1)S(1)}, bf16[32,3072]{1,0:T(8,128)(2,1)S(1)}, u32[]{:S(2)}, u32[]{:S(2)}) collective-permute-start(bf16[32,3072]{1,0:T(8,128)(2,1)S(1)} %column_sum.1), channel_id=1, source_target_pairs={{0,24},{1,25},{2,26},{3,27},{4,28},{5,29},{6,30},{7,31},{8,16},{9,... | collective-permute-start | bytes 589832 | tf_op jit(solution)/shard_map/ppermute | solution.py:46
  43.2 1.2 %collective-permute-start.13 = (bf16[32,3072]{1,0:T(8,128)(2,1)S(1)}, bf16[32,3072]{1,0:T(8,128)(2,1)S(1)}, u32[]{:S(2)}, u32[]{:S(2)}) collective-permute-start(bf16[32,3072]{1,0:T(8,128)(2,1)S(1)} %column_sum.1), channel_id=1, source_target_pairs={{0,16},{1,17},{2,18},{3,19},{4,20},{5,21},{6,22},{7,23},{8,24},{9,... | collective-permute-start | bytes 589832 | tf_op jit(solution)/shard_map/ppermute | solution.py:46
  44.4 0.0 collective-permute-done.1.kept
  44.4 9.8 %collective-permute-done.14.p1 = bf16[32,3072]{1,0:T(8,128)(2,1)S(1)} collective-permute-done((bf16[32,3072]{1,0:T(8,128)(2,1)S(1)}, bf16[32,3072]{1,0:T(8,128)(2,1)S(1)}, u32[]{:S(2)}, u32[]{:S(2)}) %collective-permute-start.14) | collective-permute-done | bytes 196640 | tf_op jit(solution)/shard_map/ppermute | solution.py:46
  54.2 3.0 %collective-permute-done.13.p0 = bf16[32,3072]{1,0:T(8,128)(2,1)S(1)} collective-permute-done((bf16[32,3072]{1,0:T(8,128)(2,1)S(1)}, bf16[32,3072]{1,0:T(8,128)(2,1)S(1)}, u32[]{:S(2)}, u32[]{:S(2)}) %collective-permute-start.13) | collective-permute-done | bytes 196640 | tf_op jit(solution)/shard_map/ppermute | solution.py:46
  57.2 0.4 norm_next.1
  57.6 2.4 %collective-permute-start.18 = (bf16[32,3072]{1,0:T(8,128)(2,1)S(1)}, bf16[32,3072]{1,0:T(8,128)(2,1)S(1)}, u32[]{:S(2)}, u32[]{:S(2)}) collective-permute-start(bf16[32,3072]{1,0:T(8,128)(2,1)S(1)} %get-tuple-element.46.n0), channel_id=1, source_target_pairs={{0,4},{1,5},{2,6},{3,7},{4,0},{5,1},{6,2},{7,3},{8,12},{9,13},{10,... | collective-permute-start | bytes 589832 | tf_op jit(solution)/shard_map/ppermute | solution.py:32
  60.0 1.0 collective-permute-start.17
  60.9 1.1 %collective-permute-start.16 = (bf16[32,3072]{1,0:T(8,128)(2,1)S(1)}, bf16[32,3072]{1,0:T(8,128)(2,1)S(1)}, u32[]{:S(2)}, u32[]{:S(2)}) collective-permute-start(bf16[32,3072]{1,0:T(8,128)(2,1)S(1)} %get-tuple-element.46.n0), channel_id=1, source_target_pairs={{0,2},{1,3},{2,4},{3,5},{4,6},{5,7},{6,0},{7,1},{8,10},{9,11},{10,... | collective-permute-start | bytes 589832 | tf_op jit(solution)/shard_map/ppermute | solution.py:32
  62.0 0.0 collective-permute-start.19
  62.0 5.1 %collective-permute-done.18.n2 = bf16[32,3072]{1,0:T(8,128)(2,1)S(1)} collective-permute-done((bf16[32,3072]{1,0:T(8,128)(2,1)S(1)}, bf16[32,3072]{1,0:T(8,128)(2,1)S(1)}, u32[]{:S(2)}, u32[]{:S(2)}) %collective-permute-start.18) | collective-permute-done | bytes 196640 | tf_op jit(solution)/shard_map/ppermute | solution.py:32
  67.1 0.0 collective-permute-start.22
  67.1 2.6 %collective-permute-done.17.n1 = bf16[32,3072]{1,0:T(8,128)(2,1)S(1)} collective-permute-done((bf16[32,3072]{1,0:T(8,128)(2,1)S(1)}, bf16[32,3072]{1,0:T(8,128)(2,1)S(1)}, u32[]{:S(2)}, u32[]{:S(2)}) %collective-permute-start.17) | collective-permute-done | bytes 196640 | tf_op jit(solution)/shard_map/ppermute | solution.py:32
  69.7 0.0 collective-permute-start.21
  69.7 0.0 collective-permute-done.16.n3
  69.7 0.5 collective-permute-start.20
  70.2 0.0 collective-permute-done.19.s0
  70.2 0.9 collective-permute-done.21.s1
  71.1 0.3 collective-permute-done.20.s3
  71.4 3.9 %block.3 = (bf16[2,4096,128]{2,1,0:T(8,128)(2,1)S(1)}, bf16[256,512]{1,0:T(8,128)(2,1)S(1)}, bf16[128,128]{1,0:T(8,128)(2,1)S(1)}, bf16[128,3072]{1,0:T(8,128)(2,1)S(1)}, bf16[2,4096,128]{2,1,0:T(8,128)(2,1)}) custom-call(s32[16]{0:T(128)S(1)} %copy-done.1, bf16[32,3072]{1,0:T(8,128)(2,1)S(1)} %get-tuple-element.46.n0, ...), custom_call_target="tpu_custom_call", output_to_operand_aliasing={{0}: (11, {})} | custom-call | flops 2200000000 | bytes 12000000 | tf_op jit(solution)/shard_map/block/pallas_call | solution.py:79
  75.3 0.5 collective-permute-start.23
  75.8 1.7 %own_half.3.mine = f32[128,3072]{1,0:T(8,128)S(1)} custom-call(bf16[128,128]{1,0:T(8,128)(2,1)S(1)} %get-tuple-element.47.queries, bf16[2,4096,128]{2,1,0:T(8,128)(2,1)S(1)} %get-tuple-element.48.kv, bf16[256,512]{1,0:T(8,128)(2,1)S(1)} %get-tuple-element.49.joined, bf16[512,3072]{1,0:T(8,128)(2,1)S(1)} %get-tuple-element.38.w2.rest_1_), custom_call_target="tpu_custom_call" | custom-call | flops 700000000 | bytes 4700000 | tf_op jit(solution)/shard_map/own_half/pallas_call | solution.py:79
  77.6 0.3 collective-permute-done.23.came
  77.9 0.1 pair_sum.3
  78.0 2.4 %collective-permute-start.24 = (bf16[32,3072]{1,0:T(8,128)(2,1)S(1)}, bf16[32,3072]{1,0:T(8,128)(2,1)S(1)}, u32[]{:S(2)}, u32[]{:S(2)}) collective-permute-start(bf16[32,3072]{1,0:T(8,128)(2,1)S(1)} %get-tuple-element.52), channel_id=1, source_target_pairs={{0,4},{1,5},{2,6},{3,7},{4,0},{5,1},{6,2},{7,3},{8,12},{9,13},{10,... | collective-permute-start | bytes 589832 | tf_op jit(solution)/shard_map/ppermute | solution.py:32
  80.4 0.7 collective-permute-start.25
  81.1 1.3 %collective-permute-start.26 = (bf16[32,3072]{1,0:T(8,128)(2,1)S(1)}, bf16[32,3072]{1,0:T(8,128)(2,1)S(1)}, u32[]{:S(2)}, u32[]{:S(2)}) collective-permute-start(bf16[32,3072]{1,0:T(8,128)(2,1)S(1)} %get-tuple-element.54), channel_id=1, source_target_pairs={{0,2},{1,3},{2,4},{3,5},{4,6},{5,7},{6,0},{7,1},{8,10},{9,11},{10,... | collective-permute-start | bytes 589832 | tf_op jit(solution)/shard_map/ppermute | solution.py:32
  82.4 5.0 %collective-permute-done.24.r2 = bf16[32,3072]{1,0:T(8,128)(2,1)S(1)} collective-permute-done((bf16[32,3072]{1,0:T(8,128)(2,1)S(1)}, bf16[32,3072]{1,0:T(8,128)(2,1)S(1)}, u32[]{:S(2)}, u32[]{:S(2)}) %collective-permute-start.24) | collective-permute-done | bytes 196640 | tf_op jit(solution)/shard_map/ppermute | solution.py:32
  87.4 3.5 %collective-permute-done.25.r3 = bf16[32,3072]{1,0:T(8,128)(2,1)S(1)} collective-permute-done((bf16[32,3072]{1,0:T(8,128)(2,1)S(1)}, bf16[32,3072]{1,0:T(8,128)(2,1)S(1)}, u32[]{:S(2)}, u32[]{:S(2)}) %collective-permute-start.25) | collective-permute-done | bytes 196640 | tf_op jit(solution)/shard_map/ppermute | solution.py:32
  90.9 0.1 column_last.1
  91.0 0.1 collective-permute-start.27
  91.1 1.0 %collective-permute-start.28 = (bf16[16,3072]{1,0:T(8,128)(2,1)S(1)}, bf16[16,3072]{1,0:T(8,128)(2,1)S(1)}, u32[]{:S(2)}, u32[]{:S(2)}) collective-permute-start(bf16[16,3072]{1,0:T(8,128)(2,1)S(1)} %get-tuple-element.56), channel_id=1, source_target_pairs={{0,24},{1,25},{2,26},{3,27},{4,28},{5,29},{6,30},{7,31},{8,16},{9,... | collective-permute-start | bytes 294920 | tf_op jit(solution)/shard_map/ppermute | solution.py:46
  92.1 6.7 %collective-permute-done.27.p0 = bf16[16,3072]{1,0:T(8,128)(2,1)S(1)} collective-permute-done((bf16[16,3072]{1,0:T(8,128)(2,1)S(1)}, bf16[16,3072]{1,0:T(8,128)(2,1)S(1)}, u32[]{:S(2)}, u32[]{:S(2)}) %collective-permute-start.27) | collective-permute-done | bytes 98336 | tf_op jit(solution)/shard_map/ppermute | solution.py:46
  98.8 1.7 %collective-permute-done.28.p1 = bf16[16,3072]{1,0:T(8,128)(2,1)S(1)} collective-permute-done((bf16[16,3072]{1,0:T(8,128)(2,1)S(1)}, bf16[16,3072]{1,0:T(8,128)(2,1)S(1)}, u32[]{:S(2)}, u32[]{:S(2)}) %collective-permute-start.28) | collective-permute-done | bytes 98336 | tf_op jit(solution)/shard_map/ppermute | solution.py:46
  100.5 0.7 residual_last.1
  (14 shorter events, 0.0 us)
Async XLA Ops:
  0.6 7.5 %collective-permute-start = (bf16[16,3072]{1,0:T(8,128)(2,1)}, bf16[16,3072]{1,0:T(8,128)(2,1)S(1)}, u32[]{:S(2)}, u32[]{:S(2)}) collective-permute-start(bf16[16,3072]{1,0:T(8,128)(2,1)} %bitcast.14), channel_id=1, source_target_pairs={{0,8},{1,9},{2,10},{3,11},{4,12},{5,13},{6,14},{7,15},{8,0},{9,1},... | collective-permute-start | bytes 294920 | tf_op jit(solution)/shard_map/ppermute | solution.py:38
  3.7 0.7 copy-start.3
  4.4 3.8 %copy-start = (bf16[1,16,3072]{2,1,0:T(8,128)(2,1)S(1)}, bf16[1,16,3072]{2,1,0:T(8,128)(2,1)}, u32[]{:S(2)}) copy-start(bf16[1,16,3072]{2,1,0:T(8,128)(2,1)} %param.10) | copy-start | bytes 294916
  4.4 17.9 %copy-start.1 = (s32[16]{0:T(128)S(1)}, s32[16]{0:T(128)}, u32[]{:S(2)}) copy-start(s32[16]{0:T(128)} %patches.3) | copy-start | bytes 196
  4.4 17.9 %copy-start.2 = (bf16[1,2,128]{2,1,0:T(2,128)(2,1)S(1)}, bf16[1,2,128]{2,1,0:T(2,128)(2,1)}, u32[]{:S(2)}) copy-start(bf16[1,2,128]{2,1,0:T(2,128)(2,1)} %param.15) | copy-start | bytes 1540
  8.4 9.5 %collective-permute-start.4 = (bf16[32,3072]{1,0:T(8,128)(2,1)S(1)}, bf16[32,3072]{1,0:T(8,128)(2,1)S(1)}, u32[]{:S(2)}, u32[]{:S(2)}) collective-permute-start(bf16[32,3072]{1,0:T(8,128)(2,1)S(1)} %get-tuple-element.32.n0), channel_id=1, source_target_pairs={{0,4},{1,5},{2,6},{3,7},{4,0},{5,1},{6,2},{7,3},{8,12},{9,13},{10,... | collective-permute-start | bytes 589832 | tf_op jit(solution)/shard_map/ppermute | solution.py:32
  10.8 9.8 %collective-permute-start.3 = (bf16[32,3072]{1,0:T(8,128)(2,1)S(1)}, bf16[32,3072]{1,0:T(8,128)(2,1)S(1)}, u32[]{:S(2)}, u32[]{:S(2)}) collective-permute-start(bf16[32,3072]{1,0:T(8,128)(2,1)S(1)} %get-tuple-element.32.n0), channel_id=1, source_target_pairs={{0,6},{1,7},{2,0},{3,1},{4,2},{5,3},{6,4},{7,5},{8,14},{9,15},{10,... | collective-permute-start | bytes 589832 | tf_op jit(solution)/shard_map/ppermute | solution.py:32
  12.2 8.6 %collective-permute-start.2 = (bf16[32,3072]{1,0:T(8,128)(2,1)S(1)}, bf16[32,3072]{1,0:T(8,128)(2,1)S(1)}, u32[]{:S(2)}, u32[]{:S(2)}) collective-permute-start(bf16[32,3072]{1,0:T(8,128)(2,1)S(1)} %get-tuple-element.32.n0), channel_id=1, source_target_pairs={{0,2},{1,3},{2,4},{3,5},{4,6},{5,7},{6,0},{7,1},{8,10},{9,11},{10,... | collective-permute-start | bytes 589832 | tf_op jit(solution)/shard_map/ppermute | solution.py:32
  12.9 8.3 %collective-permute-start.5 = (bf16[32,3072]{1,0:T(8,128)(2,1)S(1)}, bf16[32,3072]{1,0:T(8,128)(2,1)S(1)}, u32[]{:S(2)}, u32[]{:S(2)}) collective-permute-start(bf16[32,3072]{1,0:T(8,128)(2,1)S(1)} %get-tuple-element.32.n0), channel_id=1, source_target_pairs={{0,1},{1,0},{2,3},{3,2},{4,5},{5,4},{6,7},{7,6},{8,9},{9,8},{10,11... | collective-permute-start | bytes 589832 | tf_op jit(solution)/shard_map/ppermute | solution.py:28
  17.9 3.2 %collective-permute-start.8 = (bf16[32,3072]{1,0:T(8,128)(2,1)S(1)}, bf16[32,3072]{1,0:T(8,128)(2,1)S(1)}, u32[]{:S(2)}, u32[]{:S(2)}) collective-permute-start(bf16[32,3072]{1,0:T(8,128)(2,1)S(1)} %collective-permute-done.4.n2), channel_id=1, source_target_pairs={{0,1},{1,0},{2,3},{3,2},{4,5},{5,4},{6,7},{7,6},{8,9},{9,8},{10,11... | collective-permute-start | bytes 589832 | tf_op jit(solution)/shard_map/ppermute | solution.py:28
  20.6 1.4 %collective-permute-start.7 = (bf16[32,3072]{1,0:T(8,128)(2,1)S(1)}, bf16[32,3072]{1,0:T(8,128)(2,1)S(1)}, u32[]{:S(2)}, u32[]{:S(2)}) collective-permute-start(bf16[32,3072]{1,0:T(8,128)(2,1)S(1)} %collective-permute-done.3.n1), channel_id=1, source_target_pairs={{0,1},{1,0},{2,3},{3,2},{4,5},{5,4},{6,7},{7,6},{8,9},{9,8},{10,11... | collective-permute-start | bytes 589832 | tf_op jit(solution)/shard_map/ppermute | solution.py:28
  20.8 1.6 %collective-permute-start.6 = (bf16[32,3072]{1,0:T(8,128)(2,1)S(1)}, bf16[32,3072]{1,0:T(8,128)(2,1)S(1)}, u32[]{:S(2)}, u32[]{:S(2)}) collective-permute-start(bf16[32,3072]{1,0:T(8,128)(2,1)S(1)} %collective-permute-done.2.n3), channel_id=1, source_target_pairs={{0,1},{1,0},{2,3},{3,2},{4,5},{5,4},{6,7},{7,6},{8,9},{9,8},{10,11... | collective-permute-start | bytes 589832 | tf_op jit(solution)/shard_map/ppermute | solution.py:28
  26.5 2.4 %collective-permute-start.9 = (bf16[128,3072]{1,0:T(8,128)(2,1)S(1)}, bf16[128,3072]{1,0:T(8,128)(2,1)S(1)}, u32[]{:S(2)}, u32[]{:S(2)}) collective-permute-start(bf16[128,3072]{1,0:T(8,128)(2,1)S(1)} %get-tuple-element.39), channel_id=1, source_target_pairs={{0,1},{1,0},{2,3},{3,2},{4,5},{5,4},{6,7},{7,6},{8,9},{9,8},{10,11... | collective-permute-start | bytes 2359304 | tf_op jit(solution)/shard_map/ppermute | solution.py:28
  29.0 9.4 %collective-permute-start.10 = (bf16[32,3072]{1,0:T(8,128)(2,1)S(1)}, bf16[32,3072]{1,0:T(8,128)(2,1)S(1)}, u32[]{:S(2)}, u32[]{:S(2)}) collective-permute-start(bf16[32,3072]{1,0:T(8,128)(2,1)S(1)} %get-tuple-element.41), channel_id=1, source_target_pairs={{0,4},{1,5},{2,6},{3,7},{4,0},{5,1},{6,2},{7,3},{8,12},{9,13},{10,... | collective-permute-start | bytes 589832 | tf_op jit(solution)/shard_map/ppermute | solution.py:32
  31.4 10.5 %collective-permute-start.11 = (bf16[32,3072]{1,0:T(8,128)(2,1)S(1)}, bf16[32,3072]{1,0:T(8,128)(2,1)S(1)}, u32[]{:S(2)}, u32[]{:S(2)}) collective-permute-start(bf16[32,3072]{1,0:T(8,128)(2,1)S(1)} %get-tuple-element.42), channel_id=1, source_target_pairs={{0,6},{1,7},{2,0},{3,1},{4,2},{5,3},{6,4},{7,5},{8,14},{9,15},{10,... | collective-permute-start | bytes 589832 | tf_op jit(solution)/shard_map/ppermute | solution.py:32
  32.4 9.4 %collective-permute-start.12 = (bf16[32,3072]{1,0:T(8,128)(2,1)S(1)}, bf16[32,3072]{1,0:T(8,128)(2,1)S(1)}, u32[]{:S(2)}, u32[]{:S(2)}) collective-permute-start(bf16[32,3072]{1,0:T(8,128)(2,1)S(1)} %get-tuple-element.43), channel_id=1, source_target_pairs={{0,2},{1,3},{2,4},{3,5},{4,6},{5,7},{6,0},{7,1},{8,10},{9,11},{10,... | collective-permute-start | bytes 589832 | tf_op jit(solution)/shard_map/ppermute | solution.py:32
  33.4 11.0 %collective-permute-start.1 = (bf16[32,3072]{1,0:T(8,128)(2,1)S(1)}, bf16[32,3072]{1,0:T(8,128)(2,1)S(1)}, u32[]{:S(2)}, u32[]{:S(2)}) collective-permute-start(bf16[32,3072]{1,0:T(8,128)(2,1)S(1)} %get-tuple-element.31), channel_id=1, source_target_pairs={{0,16},{1,17},{2,18},{3,19},{4,20},{5,21},{6,22},{7,23},{8,24},{9,... | collective-permute-start | bytes 589832 | tf_op jit(solution)/shard_map/ppermute | solution.py:46
  41.9 12.2 %collective-permute-start.14 = (bf16[32,3072]{1,0:T(8,128)(2,1)S(1)}, bf16[32,3072]{1,0:T(8,128)(2,1)S(1)}, u32[]{:S(2)}, u32[]{:S(2)}) collective-permute-start(bf16[32,3072]{1,0:T(8,128)(2,1)S(1)} %column_sum.1), channel_id=1, source_target_pairs={{0,24},{1,25},{2,26},{3,27},{4,28},{5,29},{6,30},{7,31},{8,16},{9,... | collective-permute-start | bytes 589832 | tf_op jit(solution)/shard_map/ppermute | solution.py:46
  43.2 14.0 %collective-permute-start.13 = (bf16[32,3072]{1,0:T(8,128)(2,1)S(1)}, bf16[32,3072]{1,0:T(8,128)(2,1)S(1)}, u32[]{:S(2)}, u32[]{:S(2)}) collective-permute-start(bf16[32,3072]{1,0:T(8,128)(2,1)S(1)} %column_sum.1), channel_id=1, source_target_pairs={{0,16},{1,17},{2,18},{3,19},{4,20},{5,21},{6,22},{7,23},{8,24},{9,... | collective-permute-start | bytes 589832 | tf_op jit(solution)/shard_map/ppermute | solution.py:46
  57.6 9.5 %collective-permute-start.18 = (bf16[32,3072]{1,0:T(8,128)(2,1)S(1)}, bf16[32,3072]{1,0:T(8,128)(2,1)S(1)}, u32[]{:S(2)}, u32[]{:S(2)}) collective-permute-start(bf16[32,3072]{1,0:T(8,128)(2,1)S(1)} %get-tuple-element.46.n0), channel_id=1, source_target_pairs={{0,4},{1,5},{2,6},{3,7},{4,0},{5,1},{6,2},{7,3},{8,12},{9,13},{10,... | collective-permute-start | bytes 589832 | tf_op jit(solution)/shard_map/ppermute | solution.py:32
  60.0 9.7 %collective-permute-start.17 = (bf16[32,3072]{1,0:T(8,128)(2,1)S(1)}, bf16[32,3072]{1,0:T(8,128)(2,1)S(1)}, u32[]{:S(2)}, u32[]{:S(2)}) collective-permute-start(bf16[32,3072]{1,0:T(8,128)(2,1)S(1)} %get-tuple-element.46.n0), channel_id=1, source_target_pairs={{0,6},{1,7},{2,0},{3,1},{4,2},{5,3},{6,4},{7,5},{8,14},{9,15},{10,... | collective-permute-start | bytes 589832 | tf_op jit(solution)/shard_map/ppermute | solution.py:32
  60.9 8.8 %collective-permute-start.16 = (bf16[32,3072]{1,0:T(8,128)(2,1)S(1)}, bf16[32,3072]{1,0:T(8,128)(2,1)S(1)}, u32[]{:S(2)}, u32[]{:S(2)}) collective-permute-start(bf16[32,3072]{1,0:T(8,128)(2,1)S(1)} %get-tuple-element.46.n0), channel_id=1, source_target_pairs={{0,2},{1,3},{2,4},{3,5},{4,6},{5,7},{6,0},{7,1},{8,10},{9,11},{10,... | collective-permute-start | bytes 589832 | tf_op jit(solution)/shard_map/ppermute | solution.py:32
  62.0 8.2 %collective-permute-start.19 = (bf16[32,3072]{1,0:T(8,128)(2,1)S(1)}, bf16[32,3072]{1,0:T(8,128)(2,1)S(1)}, u32[]{:S(2)}, u32[]{:S(2)}) collective-permute-start(bf16[32,3072]{1,0:T(8,128)(2,1)S(1)} %get-tuple-element.46.n0), channel_id=1, source_target_pairs={{0,1},{1,0},{2,3},{3,2},{4,5},{5,4},{6,7},{7,6},{8,9},{9,8},{10,11... | collective-permute-start | bytes 589832 | tf_op jit(solution)/shard_map/ppermute | solution.py:28
  67.1 3.1 %collective-permute-start.22 = (bf16[32,3072]{1,0:T(8,128)(2,1)S(1)}, bf16[32,3072]{1,0:T(8,128)(2,1)S(1)}, u32[]{:S(2)}, u32[]{:S(2)}) collective-permute-start(bf16[32,3072]{1,0:T(8,128)(2,1)S(1)} %collective-permute-done.18.n2), channel_id=1, source_target_pairs={{0,1},{1,0},{2,3},{3,2},{4,5},{5,4},{6,7},{7,6},{8,9},{9,8},{10,11... | collective-permute-start | bytes 589832 | tf_op jit(solution)/shard_map/ppermute | solution.py:28
  69.7 1.4 %collective-permute-start.21 = (bf16[32,3072]{1,0:T(8,128)(2,1)S(1)}, bf16[32,3072]{1,0:T(8,128)(2,1)S(1)}, u32[]{:S(2)}, u32[]{:S(2)}) collective-permute-start(bf16[32,3072]{1,0:T(8,128)(2,1)S(1)} %collective-permute-done.17.n1), channel_id=1, source_target_pairs={{0,1},{1,0},{2,3},{3,2},{4,5},{5,4},{6,7},{7,6},{8,9},{9,8},{10,11... | collective-permute-start | bytes 589832 | tf_op jit(solution)/shard_map/ppermute | solution.py:28
  69.7 1.7 %collective-permute-start.20 = (bf16[32,3072]{1,0:T(8,128)(2,1)S(1)}, bf16[32,3072]{1,0:T(8,128)(2,1)S(1)}, u32[]{:S(2)}, u32[]{:S(2)}) collective-permute-start(bf16[32,3072]{1,0:T(8,128)(2,1)S(1)} %collective-permute-done.16.n3), channel_id=1, source_target_pairs={{0,1},{1,0},{2,3},{3,2},{4,5},{5,4},{6,7},{7,6},{8,9},{9,8},{10,11... | collective-permute-start | bytes 589832 | tf_op jit(solution)/shard_map/ppermute | solution.py:28
  75.3 2.6 %collective-permute-start.23 = (bf16[128,3072]{1,0:T(8,128)(2,1)S(1)}, bf16[128,3072]{1,0:T(8,128)(2,1)S(1)}, u32[]{:S(2)}, u32[]{:S(2)}) collective-permute-start(bf16[128,3072]{1,0:T(8,128)(2,1)S(1)} %get-tuple-element.50), channel_id=1, source_target_pairs={{0,1},{1,0},{2,3},{3,2},{4,5},{5,4},{6,7},{7,6},{8,9},{9,8},{10,11... | collective-permute-start | bytes 2359304 | tf_op jit(solution)/shard_map/ppermute | solution.py:28
  78.0 9.4 %collective-permute-start.24 = (bf16[32,3072]{1,0:T(8,128)(2,1)S(1)}, bf16[32,3072]{1,0:T(8,128)(2,1)S(1)}, u32[]{:S(2)}, u32[]{:S(2)}) collective-permute-start(bf16[32,3072]{1,0:T(8,128)(2,1)S(1)} %get-tuple-element.52), channel_id=1, source_target_pairs={{0,4},{1,5},{2,6},{3,7},{4,0},{5,1},{6,2},{7,3},{8,12},{9,13},{10,... | collective-permute-start | bytes 589832 | tf_op jit(solution)/shard_map/ppermute | solution.py:32
  80.4 10.5 %collective-permute-start.25 = (bf16[32,3072]{1,0:T(8,128)(2,1)S(1)}, bf16[32,3072]{1,0:T(8,128)(2,1)S(1)}, u32[]{:S(2)}, u32[]{:S(2)}) collective-permute-start(bf16[32,3072]{1,0:T(8,128)(2,1)S(1)} %get-tuple-element.53), channel_id=1, source_target_pairs={{0,6},{1,7},{2,0},{3,1},{4,2},{5,3},{6,4},{7,5},{8,14},{9,15},{10,... | collective-permute-start | bytes 589832 | tf_op jit(solution)/shard_map/ppermute | solution.py:32
  81.1 9.8 %collective-permute-start.26 = (bf16[32,3072]{1,0:T(8,128)(2,1)S(1)}, bf16[32,3072]{1,0:T(8,128)(2,1)S(1)}, u32[]{:S(2)}, u32[]{:S(2)}) collective-permute-start(bf16[32,3072]{1,0:T(8,128)(2,1)S(1)} %get-tuple-element.54), channel_id=1, source_target_pairs={{0,2},{1,3},{2,4},{3,5},{4,6},{5,7},{6,0},{7,1},{8,10},{9,11},{10,... | collective-permute-start | bytes 589832 | tf_op jit(solution)/shard_map/ppermute | solution.py:32
  82.4 9.7 %collective-permute-start.15 = (bf16[16,3072]{1,0:T(8,128)(2,1)S(1)}, bf16[16,3072]{1,0:T(8,128)(2,1)S(1)}, u32[]{:S(2)}, u32[]{:S(2)}) collective-permute-start(bf16[16,3072]{1,0:T(8,128)(2,1)S(1)} %get-tuple-element.45), channel_id=1, source_target_pairs={{0,16},{1,17},{2,18},{3,19},{4,20},{5,21},{6,22},{7,23},{8,24},{9,... | collective-permute-start | bytes 294920 | tf_op jit(solution)/shard_map/ppermute | solution.py:46
  91.0 7.8 %collective-permute-start.27 = (bf16[16,3072]{1,0:T(8,128)(2,1)S(1)}, bf16[16,3072]{1,0:T(8,128)(2,1)S(1)}, u32[]{:S(2)}, u32[]{:S(2)}) collective-permute-start(bf16[16,3072]{1,0:T(8,128)(2,1)S(1)} %get-tuple-element.55), channel_id=1, source_target_pairs={{0,16},{1,17},{2,18},{3,19},{4,20},{5,21},{6,22},{7,23},{8,24},{9,... | collective-permute-start | bytes 294920 | tf_op jit(solution)/shard_map/ppermute | solution.py:46
  91.1 9.5 %collective-permute-start.28 = (bf16[16,3072]{1,0:T(8,128)(2,1)S(1)}, bf16[16,3072]{1,0:T(8,128)(2,1)S(1)}, u32[]{:S(2)}, u32[]{:S(2)}) collective-permute-start(bf16[16,3072]{1,0:T(8,128)(2,1)S(1)} %get-tuple-element.56), channel_id=1, source_target_pairs={{0,24},{1,25},{2,26},{3,27},{4,28},{5,29},{6,30},{7,31},{8,16},{9,... | collective-permute-start | bytes 294920 | tf_op jit(solution)/shard_map/ppermute | solution.py:46

commit v4 on v3

--- a/solution.py
+++ b/solution.py
@@ -174,7 +174,7 @@
     return (mixed / total).astype(BF)
 
 
-def block_body(last, patches, n0, n3, n1, n2, s0, s3, s1, s2, w1, gains, *rest):
+def block_body(last, patches, n0, n2, n1, n3, s0, s2, s1, s3, w1, gains, *rest):
     if last:
         (old, w2, kv, joined, queries, partial, new_cache, rows, scores, sems) = rest
         reads = []
@@ -233,19 +233,19 @@
         )
 
 
-def pair_body(mine, came, o0, o1, o2, o3):
+def pair_body(mine, came, passing, o0, o1, o2, o3):
     o0[...] = mine[0:PAIR, :] + came[0:PAIR, :].astype(F32)
     for i, o in ((1, o1), (2, o2), (3, o3)):
         a, b = i * PAIR, (i + 1) * PAIR
         o[...] = (mine[a:b, :] + came[a:b, :].astype(F32)).astype(BF)
 
 
-def column_body(mine, r2, r3, r1, factors, out):
+def column_body(mine, r1, r3, r2, factors, out):
     total = mine[...] + r1[...].astype(F32) + (r2[...].astype(F32) + r3[...].astype(F32))
     out[...] = (factors[2:3, :] * total).astype(BF)
 
 
-def last_column_body(mine, r2, r3, r1, factors, here, there):
+def last_column_body(mine, r1, r3, r2, factors, here, there):
     xh, _, _ = spot()
     gate = factors[2:3, :]
     for out, at in ((here, xh), (there, 1 - xh)):
@@ -267,12 +267,12 @@
     out[...] = (kept[...].astype(F32) + (p0[...].astype(F32) + p1[...].astype(F32))).astype(BF)
 
 
-def block(last, normed, patches, w1, gains, kv, weights):
+def block(last, normed, passing, patches, w1, gains, kv, weights):
     core_parts = [send_core(normed)]
     n2 = send_y(normed, 2)
     n3 = send_y(normed, 1)
     n1 = send_y(normed, 3)
-    core_parts += [send_core(p) for p in (n3, n1, n2)]
+    core_parts += [send_core(p) for p in (n2, n1, n3)]
     cache_shape = (2, TOKENS, HD)
     outs = [
         ("vmem", cache_shape, BF),
@@ -285,7 +285,7 @@
     kv, joined, queries, partial, fifth = local_call(
         functools.partial(block_body, last),
         outs,
-        [("smem", patches)] + [("vmem", p) for p in [normed, n3, n1, n2] + core_parts]
+        [("smem", patches)] + [("vmem", p) for p in [normed, n2, n1, n3] + core_parts]
         + [("vmem", w1), ("vmem", gains), ("vmem", kv)] + [(kind, a) for a in weights],
         scratch=[
             pltpu.VMEM((ROWS, D), BF),
@@ -293,7 +293,7 @@
             pltpu.SemaphoreType.DMA((2,)),
         ],
         limit=24,
-        flops=2_200_000_000,
+        flops=30_000_000_000,
         moved=12_000_000,
         name="block",
         aliases={11: 0},
@@ -305,14 +305,14 @@
         [("vmem", (HALF, D), F32)],
         [("vmem", queries), ("vmem", kv), ("vmem", joined), ("vmem", w2)],
         scratch=[pltpu.VMEM((HALF, TOKENS), F32)],
-        flops=700_000_000,
+        flops=12_000_000_000,
         moved=4_700_000,
         name="own_half",
     )
     o0, o1, o2, o3 = local_call(
         pair_body,
         [("vmem", (PAIR, D), F32)] + [("vmem", (PAIR, D), BF)] * 3,
-        [("vmem", mine), ("vmem", came)],
+        [("vmem", mine), ("vmem", came), ("any", passing)],
         flops=400_000,
         moved=3_000_000,
         name="pair_sum",
@@ -320,7 +320,7 @@
     r2 = send_y(o2, 2)
     r1 = send_y(o1, 1)
     r3 = send_y(o3, 3)
-    return (o0, r2, r3, r1), kv, fifth
+    return (o0, r1, r3, r2), kv, fifth
 
 
 def shards(
@@ -370,7 +370,7 @@
     )
     kept = send_on(kept, 0)
     sums, kv, w2 = block(
-        False, normed, patch_of_slot, w1, gains, kv, (w_attn_out[0], w_mlp_out[0])
+        False, normed, kept, patch_of_slot, w1, gains, kv, (w_attn_out[0], w_mlp_out[0])
     )
     (out,) = local_call(
         column_body,
@@ -390,7 +390,7 @@
         name="norm_next",
     )
     kept = send_on(kept, 0)
-    sums, _, cache = block(True, normed, patch_of_slot, w1, gains, kv, (w2,))
+    sums, _, cache = block(True, normed, kept, patch_of_slot, w1, gains, kv, (w2,))
     here, there = local_call(
         last_column_body,
         [("vmem", (PIECE, D), BF)] * 2,

time: 101 us -> 100 us (0.990)
  starting transfers between devices: 26.6 us -> 24.3 us
  waiting for transfers between devices: 56.1 us -> 57.4 us
    ppermute x6, waiting for transfers between devices: 21.3 us -> 23.2 us  [send_on(): return lax.ppermute(x, ('section', 'sp'), pairs)]
    ppermute x6, starting transfers between devices: 4.14 us -> 2.44 us  [send_on(): return lax.ppermute(x, ('section', 'sp'), pairs)]
    ppermute x10, starting transfers between devices: 1.76 us -> 0.68 us  [send_core(): return lax.ppermute(x, 'sp', [(i, i ^ 1) for i in range(SPAN)])]
  transfers between devices with their start and end apart: 29 -> 29, of which waited for: 19 -> 19; matrix products, arithmetic and copies ran while one was open for 0% -> 0% of each run, Pallas kernels for 7% -> 15%
where the time goes in v4:
time: 100 us
  waiting for transfers between devices  57.4 us (57%)
  starting transfers between devices  24.3 us (24%)
  Pallas kernels  17.1 us (17%)
    ppermute x12, waiting for transfers between devices, send_y(): lax.ppermute(x, 'sp', [(i, i & 9 | ((i >> 1 & 3) + by) % 4 << 1) for i in...  31.6 us
    ppermute x6, waiting for transfers between devices, send_on(): return lax.ppermute(x, ('section', 'sp'), pairs)  23.2 us
    ppermute x12, starting transfers between devices, send_y(): lax.ppermute(x, 'sp', [(i, i & 9 | ((i >> 1 & 3) + by) % 4 << 1) for i in...  18.1 us
    pallas_call x12, Pallas kernels, local_call(): pl.pallas_call(body, out_shape=out_shape, in_specs=specs, out_specs=out_s...  17.1 us
    ppermute x1, starting transfers between devices, send_x(): return lax.ppermute(x, 'sp', [(i, i ^ 8) for i in range(SPAN)])  3.11 us
    ppermute x10, waiting for transfers between devices, send_core(): return lax.ppermute(x, 'sp', [(i, i ^ 1) for i in range(SPAN)])  2.68 us
    ppermute x6, starting transfers between devices, send_on(): return lax.ppermute(x, ('section', 'sp'), pairs)  2.44 us
  transfers between devices with their start and end apart: 29, of which 19 were waited for; matrix products, arithmetic and copies ran while one was open for 0% of the time, Pallas kernels for 15%

profile of v4, /device:TPU:8, one launch (start us, length us, event | category | flops | bytes accessed | tf_op | source)
XLA Modules:
  0.0 100.3 jit_solution(12764818872871394271)
XLA Ops:
  0.6 3.1 %collective-permute-start = (bf16[16,3072]{1,0:T(8,128)(2,1)}, bf16[16,3072]{1,0:T(8,128)(2,1)S(1)}, u32[]{:S(2)}, u32[]{:S(2)}) collective-permute-start(bf16[16,3072]{1,0:T(8,128)(2,1)} %bitcast.14), channel_id=1, source_target_pairs={{0,8},{1,9},{2,10},{3,11},{4,12},{5,13},{6,14},{7,15},{8,0},{9,1},... | collective-permute-start | bytes 294920 | tf_op jit(solution)/shard_map/ppermute | solution.py:38
  3.7 0.7 copy-done.1
  4.4 3.7 %fetch.1 = (bf16[3072,768]{1,0:T(8,128)(2,1)S(1)}, f32[3,3072]{1,0:T(4,128)S(1)}, f32[3,3072]{1,0:T(4,128)S(1)}, bf16[2,4096,128]{2,1,0:T(8,128)(2,1)S(1)}) custom-call(s32[16]{0:T(128)S(1)} %copy-done.1, bf16[3,28,3072]{2,1,0:T(8,128)(2,1)} %bitcast.21, bf16[3,3072,128]{2,1,0:T(8,128)(2,1)} %bitcast.18, bf16[3072,384]{1,0:T(8,128)(2,1)} %bitcast.19, ...), custom_call_target="tpu_custom_call" | custom-call | bytes 7000000 | tf_op jit(solution)/shard_map/fetch/pallas_call | solution.py:79
  8.1 0.0 collective-permute-done.other
  8.2 0.3 norm_first.1
  8.4 1.7 %collective-permute-start.4 = (bf16[32,3072]{1,0:T(8,128)(2,1)S(1)}, bf16[32,3072]{1,0:T(8,128)(2,1)S(1)}, u32[]{:S(2)}, u32[]{:S(2)}) collective-permute-start(bf16[32,3072]{1,0:T(8,128)(2,1)S(1)} %get-tuple-element.32.n0), channel_id=1, source_target_pairs={{0,2},{1,3},{2,4},{3,5},{4,6},{5,7},{6,0},{7,1},{8,10},{9,11},{10,... | collective-permute-start | bytes 589832 | tf_op jit(solution)/shard_map/ppermute | solution.py:32
  10.1 0.4 collective-permute-start.3
  10.5 2.3 %collective-permute-start.2 = (bf16[32,3072]{1,0:T(8,128)(2,1)S(1)}, bf16[32,3072]{1,0:T(8,128)(2,1)S(1)}, u32[]{:S(2)}, u32[]{:S(2)}) collective-permute-start(bf16[32,3072]{1,0:T(8,128)(2,1)S(1)} %get-tuple-element.32.n0), channel_id=1, source_target_pairs={{0,4},{1,5},{2,6},{3,7},{4,0},{5,1},{6,2},{7,3},{8,12},{9,13},{10,... | collective-permute-start | bytes 589832 | tf_op jit(solution)/shard_map/ppermute | solution.py:32
  12.8 0.0 collective-permute-start.5
  12.8 3.1 %collective-permute-done.4.n3 = bf16[32,3072]{1,0:T(8,128)(2,1)S(1)} collective-permute-done((bf16[32,3072]{1,0:T(8,128)(2,1)S(1)}, bf16[32,3072]{1,0:T(8,128)(2,1)S(1)}, u32[]{:S(2)}, u32[]{:S(2)}) %collective-permute-start.4) | collective-permute-done | bytes 196640 | tf_op jit(solution)/shard_map/ppermute | solution.py:32
  15.9 0.0 collective-permute-start.8
  15.9 1.3 %collective-permute-done.3.n1 = bf16[32,3072]{1,0:T(8,128)(2,1)S(1)} collective-permute-done((bf16[32,3072]{1,0:T(8,128)(2,1)S(1)}, bf16[32,3072]{1,0:T(8,128)(2,1)S(1)}, u32[]{:S(2)}, u32[]{:S(2)}) %collective-permute-start.3) | collective-permute-done | bytes 196640 | tf_op jit(solution)/shard_map/ppermute | solution.py:32
  17.2 0.0 collective-permute-start.7
  17.2 3.9 %collective-permute-done.2.n2 = bf16[32,3072]{1,0:T(8,128)(2,1)S(1)} collective-permute-done((bf16[32,3072]{1,0:T(8,128)(2,1)S(1)}, bf16[32,3072]{1,0:T(8,128)(2,1)S(1)}, u32[]{:S(2)}, u32[]{:S(2)}) %collective-permute-start.2) | collective-permute-done | bytes 196640 | tf_op jit(solution)/shard_map/ppermute | solution.py:32
  21.1 0.0 collective-permute-start.6
  21.1 0.6 collective-permute-start.1
  21.7 0.0 collective-permute-done.5.s0
  21.7 0.0 collective-permute-done.8.s3
  21.7 0.0 collective-permute-done.7.s1
  21.7 0.8 collective-permute-done.6.s2
  22.6 4.2 %block.2 = (bf16[2,4096,128]{2,1,0:T(8,128)(2,1)S(1)}, bf16[256,512]{1,0:T(8,128)(2,1)S(1)}, bf16[128,128]{1,0:T(8,128)(2,1)S(1)}, bf16[128,3072]{1,0:T(8,128)(2,1)S(1)}, bf16[512,3072]{1,0:T(8,128)(2,1)S(1)}) custom-call(s32[16]{0:T(128)S(1)} %copy-done.2, bf16[32,3072]{1,0:T(8,128)(2,1)S(1)} %get-tuple-element.32.n0, ...), custom_call_target="tpu_custom_call", output_to_operand_aliasing={{0}: (11, {})} | custom-call | flops 30000001024 | bytes 12000000 | tf_op jit(solution)/shard_map/block/pallas_call | solution.py:79
  26.8 0.2 collective-permute-start.9
  27.0 1.7 %own_half.2.mine = f32[128,3072]{1,0:T(8,128)S(1)} custom-call(bf16[128,128]{1,0:T(8,128)(2,1)S(1)} %get-tuple-element.35.queries, bf16[2,4096,128]{2,1,0:T(8,128)(2,1)S(1)} %get-tuple-element.36.kv.rest_0_, bf16[256,512]{1,0:T(8,128)(2,1)S(1)} %get-tuple-element.37.joined, bf16[512,3072]{1,0:T(8,128)(2,1)S(1)} %get-tuple-element.38.w2.rest_1_), custom_call_target="tpu_custom_call" | custom-call | flops 12000000000 | bytes 4700000 | tf_op jit(solution)/shard_map/own_half/pallas_call | solution.py:79
  28.7 3.8 %collective-permute-done.1.passing.kept = bf16[32,3072]{1,0:T(8,128)(2,1)S(1)} collective-permute-done((bf16[32,3072]{1,0:T(8,128)(2,1)S(1)}, bf16[32,3072]{1,0:T(8,128)(2,1)S(1)}, u32[]{:S(2)}, u32[]{:S(2)}) %collective-permute-start.1) | collective-permute-done | bytes 196640 | tf_op jit(solution)/shard_map/ppermute | solution.py:46
  32.6 0.1 pair_sum.2
  32.7 0.3 collective-permute-start.10
  33.0 1.9 %collective-permute-start.11 = (bf16[32,3072]{1,0:T(8,128)(2,1)S(1)}, bf16[32,3072]{1,0:T(8,128)(2,1)S(1)}, u32[]{:S(2)}, u32[]{:S(2)}) collective-permute-start(bf16[32,3072]{1,0:T(8,128)(2,1)S(1)} %get-tuple-element.42), channel_id=1, source_target_pairs={{0,6},{1,7},{2,0},{3,1},{4,2},{5,3},{6,4},{7,5},{8,14},{9,15},{10,... | collective-permute-start | bytes 589832 | tf_op jit(solution)/shard_map/ppermute | solution.py:32
  35.0 1.6 %collective-permute-start.12 = (bf16[32,3072]{1,0:T(8,128)(2,1)S(1)}, bf16[32,3072]{1,0:T(8,128)(2,1)S(1)}, u32[]{:S(2)}, u32[]{:S(2)}) collective-permute-start(bf16[32,3072]{1,0:T(8,128)(2,1)S(1)} %get-tuple-element.43), channel_id=1, source_target_pairs={{0,4},{1,5},{2,6},{3,7},{4,0},{5,1},{6,2},{7,3},{8,12},{9,13},{10,... | collective-permute-start | bytes 589832 | tf_op jit(solution)/shard_map/ppermute | solution.py:32
  36.6 4.2 %collective-permute-done.10.r1 = bf16[32,3072]{1,0:T(8,128)(2,1)S(1)} collective-permute-done((bf16[32,3072]{1,0:T(8,128)(2,1)S(1)}, bf16[32,3072]{1,0:T(8,128)(2,1)S(1)}, u32[]{:S(2)}, u32[]{:S(2)}) %collective-permute-start.10) | collective-permute-done | bytes 196640 | tf_op jit(solution)/shard_map/ppermute | solution.py:32
  40.7 0.0 collective-permute-done.11.r3
  40.7 4.1 %collective-permute-done.12.r2 = bf16[32,3072]{1,0:T(8,128)(2,1)S(1)} collective-permute-done((bf16[32,3072]{1,0:T(8,128)(2,1)S(1)}, bf16[32,3072]{1,0:T(8,128)(2,1)S(1)}, u32[]{:S(2)}, u32[]{:S(2)}) %collective-permute-start.12) | collective-permute-done | bytes 196640 | tf_op jit(solution)/shard_map/ppermute | solution.py:32
  44.8 0.1 column_sum.1
  45.0 0.1 collective-permute-start.14
  45.1 0.1 collective-permute-start.13
  45.2 10.4 %collective-permute-done.14.p1 = bf16[32,3072]{1,0:T(8,128)(2,1)S(1)} collective-permute-done((bf16[32,3072]{1,0:T(8,128)(2,1)S(1)}, bf16[32,3072]{1,0:T(8,128)(2,1)S(1)}, u32[]{:S(2)}, u32[]{:S(2)}) %collective-permute-start.14) | collective-permute-done | bytes 196640 | tf_op jit(solution)/shard_map/ppermute | solution.py:46
  55.6 1.2 %collective-permute-done.13.p0 = bf16[32,3072]{1,0:T(8,128)(2,1)S(1)} collective-permute-done((bf16[32,3072]{1,0:T(8,128)(2,1)S(1)}, bf16[32,3072]{1,0:T(8,128)(2,1)S(1)}, u32[]{:S(2)}, u32[]{:S(2)}) %collective-permute-start.13) | collective-permute-done | bytes 196640 | tf_op jit(solution)/shard_map/ppermute | solution.py:46
  56.8 0.4 norm_next.1
  57.2 1.0 collective-permute-start.18
  58.2 1.1 %collective-permute-start.17 = (bf16[32,3072]{1,0:T(8,128)(2,1)S(1)}, bf16[32,3072]{1,0:T(8,128)(2,1)S(1)}, u32[]{:S(2)}, u32[]{:S(2)}) collective-permute-start(bf16[32,3072]{1,0:T(8,128)(2,1)S(1)} %get-tuple-element.46.n0), channel_id=1, source_target_pairs={{0,6},{1,7},{2,0},{3,1},{4,2},{5,3},{6,4},{7,5},{8,14},{9,15},{10,... | collective-permute-start | bytes 589832 | tf_op jit(solution)/shard_map/ppermute | solution.py:32
  59.3 2.4 %collective-permute-start.16 = (bf16[32,3072]{1,0:T(8,128)(2,1)S(1)}, bf16[32,3072]{1,0:T(8,128)(2,1)S(1)}, u32[]{:S(2)}, u32[]{:S(2)}) collective-permute-start(bf16[32,3072]{1,0:T(8,128)(2,1)S(1)} %get-tuple-element.46.n0), channel_id=1, source_target_pairs={{0,4},{1,5},{2,6},{3,7},{4,0},{5,1},{6,2},{7,3},{8,12},{9,13},{10,... | collective-permute-start | bytes 589832 | tf_op jit(solution)/shard_map/ppermute | solution.py:32
  61.7 0.0 collective-permute-start.19
  61.7 2.9 %collective-permute-done.18.n3 = bf16[32,3072]{1,0:T(8,128)(2,1)S(1)} collective-permute-done((bf16[32,3072]{1,0:T(8,128)(2,1)S(1)}, bf16[32,3072]{1,0:T(8,128)(2,1)S(1)}, u32[]{:S(2)}, u32[]{:S(2)}) %collective-permute-start.18) | collective-permute-done | bytes 196640 | tf_op jit(solution)/shard_map/ppermute | solution.py:32
  64.6 1.1 %collective-permute-done.17.n1 = bf16[32,3072]{1,0:T(8,128)(2,1)S(1)} collective-permute-done((bf16[32,3072]{1,0:T(8,128)(2,1)S(1)}, bf16[32,3072]{1,0:T(8,128)(2,1)S(1)}, u32[]{:S(2)}, u32[]{:S(2)}) %collective-permute-start.17) | collective-permute-done | bytes 196640 | tf_op jit(solution)/shard_map/ppermute | solution.py:32
  65.7 2.1 %collective-permute-done.16.n2 = bf16[32,3072]{1,0:T(8,128)(2,1)S(1)} collective-permute-done((bf16[32,3072]{1,0:T(8,128)(2,1)S(1)}, bf16[32,3072]{1,0:T(8,128)(2,1)S(1)}, u32[]{:S(2)}, u32[]{:S(2)}) %collective-permute-start.16) | collective-permute-done | bytes 196640 | tf_op jit(solution)/shard_map/ppermute | solution.py:32
  67.9 0.0 collective-permute-done.22.s3
  67.9 1.4 %collective-permute-done.20.s2 = bf16[32,3072]{1,0:T(8,128)(2,1)S(1)} collective-permute-done((bf16[32,3072]{1,0:T(8,128)(2,1)S(1)}, bf16[32,3072]{1,0:T(8,128)(2,1)S(1)}, u32[]{:S(2)}, u32[]{:S(2)}) %collective-permute-start.20) | collective-permute-done | bytes 196640 | tf_op jit(solution)/shard_map/ppermute | solution.py:28
  69.3 3.8 %block.3 = (bf16[2,4096,128]{2,1,0:T(8,128)(2,1)S(1)}, bf16[256,512]{1,0:T(8,128)(2,1)S(1)}, bf16[128,128]{1,0:T(8,128)(2,1)S(1)}, bf16[128,3072]{1,0:T(8,128)(2,1)S(1)}, bf16[2,4096,128]{2,1,0:T(8,128)(2,1)}) custom-call(s32[16]{0:T(128)S(1)} %copy-done.2, bf16[32,3072]{1,0:T(8,128)(2,1)S(1)} %get-tuple-element.46.n0, ...), custom_call_target="tpu_custom_call", output_to_operand_aliasing={{0}: (11, {})} | custom-call | flops 30000001024 | bytes 12000000 | tf_op jit(solution)/shard_map/block/pallas_call | solution.py:79
  73.1 0.4 collective-permute-start.23
  73.6 1.7 %own_half.3.mine = f32[128,3072]{1,0:T(8,128)S(1)} custom-call(bf16[128,128]{1,0:T(8,128)(2,1)S(1)} %get-tuple-element.47.queries, bf16[2,4096,128]{2,1,0:T(8,128)(2,1)S(1)} %get-tuple-element.48.kv, bf16[256,512]{1,0:T(8,128)(2,1)S(1)} %get-tuple-element.49.joined, bf16[512,3072]{1,0:T(8,128)(2,1)S(1)} %get-tuple-element.38.w2.rest_1_), custom_call_target="tpu_custom_call" | custom-call | flops 12000000000 | bytes 4700000 | tf_op jit(solution)/shard_map/own_half/pallas_call | solution.py:79
  75.3 0.0 collective-permute-done.15.passing.kept
  75.3 0.4 collective-permute-done.23.came
  75.7 0.1 pair_sum.3
  75.9 0.4 collective-permute-start.24
  76.3 1.8 %collective-permute-start.25 = (bf16[32,3072]{1,0:T(8,128)(2,1)S(1)}, bf16[32,3072]{1,0:T(8,128)(2,1)S(1)}, u32[]{:S(2)}, u32[]{:S(2)}) collective-permute-start(bf16[32,3072]{1,0:T(8,128)(2,1)S(1)} %get-tuple-element.53), channel_id=1, source_target_pairs={{0,6},{1,7},{2,0},{3,1},{4,2},{5,3},{6,4},{7,5},{8,14},{9,15},{10,... | collective-permute-start | bytes 589832 | tf_op jit(solution)/shard_map/ppermute | solution.py:32
  78.1 3.1 %collective-permute-start.26 = (bf16[32,3072]{1,0:T(8,128)(2,1)S(1)}, bf16[32,3072]{1,0:T(8,128)(2,1)S(1)}, u32[]{:S(2)}, u32[]{:S(2)}) collective-permute-start(bf16[32,3072]{1,0:T(8,128)(2,1)S(1)} %get-tuple-element.54), channel_id=1, source_target_pairs={{0,4},{1,5},{2,6},{3,7},{4,0},{5,1},{6,2},{7,3},{8,12},{9,13},{10,... | collective-permute-start | bytes 589832 | tf_op jit(solution)/shard_map/ppermute | solution.py:32
  81.2 2.5 %collective-permute-done.24.r1 = bf16[32,3072]{1,0:T(8,128)(2,1)S(1)} collective-permute-done((bf16[32,3072]{1,0:T(8,128)(2,1)S(1)}, bf16[32,3072]{1,0:T(8,128)(2,1)S(1)}, u32[]{:S(2)}, u32[]{:S(2)}) %collective-permute-start.24) | collective-permute-done | bytes 196640 | tf_op jit(solution)/shard_map/ppermute | solution.py:32
  83.7 1.1 %collective-permute-done.25.r3 = bf16[32,3072]{1,0:T(8,128)(2,1)S(1)} collective-permute-done((bf16[32,3072]{1,0:T(8,128)(2,1)S(1)}, bf16[32,3072]{1,0:T(8,128)(2,1)S(1)}, u32[]{:S(2)}, u32[]{:S(2)}) %collective-permute-start.25) | collective-permute-done | bytes 196640 | tf_op jit(solution)/shard_map/ppermute | solution.py:32
  84.8 5.4 %collective-permute-done.26.r2 = bf16[32,3072]{1,0:T(8,128)(2,1)S(1)} collective-permute-done((bf16[32,3072]{1,0:T(8,128)(2,1)S(1)}, bf16[32,3072]{1,0:T(8,128)(2,1)S(1)}, u32[]{:S(2)}, u32[]{:S(2)}) %collective-permute-start.26) | collective-permute-done | bytes 196640 | tf_op jit(solution)/shard_map/ppermute | solution.py:32
  90.2 0.1 column_last.1
  90.3 0.1 collective-permute-start.27
  90.4 1.5 %collective-permute-start.28 = (bf16[16,3072]{1,0:T(8,128)(2,1)S(1)}, bf16[16,3072]{1,0:T(8,128)(2,1)S(1)}, u32[]{:S(2)}, u32[]{:S(2)}) collective-permute-start(bf16[16,3072]{1,0:T(8,128)(2,1)S(1)} %get-tuple-element.56), channel_id=1, source_target_pairs={{0,24},{1,25},{2,26},{3,27},{4,28},{5,29},{6,30},{7,31},{8,16},{9,... | collective-permute-start | bytes 294920 | tf_op jit(solution)/shard_map/ppermute | solution.py:46
  91.9 5.4 %collective-permute-done.27.p0 = bf16[16,3072]{1,0:T(8,128)(2,1)S(1)} collective-permute-done((bf16[16,3072]{1,0:T(8,128)(2,1)S(1)}, bf16[16,3072]{1,0:T(8,128)(2,1)S(1)}, u32[]{:S(2)}, u32[]{:S(2)}) %collective-permute-start.27) | collective-permute-done | bytes 98336 | tf_op jit(solution)/shard_map/ppermute | solution.py:46
  97.3 2.3 %collective-permute-done.28.p1 = bf16[16,3072]{1,0:T(8,128)(2,1)S(1)} collective-permute-done((bf16[16,3072]{1,0:T(8,128)(2,1)S(1)}, bf16[16,3072]{1,0:T(8,128)(2,1)S(1)}, u32[]{:S(2)}, u32[]{:S(2)}) %collective-permute-start.28) | collective-permute-done | bytes 98336 | tf_op jit(solution)/shard_map/ppermute | solution.py:46
  99.6 0.7 residual_last.1
  (14 shorter events, 0.0 us)
Async XLA Ops:
  0.6 7.5 %collective-permute-start = (bf16[16,3072]{1,0:T(8,128)(2,1)}, bf16[16,3072]{1,0:T(8,128)(2,1)S(1)}, u32[]{:S(2)}, u32[]{:S(2)}) collective-permute-start(bf16[16,3072]{1,0:T(8,128)(2,1)} %bitcast.14), channel_id=1, source_target_pairs={{0,8},{1,9},{2,10},{3,11},{4,12},{5,13},{6,14},{7,15},{8,0},{9,1},... | collective-permute-start | bytes 294920 | tf_op jit(solution)/shard_map/ppermute | solution.py:38
  3.7 0.7 copy-start.1
  4.4 3.8 %copy-start = (bf16[1,16,3072]{2,1,0:T(8,128)(2,1)S(1)}, bf16[1,16,3072]{2,1,0:T(8,128)(2,1)}, u32[]{:S(2)}) copy-start(bf16[1,16,3072]{2,1,0:T(8,128)(2,1)} %param.10) | copy-start | bytes 294916
  4.4 18.2 %copy-start.2 = (s32[16]{0:T(128)S(1)}, s32[16]{0:T(128)}, u32[]{:S(2)}) copy-start(s32[16]{0:T(128)} %patches.3) | copy-start | bytes 196
  4.4 18.2 %copy-start.3 = (bf16[1,2,128]{2,1,0:T(2,128)(2,1)S(1)}, bf16[1,2,128]{2,1,0:T(2,128)(2,1)}, u32[]{:S(2)}) copy-start(bf16[1,2,128]{2,1,0:T(2,128)(2,1)} %param.15) | copy-start | bytes 1540
  8.4 7.5 %collective-permute-start.4 = (bf16[32,3072]{1,0:T(8,128)(2,1)S(1)}, bf16[32,3072]{1,0:T(8,128)(2,1)S(1)}, u32[]{:S(2)}, u32[]{:S(2)}) collective-permute-start(bf16[32,3072]{1,0:T(8,128)(2,1)S(1)} %get-tuple-element.32.n0), channel_id=1, source_target_pairs={{0,2},{1,3},{2,4},{3,5},{4,6},{5,7},{6,0},{7,1},{8,10},{9,11},{10,... | collective-permute-start | bytes 589832 | tf_op jit(solution)/shard_map/ppermute | solution.py:32
  10.1 7.1 %collective-permute-start.3 = (bf16[32,3072]{1,0:T(8,128)(2,1)S(1)}, bf16[32,3072]{1,0:T(8,128)(2,1)S(1)}, u32[]{:S(2)}, u32[]{:S(2)}) collective-permute-start(bf16[32,3072]{1,0:T(8,128)(2,1)S(1)} %get-tuple-element.32.n0), channel_id=1, source_target_pairs={{0,6},{1,7},{2,0},{3,1},{4,2},{5,3},{6,4},{7,5},{8,14},{9,15},{10,... | collective-permute-start | bytes 589832 | tf_op jit(solution)/shard_map/ppermute | solution.py:32
  10.5 10.6 %collective-permute-start.2 = (bf16[32,3072]{1,0:T(8,128)(2,1)S(1)}, bf16[32,3072]{1,0:T(8,128)(2,1)S(1)}, u32[]{:S(2)}, u32[]{:S(2)}) collective-permute-start(bf16[32,3072]{1,0:T(8,128)(2,1)S(1)} %get-tuple-element.32.n0), channel_id=1, source_target_pairs={{0,4},{1,5},{2,6},{3,7},{4,0},{5,1},{6,2},{7,3},{8,12},{9,13},{10,... | collective-permute-start | bytes 589832 | tf_op jit(solution)/shard_map/ppermute | solution.py:32
  12.8 8.9 %collective-permute-start.5 = (bf16[32,3072]{1,0:T(8,128)(2,1)S(1)}, bf16[32,3072]{1,0:T(8,128)(2,1)S(1)}, u32[]{:S(2)}, u32[]{:S(2)}) collective-permute-start(bf16[32,3072]{1,0:T(8,128)(2,1)S(1)} %get-tuple-element.32.n0), channel_id=1, source_target_pairs={{0,1},{1,0},{2,3},{3,2},{4,5},{5,4},{6,7},{7,6},{8,9},{9,8},{10,11... | collective-permute-start | bytes 589832 | tf_op jit(solution)/shard_map/ppermute | solution.py:28
  15.9 5.8 %collective-permute-start.8 = (bf16[32,3072]{1,0:T(8,128)(2,1)S(1)}, bf16[32,3072]{1,0:T(8,128)(2,1)S(1)}, u32[]{:S(2)}, u32[]{:S(2)}) collective-permute-start(bf16[32,3072]{1,0:T(8,128)(2,1)S(1)} %collective-permute-done.4.n3), channel_id=1, source_target_pairs={{0,1},{1,0},{2,3},{3,2},{4,5},{5,4},{6,7},{7,6},{8,9},{9,8},{10,11... | collective-permute-start | bytes 589832 | tf_op jit(solution)/shard_map/ppermute | solution.py:28
  17.2 4.5 %collective-permute-start.7 = (bf16[32,3072]{1,0:T(8,128)(2,1)S(1)}, bf16[32,3072]{1,0:T(8,128)(2,1)S(1)}, u32[]{:S(2)}, u32[]{:S(2)}) collective-permute-start(bf16[32,3072]{1,0:T(8,128)(2,1)S(1)} %collective-permute-done.3.n1), channel_id=1, source_target_pairs={{0,1},{1,0},{2,3},{3,2},{4,5},{5,4},{6,7},{7,6},{8,9},{9,8},{10,11... | collective-permute-start | bytes 589832 | tf_op jit(solution)/shard_map/ppermute | solution.py:28
  21.1 1.4 %collective-permute-start.6 = (bf16[32,3072]{1,0:T(8,128)(2,1)S(1)}, bf16[32,3072]{1,0:T(8,128)(2,1)S(1)}, u32[]{:S(2)}, u32[]{:S(2)}) collective-permute-start(bf16[32,3072]{1,0:T(8,128)(2,1)S(1)} %collective-permute-done.2.n2), channel_id=1, source_target_pairs={{0,1},{1,0},{2,3},{3,2},{4,5},{5,4},{6,7},{7,6},{8,9},{9,8},{10,11... | collective-permute-start | bytes 589832 | tf_op jit(solution)/shard_map/ppermute | solution.py:28
  21.1 11.5 %collective-permute-start.1 = (bf16[32,3072]{1,0:T(8,128)(2,1)S(1)}, bf16[32,3072]{1,0:T(8,128)(2,1)S(1)}, u32[]{:S(2)}, u32[]{:S(2)}) collective-permute-start(bf16[32,3072]{1,0:T(8,128)(2,1)S(1)} %get-tuple-element.31), channel_id=1, source_target_pairs={{0,16},{1,17},{2,18},{3,19},{4,20},{5,21},{6,22},{7,23},{8,24},{9,... | collective-permute-start | bytes 589832 | tf_op jit(solution)/shard_map/ppermute | solution.py:46
  26.8 5.8 %collective-permute-start.9 = (bf16[128,3072]{1,0:T(8,128)(2,1)S(1)}, bf16[128,3072]{1,0:T(8,128)(2,1)S(1)}, u32[]{:S(2)}, u32[]{:S(2)}) collective-permute-start(bf16[128,3072]{1,0:T(8,128)(2,1)S(1)} %get-tuple-element.39), channel_id=1, source_target_pairs={{0,1},{1,0},{2,3},{3,2},{4,5},{5,4},{6,7},{7,6},{8,9},{9,8},{10,11... | collective-permute-start | bytes 2359304 | tf_op jit(solution)/shard_map/ppermute | solution.py:28
  32.7 8.0 %collective-permute-start.10 = (bf16[32,3072]{1,0:T(8,128)(2,1)S(1)}, bf16[32,3072]{1,0:T(8,128)(2,1)S(1)}, u32[]{:S(2)}, u32[]{:S(2)}) collective-permute-start(bf16[32,3072]{1,0:T(8,128)(2,1)S(1)} %get-tuple-element.41), channel_id=1, source_target_pairs={{0,2},{1,3},{2,4},{3,5},{4,6},{5,7},{6,0},{7,1},{8,10},{9,11},{10,... | collective-permute-start | bytes 589832 | tf_op jit(solution)/shard_map/ppermute | solution.py:32
  33.0 7.7 %collective-permute-start.11 = (bf16[32,3072]{1,0:T(8,128)(2,1)S(1)}, bf16[32,3072]{1,0:T(8,128)(2,1)S(1)}, u32[]{:S(2)}, u32[]{:S(2)}) collective-permute-start(bf16[32,3072]{1,0:T(8,128)(2,1)S(1)} %get-tuple-element.42), channel_id=1, source_target_pairs={{0,6},{1,7},{2,0},{3,1},{4,2},{5,3},{6,4},{7,5},{8,14},{9,15},{10,... | collective-permute-start | bytes 589832 | tf_op jit(solution)/shard_map/ppermute | solution.py:32
  35.0 9.9 %collective-permute-start.12 = (bf16[32,3072]{1,0:T(8,128)(2,1)S(1)}, bf16[32,3072]{1,0:T(8,128)(2,1)S(1)}, u32[]{:S(2)}, u32[]{:S(2)}) collective-permute-start(bf16[32,3072]{1,0:T(8,128)(2,1)S(1)} %get-tuple-element.43), channel_id=1, source_target_pairs={{0,4},{1,5},{2,6},{3,7},{4,0},{5,1},{6,2},{7,3},{8,12},{9,13},{10,... | collective-permute-start | bytes 589832 | tf_op jit(solution)/shard_map/ppermute | solution.py:32
  45.0 10.7 %collective-permute-start.14 = (bf16[32,3072]{1,0:T(8,128)(2,1)S(1)}, bf16[32,3072]{1,0:T(8,128)(2,1)S(1)}, u32[]{:S(2)}, u32[]{:S(2)}) collective-permute-start(bf16[32,3072]{1,0:T(8,128)(2,1)S(1)} %column_sum.1), channel_id=1, source_target_pairs={{0,24},{1,25},{2,26},{3,27},{4,28},{5,29},{6,30},{7,31},{8,16},{9,... | collective-permute-start | bytes 589832 | tf_op jit(solution)/shard_map/ppermute | solution.py:46
  45.1 11.8 %collective-permute-start.13 = (bf16[32,3072]{1,0:T(8,128)(2,1)S(1)}, bf16[32,3072]{1,0:T(8,128)(2,1)S(1)}, u32[]{:S(2)}, u32[]{:S(2)}) collective-permute-start(bf16[32,3072]{1,0:T(8,128)(2,1)S(1)} %column_sum.1), channel_id=1, source_target_pairs={{0,16},{1,17},{2,18},{3,19},{4,20},{5,21},{6,22},{7,23},{8,24},{9,... | collective-permute-start | bytes 589832 | tf_op jit(solution)/shard_map/ppermute | solution.py:46
  57.2 7.4 %collective-permute-start.18 = (bf16[32,3072]{1,0:T(8,128)(2,1)S(1)}, bf16[32,3072]{1,0:T(8,128)(2,1)S(1)}, u32[]{:S(2)}, u32[]{:S(2)}) collective-permute-start(bf16[32,3072]{1,0:T(8,128)(2,1)S(1)} %get-tuple-element.46.n0), channel_id=1, source_target_pairs={{0,2},{1,3},{2,4},{3,5},{4,6},{5,7},{6,0},{7,1},{8,10},{9,11},{10,... | collective-permute-start | bytes 589832 | tf_op jit(solution)/shard_map/ppermute | solution.py:32
  58.2 7.5 %collective-permute-start.17 = (bf16[32,3072]{1,0:T(8,128)(2,1)S(1)}, bf16[32,3072]{1,0:T(8,128)(2,1)S(1)}, u32[]{:S(2)}, u32[]{:S(2)}) collective-permute-start(bf16[32,3072]{1,0:T(8,128)(2,1)S(1)} %get-tuple-element.46.n0), channel_id=1, source_target_pairs={{0,6},{1,7},{2,0},{3,1},{4,2},{5,3},{6,4},{7,5},{8,14},{9,15},{10,... | collective-permute-start | bytes 589832 | tf_op jit(solution)/shard_map/ppermute | solution.py:32
  59.3 8.5 %collective-permute-start.16 = (bf16[32,3072]{1,0:T(8,128)(2,1)S(1)}, bf16[32,3072]{1,0:T(8,128)(2,1)S(1)}, u32[]{:S(2)}, u32[]{:S(2)}) collective-permute-start(bf16[32,3072]{1,0:T(8,128)(2,1)S(1)} %get-tuple-element.46.n0), channel_id=1, source_target_pairs={{0,4},{1,5},{2,6},{3,7},{4,0},{5,1},{6,2},{7,3},{8,12},{9,13},{10,... | collective-permute-start | bytes 589832 | tf_op jit(solution)/shard_map/ppermute | solution.py:32
  61.7 6.1 %collective-permute-start.19 = (bf16[32,3072]{1,0:T(8,128)(2,1)S(1)}, bf16[32,3072]{1,0:T(8,128)(2,1)S(1)}, u32[]{:S(2)}, u32[]{:S(2)}) collective-permute-start(bf16[32,3072]{1,0:T(8,128)(2,1)S(1)} %get-tuple-element.46.n0), channel_id=1, source_target_pairs={{0,1},{1,0},{2,3},{3,2},{4,5},{5,4},{6,7},{7,6},{8,9},{9,8},{10,11... | collective-permute-start | bytes 589832 | tf_op jit(solution)/shard_map/ppermute | solution.py:28
  64.6 3.2 %collective-permute-start.22 = (bf16[32,3072]{1,0:T(8,128)(2,1)S(1)}, bf16[32,3072]{1,0:T(8,128)(2,1)S(1)}, u32[]{:S(2)}, u32[]{:S(2)}) collective-permute-start(bf16[32,3072]{1,0:T(8,128)(2,1)S(1)} %collective-permute-done.18.n3), channel_id=1, source_target_pairs={{0,1},{1,0},{2,3},{3,2},{4,5},{5,4},{6,7},{7,6},{8,9},{9,8},{10,11... | collective-permute-start | bytes 589832 | tf_op jit(solution)/shard_map/ppermute | solution.py:28
  65.7 2.1 %collective-permute-start.21 = (bf16[32,3072]{1,0:T(8,128)(2,1)S(1)}, bf16[32,3072]{1,0:T(8,128)(2,1)S(1)}, u32[]{:S(2)}, u32[]{:S(2)}) collective-permute-start(bf16[32,3072]{1,0:T(8,128)(2,1)S(1)} %collective-permute-done.17.n1), channel_id=1, source_target_pairs={{0,1},{1,0},{2,3},{3,2},{4,5},{5,4},{6,7},{7,6},{8,9},{9,8},{10,11... | collective-permute-start | bytes 589832 | tf_op jit(solution)/shard_map/ppermute | solution.py:28
  67.8 1.4 %collective-permute-start.20 = (bf16[32,3072]{1,0:T(8,128)(2,1)S(1)}, bf16[32,3072]{1,0:T(8,128)(2,1)S(1)}, u32[]{:S(2)}, u32[]{:S(2)}) collective-permute-start(bf16[32,3072]{1,0:T(8,128)(2,1)S(1)} %collective-permute-done.16.n2), channel_id=1, source_target_pairs={{0,1},{1,0},{2,3},{3,2},{4,5},{5,4},{6,7},{7,6},{8,9},{9,8},{10,11... | collective-permute-start | bytes 589832 | tf_op jit(solution)/shard_map/ppermute | solution.py:28
  67.8 7.5 %collective-permute-start.15 = (bf16[16,3072]{1,0:T(8,128)(2,1)S(1)}, bf16[16,3072]{1,0:T(8,128)(2,1)S(1)}, u32[]{:S(2)}, u32[]{:S(2)}) collective-permute-start(bf16[16,3072]{1,0:T(8,128)(2,1)S(1)} %get-tuple-element.45), channel_id=1, source_target_pairs={{0,16},{1,17},{2,18},{3,19},{4,20},{5,21},{6,22},{7,23},{8,24},{9,... | collective-permute-start | bytes 294920 | tf_op jit(solution)/shard_map/ppermute | solution.py:46
  73.1 2.6 %collective-permute-start.23 = (bf16[128,3072]{1,0:T(8,128)(2,1)S(1)}, bf16[128,3072]{1,0:T(8,128)(2,1)S(1)}, u32[]{:S(2)}, u32[]{:S(2)}) collective-permute-start(bf16[128,3072]{1,0:T(8,128)(2,1)S(1)} %get-tuple-element.50), channel_id=1, source_target_pairs={{0,1},{1,0},{2,3},{3,2},{4,5},{5,4},{6,7},{7,6},{8,9},{9,8},{10,11... | collective-permute-start | bytes 2359304 | tf_op jit(solution)/shard_map/ppermute | solution.py:28
  75.9 7.8 %collective-permute-start.24 = (bf16[32,3072]{1,0:T(8,128)(2,1)S(1)}, bf16[32,3072]{1,0:T(8,128)(2,1)S(1)}, u32[]{:S(2)}, u32[]{:S(2)}) collective-permute-start(bf16[32,3072]{1,0:T(8,128)(2,1)S(1)} %get-tuple-element.52), channel_id=1, source_target_pairs={{0,2},{1,3},{2,4},{3,5},{4,6},{5,7},{6,0},{7,1},{8,10},{9,11},{10,... | collective-permute-start | bytes 589832 | tf_op jit(solution)/shard_map/ppermute | solution.py:32
  76.3 8.4 %collective-permute-start.25 = (bf16[32,3072]{1,0:T(8,128)(2,1)S(1)}, bf16[32,3072]{1,0:T(8,128)(2,1)S(1)}, u32[]{:S(2)}, u32[]{:S(2)}) collective-permute-start(bf16[32,3072]{1,0:T(8,128)(2,1)S(1)} %get-tuple-element.53), channel_id=1, source_target_pairs={{0,6},{1,7},{2,0},{3,1},{4,2},{5,3},{6,4},{7,5},{8,14},{9,15},{10,... | collective-permute-start | bytes 589832 | tf_op jit(solution)/shard_map/ppermute | solution.py:32
  78.1 12.1 %collective-permute-start.26 = (bf16[32,3072]{1,0:T(8,128)(2,1)S(1)}, bf16[32,3072]{1,0:T(8,128)(2,1)S(1)}, u32[]{:S(2)}, u32[]{:S(2)}) collective-permute-start(bf16[32,3072]{1,0:T(8,128)(2,1)S(1)} %get-tuple-element.54), channel_id=1, source_target_pairs={{0,4},{1,5},{2,6},{3,7},{4,0},{5,1},{6,2},{7,3},{8,12},{9,13},{10,... | collective-permute-start | bytes 589832 | tf_op jit(solution)/shard_map/ppermute | solution.py:32
  90.3 7.0 %collective-permute-start.27 = (bf16[16,3072]{1,0:T(8,128)(2,1)S(1)}, bf16[16,3072]{1,0:T(8,128)(2,1)S(1)}, u32[]{:S(2)}, u32[]{:S(2)}) collective-permute-start(bf16[16,3072]{1,0:T(8,128)(2,1)S(1)} %get-tuple-element.55), channel_id=1, source_target_pairs={{0,16},{1,17},{2,18},{3,19},{4,20},{5,21},{6,22},{7,23},{8,24},{9,... | collective-permute-start | bytes 294920 | tf_op jit(solution)/shard_map/ppermute | solution.py:46
  90.4 9.3 %collective-permute-start.28 = (bf16[16,3072]{1,0:T(8,128)(2,1)S(1)}, bf16[16,3072]{1,0:T(8,128)(2,1)S(1)}, u32[]{:S(2)}, u32[]{:S(2)}) collective-permute-start(bf16[16,3072]{1,0:T(8,128)(2,1)S(1)} %get-tuple-element.56), channel_id=1, source_target_pairs={{0,24},{1,25},{2,26},{3,27},{4,28},{5,29},{6,30},{7,31},{8,16},{9,... | collective-permute-start | bytes 294920 | tf_op jit(solution)/shard_map/ppermute | solution.py:46

commit v5 on v4

--- a/solution.py
+++ b/solution.py
@@ -174,7 +174,15 @@
     return (mixed / total).astype(BF)
 
 
-def block_body(last, patches, n0, n2, n1, n3, s0, s2, s1, s3, w1, gains, *rest):
+def project_body(n0, n2, n1, n3, w1, out, rows):
+    for i, piece in enumerate((n0, n1, n2, n3)):
+        rows[i * PAIR:(i + 1) * PAIR, :] = piece[...]
+    for j in range(3):
+        at = slice(j * 256, (j + 1) * 256)
+        out[:, at] = jnp.dot(rows[...], w1[:, at], preferred_element_type=F32)
+
+
+def block_body(last, patches, first, s0, s2, s1, s3, w1, gains, *rest):
     if last:
         (old, w2, kv, joined, queries, partial, new_cache, rows, scores, sems) = rest
         reads = []
@@ -187,12 +195,14 @@
     anchor, _ = turn(1 if last else 0)
     patch = pl.multiple_of(patches[anchor] * ROWS, ROWS)
     _, y, core = spot()
-    for i, piece in enumerate((n0, n1, n2, n3, s0, s1, s2, s3)):
+    for i, piece in enumerate((s0, s1, s2, s3)):
         rows[i * PAIR:(i + 1) * PAIR, :] = piece[...]
-    h = rows[...]
-    qk = jnp.dot(h, w1[:, 0:256], preferred_element_type=F32).astype(BF)
-    vm = jnp.dot(h, w1[:, 256:512], preferred_element_type=F32)
-    mm = jnp.dot(h, w1[:, 512:768], preferred_element_type=F32)
+    parts = []
+    for j in range(3):
+        at = slice(j * 256, (j + 1) * 256)
+        second = jnp.dot(rows[...], w1[:, at], preferred_element_type=F32)
+        parts.append(jnp.concatenate([first[:, at], second], axis=0))
+    qk, vm, mm = parts[0].astype(BF), parts[1], parts[2]
     query = head_norm(qk[:, :HD], gains[0:1, :])
     key = head_norm(qk[:, HD:], gains[1:2, :])
     value = vm[:, :HD].astype(BF)
@@ -233,7 +243,8 @@
         )
 
 
-def pair_body(mine, came, passing, o0, o1, o2, o3):
+def pair_body(mine, came, *outs):
+    o0, o1, o2, o3 = outs[-4:]
     o0[...] = mine[0:PAIR, :] + came[0:PAIR, :].astype(F32)
     for i, o in ((1, o1), (2, o2), (3, o3)):
         a, b = i * PAIR, (i + 1) * PAIR
@@ -273,6 +284,15 @@
     n3 = send_y(normed, 1)
     n1 = send_y(normed, 3)
     core_parts += [send_core(p) for p in (n2, n1, n3)]
+    (first,) = local_call(
+        project_body,
+        [("vmem", (HALF, 6 * HD), F32)],
+        [("vmem", p) for p in (normed, n2, n1, n3)] + [("vmem", w1)],
+        scratch=[pltpu.VMEM((HALF, D), BF)],
+        flops=3_000_000_000,
+        moved=5_500_000,
+        name="project_own",
+    )
     cache_shape = (2, TOKENS, HD)
     outs = [
         ("vmem", cache_shape, BF),
@@ -285,10 +305,10 @@
     kv, joined, queries, partial, fifth = local_call(
         functools.partial(block_body, last),
         outs,
-        [("smem", patches)] + [("vmem", p) for p in [normed, n2, n1, n3] + core_parts]
+        [("smem", patches)] + [("vmem", p) for p in [first] + core_parts]
         + [("vmem", w1), ("vmem", gains), ("vmem", kv)] + [(kind, a) for a in weights],
         scratch=[
-            pltpu.VMEM((ROWS, D), BF),
+            pltpu.VMEM((HALF, D), BF),
             pltpu.VMEM((HALF, TOKENS), F32),
             pltpu.SemaphoreType.DMA((2,)),
         ],
@@ -296,7 +316,7 @@
         flops=30_000_000_000,
         moved=12_000_000,
         name="block",
-        aliases={11: 0},
+        aliases={8: 0},
     )
     w2 = weights[0] if last else fifth
     came = send_core(partial)
@@ -312,7 +332,7 @@
     o0, o1, o2, o3 = local_call(
         pair_body,
         [("vmem", (PAIR, D), F32)] + [("vmem", (PAIR, D), BF)] * 3,
-        [("vmem", mine), ("vmem", came), ("any", passing)],
+        [("vmem", mine), ("vmem", came)] + [("any", p) for p in passing],
         flops=400_000,
         moved=3_000_000,
         name="pair_sum",
@@ -370,7 +390,7 @@
     )
     kept = send_on(kept, 0)
     sums, kv, w2 = block(
-        False, normed, kept, patch_of_slot, w1, gains, kv, (w_attn_out[0], w_mlp_out[0])
+        False, normed, (), patch_of_slot, w1, gains, kv, (w_attn_out[0], w_mlp_out[0])
     )
     (out,) = local_call(
         column_body,
@@ -390,7 +410,7 @@
         name="norm_next",
     )
     kept = send_on(kept, 0)
-    sums, _, cache = block(True, normed, kept, patch_of_slot, w1, gains, kv, (w2,))
+    sums, _, cache = block(True, normed, (kept,), patch_of_slot, w1, gains, kv, (w2,))
     here, there = local_call(
         last_column_body,
         [("vmem", (PIECE, D), BF)] * 2,

time: 100 us -> 98.9 us (0.989)
  waiting for transfers between devices: 57.4 us -> 53.9 us
  starting transfers between devices: 24.3 us -> 25.8 us
    ppermute x6, waiting for transfers between devices: 23.2 us -> 19.4 us  [send_on(): return lax.ppermute(x, ('section', 'sp'), pairs)]
    ppermute x6, starting transfers between devices: 2.44 us -> 4.09 us  [send_on(): return lax.ppermute(x, ('section', 'sp'), pairs)]
    pallas_call x12 -> x14, Pallas kernels: 17.1 us -> 17.6 us  [local_call(): pl.pallas_call(body, out_shape=out_shape, in_specs=specs, out_specs=out_s...]
  transfers between devices with their start and end apart: 29 -> 29, of which waited for: 19 -> 18; matrix products, arithmetic and copies ran while one was open for 0% -> 0% of each run, Pallas kernels for 15% -> 12%
where the time goes in v5:
time: 98.9 us; the launch traced here: 98.8 us
  waiting for transfers between devices  53.9 us (54%)
  starting transfers between devices  25.8 us (26%)
  Pallas kernels  17.6 us (18%)
    ppermute x12, waiting for transfers between devices, send_y(): lax.ppermute(x, 'sp', [(i, i & 9 | ((i >> 1 & 3) + by) % 4 << 1) for i in...  32.6 us
    ppermute x6, waiting for transfers between devices, send_on(): return lax.ppermute(x, ('section', 'sp'), pairs)  19.4 us
    pallas_call x14, Pallas kernels, local_call(): pl.pallas_call(body, out_shape=out_shape, in_specs=specs, out_specs=out_s...  17.6 us
    ppermute x12, starting transfers between devices, send_y(): lax.ppermute(x, 'sp', [(i, i & 9 | ((i >> 1 & 3) + by) % 4 << 1) for i in...  17.4 us
    ppermute x6, starting transfers between devices, send_on(): return lax.ppermute(x, ('section', 'sp'), pairs)  4.09 us
    ppermute x1, starting transfers between devices, send_x(): return lax.ppermute(x, 'sp', [(i, i ^ 8) for i in range(SPAN)])  3.11 us
  transfers between devices with their start and end apart: 29, of which 18 were waited for; matrix products, arithmetic and copies ran while one was open for 0% of the time, Pallas kernels for 12%

profile of v5, /device:TPU:8, one launch (start us, length us, event | category | flops | bytes accessed | tf_op | source)
XLA Modules:
  0.0 98.8 jit_solution(3569708050946675514)
XLA Ops:
  0.6 3.1 %collective-permute-start = (bf16[16,3072]{1,0:T(8,128)(2,1)}, bf16[16,3072]{1,0:T(8,128)(2,1)S(1)}, u32[]{:S(2)}, u32[]{:S(2)}) collective-permute-start(bf16[16,3072]{1,0:T(8,128)(2,1)} %bitcast.14), channel_id=1, source_target_pairs={{0,8},{1,9},{2,10},{3,11},{4,12},{5,13},{6,14},{7,15},{8,0},{9,1},... | collective-permute-start | bytes 294920 | tf_op jit(solution)/shard_map/ppermute | solution.py:38
  3.7 0.7 copy-done.1
  4.4 3.7 %fetch.1 = (bf16[3072,768]{1,0:T(8,128)(2,1)S(1)}, f32[3,3072]{1,0:T(4,128)S(1)}, f32[3,3072]{1,0:T(4,128)S(1)}, bf16[2,4096,128]{2,1,0:T(8,128)(2,1)S(1)}) custom-call(s32[16]{0:T(128)S(1)} %copy-done.1, bf16[3,28,3072]{2,1,0:T(8,128)(2,1)} %bitcast.21, bf16[3,3072,128]{2,1,0:T(8,128)(2,1)} %bitcast.18, bf16[3072,384]{1,0:T(8,128)(2,1)} %bitcast.19, ...), custom_call_target="tpu_custom_call" | custom-call | bytes 7000000 | tf_op jit(solution)/shard_map/fetch/pallas_call | solution.py:79
  8.2 0.3 norm_first.1
  8.4 1.7 %collective-permute-start.4 = (bf16[32,3072]{1,0:T(8,128)(2,1)S(1)}, bf16[32,3072]{1,0:T(8,128)(2,1)S(1)}, u32[]{:S(2)}, u32[]{:S(2)}) collective-permute-start(bf16[32,3072]{1,0:T(8,128)(2,1)S(1)} %get-tuple-element.32.n0), channel_id=1, source_target_pairs={{0,2},{1,3},{2,4},{3,5},{4,6},{5,7},{6,0},{7,1},{8,10},{9,11},{10,... | collective-permute-start | bytes 589832 | tf_op jit(solution)/shard_map/ppermute | solution.py:32
  10.1 0.4 collective-permute-start.3
  10.5 2.3 %collective-permute-start.2 = (bf16[32,3072]{1,0:T(8,128)(2,1)S(1)}, bf16[32,3072]{1,0:T(8,128)(2,1)S(1)}, u32[]{:S(2)}, u32[]{:S(2)}) collective-permute-start(bf16[32,3072]{1,0:T(8,128)(2,1)S(1)} %get-tuple-element.32.n0), channel_id=1, source_target_pairs={{0,4},{1,5},{2,6},{3,7},{4,0},{5,1},{6,2},{7,3},{8,12},{9,13},{10,... | collective-permute-start | bytes 589832 | tf_op jit(solution)/shard_map/ppermute | solution.py:32
  12.8 0.0 collective-permute-start.5
  12.8 3.1 %collective-permute-done.4.n3 = bf16[32,3072]{1,0:T(8,128)(2,1)S(1)} collective-permute-done((bf16[32,3072]{1,0:T(8,128)(2,1)S(1)}, bf16[32,3072]{1,0:T(8,128)(2,1)S(1)}, u32[]{:S(2)}, u32[]{:S(2)}) %collective-permute-start.4) | collective-permute-done | bytes 196640 | tf_op jit(solution)/shard_map/ppermute | solution.py:32
  15.9 0.0 collective-permute-start.8
  15.9 1.3 %collective-permute-done.3.n1 = bf16[32,3072]{1,0:T(8,128)(2,1)S(1)} collective-permute-done((bf16[32,3072]{1,0:T(8,128)(2,1)S(1)}, bf16[32,3072]{1,0:T(8,128)(2,1)S(1)}, u32[]{:S(2)}, u32[]{:S(2)}) %collective-permute-start.3) | collective-permute-done | bytes 196640 | tf_op jit(solution)/shard_map/ppermute | solution.py:32
  17.2 0.0 collective-permute-start.7
  17.2 3.9 %collective-permute-done.2.n2 = bf16[32,3072]{1,0:T(8,128)(2,1)S(1)} collective-permute-done((bf16[32,3072]{1,0:T(8,128)(2,1)S(1)}, bf16[32,3072]{1,0:T(8,128)(2,1)S(1)}, u32[]{:S(2)}, u32[]{:S(2)}) %collective-permute-start.2) | collective-permute-done | bytes 196640 | tf_op jit(solution)/shard_map/ppermute | solution.py:32
  21.1 0.0 collective-permute-start.6
  21.1 0.8 project_own.2.first
  22.0 0.0 collective-permute-done.8.s3
  22.0 0.6 collective-permute-done.6.s2
  22.6 3.7 %block.2 = (bf16[2,4096,128]{2,1,0:T(8,128)(2,1)S(1)}, bf16[256,512]{1,0:T(8,128)(2,1)S(1)}, bf16[128,128]{1,0:T(8,128)(2,1)S(1)}, bf16[128,3072]{1,0:T(8,128)(2,1)S(1)}, bf16[512,3072]{1,0:T(8,128)(2,1)S(1)}) custom-call(s32[16]{0:T(128)S(1)} %copy-done.2, f32[128,768]{1,0:T(8,128)S(1)} %project_own.2.first, ...), custom_call_target="tpu_custom_call", output_to_operand_aliasing={{0}: (8, {})} | custom-call | flops 30000001024 | bytes 12000000 | tf_op jit(solution)/shard_map/block/pallas_call | solution.py:79
  26.2 0.2 collective-permute-start.9
  26.5 1.7 %own_half.2.mine = f32[128,3072]{1,0:T(8,128)S(1)} custom-call(bf16[128,128]{1,0:T(8,128)(2,1)S(1)} %get-tuple-element.35.queries, bf16[2,4096,128]{2,1,0:T(8,128)(2,1)S(1)} %get-tuple-element.36.kv.rest_0_, bf16[256,512]{1,0:T(8,128)(2,1)S(1)} %get-tuple-element.37.joined, bf16[512,3072]{1,0:T(8,128)(2,1)S(1)} %get-tuple-element.38.w2.rest_1_), custom_call_target="tpu_custom_call" | custom-call | flops 12000000000 | bytes 4700000 | tf_op jit(solution)/shard_map/own_half/pallas_call | solution.py:79
  28.2 0.4 collective-permute-done.9.came
  28.6 0.1 pair_sum.2
  28.8 0.2 collective-permute-start.10
  29.0 1.9 %collective-permute-start.11 = (bf16[32,3072]{1,0:T(8,128)(2,1)S(1)}, bf16[32,3072]{1,0:T(8,128)(2,1)S(1)}, u32[]{:S(2)}, u32[]{:S(2)}) collective-permute-start(bf16[32,3072]{1,0:T(8,128)(2,1)S(1)} %get-tuple-element.42), channel_id=1, source_target_pairs={{0,6},{1,7},{2,0},{3,1},{4,2},{5,3},{6,4},{7,5},{8,14},{9,15},{10,... | collective-permute-start | bytes 589832 | tf_op jit(solution)/shard_map/ppermute | solution.py:32
  30.9 1.9 %collective-permute-start.12 = (bf16[32,3072]{1,0:T(8,128)(2,1)S(1)}, bf16[32,3072]{1,0:T(8,128)(2,1)S(1)}, u32[]{:S(2)}, u32[]{:S(2)}) collective-permute-start(bf16[32,3072]{1,0:T(8,128)(2,1)S(1)} %get-tuple-element.43), channel_id=1, source_target_pairs={{0,4},{1,5},{2,6},{3,7},{4,0},{5,1},{6,2},{7,3},{8,12},{9,13},{10,... | collective-permute-start | bytes 589832 | tf_op jit(solution)/shard_map/ppermute | solution.py:32
  32.8 0.6 collective-permute-start.1
  33.3 3.3 %collective-permute-done.10.r1 = bf16[32,3072]{1,0:T(8,128)(2,1)S(1)} collective-permute-done((bf16[32,3072]{1,0:T(8,128)(2,1)S(1)}, bf16[32,3072]{1,0:T(8,128)(2,1)S(1)}, u32[]{:S(2)}, u32[]{:S(2)}) %collective-permute-start.10) | collective-permute-done | bytes 196640 | tf_op jit(solution)/shard_map/ppermute | solution.py:32
  36.6 0.0 collective-permute-done.11.r3
  36.6 5.1 %collective-permute-done.12.r2 = bf16[32,3072]{1,0:T(8,128)(2,1)S(1)} collective-permute-done((bf16[32,3072]{1,0:T(8,128)(2,1)S(1)}, bf16[32,3072]{1,0:T(8,128)(2,1)S(1)}, u32[]{:S(2)}, u32[]{:S(2)}) %collective-permute-start.12) | collective-permute-done | bytes 196640 | tf_op jit(solution)/shard_map/ppermute | solution.py:32
  41.7 0.1 column_sum.1
  41.8 1.2 %collective-permute-start.14 = (bf16[32,3072]{1,0:T(8,128)(2,1)S(1)}, bf16[32,3072]{1,0:T(8,128)(2,1)S(1)}, u32[]{:S(2)}, u32[]{:S(2)}) collective-permute-start(bf16[32,3072]{1,0:T(8,128)(2,1)S(1)} %column_sum.1), channel_id=1, source_target_pairs={{0,24},{1,25},{2,26},{3,27},{4,28},{5,29},{6,30},{7,31},{8,16},{9,... | collective-permute-start | bytes 589832 | tf_op jit(solution)/shard_map/ppermute | solution.py:46
  43.0 1.2 %collective-permute-start.13 = (bf16[32,3072]{1,0:T(8,128)(2,1)S(1)}, bf16[32,3072]{1,0:T(8,128)(2,1)S(1)}, u32[]{:S(2)}, u32[]{:S(2)}) collective-permute-start(bf16[32,3072]{1,0:T(8,128)(2,1)S(1)} %column_sum.1), channel_id=1, source_target_pairs={{0,16},{1,17},{2,18},{3,19},{4,20},{5,21},{6,22},{7,23},{8,24},{9,... | collective-permute-start | bytes 589832 | tf_op jit(solution)/shard_map/ppermute | solution.py:46
  44.2 9.9 %collective-permute-done.14.p1 = bf16[32,3072]{1,0:T(8,128)(2,1)S(1)} collective-permute-done((bf16[32,3072]{1,0:T(8,128)(2,1)S(1)}, bf16[32,3072]{1,0:T(8,128)(2,1)S(1)}, u32[]{:S(2)}, u32[]{:S(2)}) %collective-permute-start.14) | collective-permute-done | bytes 196640 | tf_op jit(solution)/shard_map/ppermute | solution.py:46
  54.1 2.0 %collective-permute-done.13.p0 = bf16[32,3072]{1,0:T(8,128)(2,1)S(1)} collective-permute-done((bf16[32,3072]{1,0:T(8,128)(2,1)S(1)}, bf16[32,3072]{1,0:T(8,128)(2,1)S(1)}, u32[]{:S(2)}, u32[]{:S(2)}) %collective-permute-start.13) | collective-permute-done | bytes 196640 | tf_op jit(solution)/shard_map/ppermute | solution.py:46
  56.1 0.4 norm_next.1
  56.5 0.1 collective-permute-start.18
  56.6 2.0 %collective-permute-start.17 = (bf16[32,3072]{1,0:T(8,128)(2,1)S(1)}, bf16[32,3072]{1,0:T(8,128)(2,1)S(1)}, u32[]{:S(2)}, u32[]{:S(2)}) collective-permute-start(bf16[32,3072]{1,0:T(8,128)(2,1)S(1)} %get-tuple-element.46.n0), channel_id=1, source_target_pairs={{0,6},{1,7},{2,0},{3,1},{4,2},{5,3},{6,4},{7,5},{8,14},{9,15},{10,... | collective-permute-start | bytes 589832 | tf_op jit(solution)/shard_map/ppermute | solution.py:32
  58.6 1.5 %collective-permute-start.16 = (bf16[32,3072]{1,0:T(8,128)(2,1)S(1)}, bf16[32,3072]{1,0:T(8,128)(2,1)S(1)}, u32[]{:S(2)}, u32[]{:S(2)}) collective-permute-start(bf16[32,3072]{1,0:T(8,128)(2,1)S(1)} %get-tuple-element.46.n0), channel_id=1, source_target_pairs={{0,4},{1,5},{2,6},{3,7},{4,0},{5,1},{6,2},{7,3},{8,12},{9,13},{10,... | collective-permute-start | bytes 589832 | tf_op jit(solution)/shard_map/ppermute | solution.py:32
  60.1 4.2 %collective-permute-done.18.n3 = bf16[32,3072]{1,0:T(8,128)(2,1)S(1)} collective-permute-done((bf16[32,3072]{1,0:T(8,128)(2,1)S(1)}, bf16[32,3072]{1,0:T(8,128)(2,1)S(1)}, u32[]{:S(2)}, u32[]{:S(2)}) %collective-permute-start.18) | collective-permute-done | bytes 196640 | tf_op jit(solution)/shard_map/ppermute | solution.py:32
  64.3 0.0 collective-permute-start.22
  64.3 0.5 collective-permute-start.21
  64.8 2.8 %collective-permute-done.16.n2 = bf16[32,3072]{1,0:T(8,128)(2,1)S(1)} collective-permute-done((bf16[32,3072]{1,0:T(8,128)(2,1)S(1)}, bf16[32,3072]{1,0:T(8,128)(2,1)S(1)}, u32[]{:S(2)}, u32[]{:S(2)}) %collective-permute-start.16) | collective-permute-done | bytes 196640 | tf_op jit(solution)/shard_map/ppermute | solution.py:32
  67.6 0.0 collective-permute-start.20
  67.6 0.8 project_own.3.first
  68.5 0.0 collective-permute-done.22.s3
  68.5 0.0 collective-permute-done.21.s1
  68.5 0.6 collective-permute-done.20.s2
  69.1 3.2 %block.3 = (bf16[2,4096,128]{2,1,0:T(8,128)(2,1)S(1)}, bf16[256,512]{1,0:T(8,128)(2,1)S(1)}, bf16[128,128]{1,0:T(8,128)(2,1)S(1)}, bf16[128,3072]{1,0:T(8,128)(2,1)S(1)}, bf16[2,4096,128]{2,1,0:T(8,128)(2,1)}) custom-call(s32[16]{0:T(128)S(1)} %copy-done.2, f32[128,768]{1,0:T(8,128)S(1)} %project_own.3.first, ...), custom_call_target="tpu_custom_call", output_to_operand_aliasing={{0}: (8, {})} | custom-call | flops 30000001024 | bytes 12000000 | tf_op jit(solution)/shard_map/block/pallas_call | solution.py:79
  72.3 0.4 collective-permute-start.23
  72.7 1.7 %own_half.3.mine = f32[128,3072]{1,0:T(8,128)S(1)} custom-call(bf16[128,128]{1,0:T(8,128)(2,1)S(1)} %get-tuple-element.47.queries, bf16[2,4096,128]{2,1,0:T(8,128)(2,1)S(1)} %get-tuple-element.48.kv, bf16[256,512]{1,0:T(8,128)(2,1)S(1)} %get-tuple-element.49.joined, bf16[512,3072]{1,0:T(8,128)(2,1)S(1)} %get-tuple-element.38.w2.rest_1_), custom_call_target="tpu_custom_call" | custom-call | flops 12000000000 | bytes 4700000 | tf_op jit(solution)/shard_map/own_half/pallas_call | solution.py:79
  74.5 0.4 collective-permute-done.23.came
  74.9 0.1 pair_sum.3
  75.0 0.3 collective-permute-start.24
  75.4 1.8 %collective-permute-start.25 = (bf16[32,3072]{1,0:T(8,128)(2,1)S(1)}, bf16[32,3072]{1,0:T(8,128)(2,1)S(1)}, u32[]{:S(2)}, u32[]{:S(2)}) collective-permute-start(bf16[32,3072]{1,0:T(8,128)(2,1)S(1)} %get-tuple-element.53), channel_id=1, source_target_pairs={{0,6},{1,7},{2,0},{3,1},{4,2},{5,3},{6,4},{7,5},{8,14},{9,15},{10,... | collective-permute-start | bytes 589832 | tf_op jit(solution)/shard_map/ppermute | solution.py:32
  77.1 3.2 %collective-permute-start.26 = (bf16[32,3072]{1,0:T(8,128)(2,1)S(1)}, bf16[32,3072]{1,0:T(8,128)(2,1)S(1)}, u32[]{:S(2)}, u32[]{:S(2)}) collective-permute-start(bf16[32,3072]{1,0:T(8,128)(2,1)S(1)} %get-tuple-element.54), channel_id=1, source_target_pairs={{0,4},{1,5},{2,6},{3,7},{4,0},{5,1},{6,2},{7,3},{8,12},{9,13},{10,... | collective-permute-start | bytes 589832 | tf_op jit(solution)/shard_map/ppermute | solution.py:32
  80.4 2.5 %collective-permute-done.24.r1 = bf16[32,3072]{1,0:T(8,128)(2,1)S(1)} collective-permute-done((bf16[32,3072]{1,0:T(8,128)(2,1)S(1)}, bf16[32,3072]{1,0:T(8,128)(2,1)S(1)}, u32[]{:S(2)}, u32[]{:S(2)}) %collective-permute-start.24) | collective-permute-done | bytes 196640 | tf_op jit(solution)/shard_map/ppermute | solution.py:32
  82.8 1.1 %collective-permute-done.25.r3 = bf16[32,3072]{1,0:T(8,128)(2,1)S(1)} collective-permute-done((bf16[32,3072]{1,0:T(8,128)(2,1)S(1)}, bf16[32,3072]{1,0:T(8,128)(2,1)S(1)}, u32[]{:S(2)}, u32[]{:S(2)}) %collective-permute-start.25) | collective-permute-done | bytes 196640 | tf_op jit(solution)/shard_map/ppermute | solution.py:32
  83.9 5.4 %collective-permute-done.26.r2 = bf16[32,3072]{1,0:T(8,128)(2,1)S(1)} collective-permute-done((bf16[32,3072]{1,0:T(8,128)(2,1)S(1)}, bf16[32,3072]{1,0:T(8,128)(2,1)S(1)}, u32[]{:S(2)}, u32[]{:S(2)}) %collective-permute-start.26) | collective-permute-done | bytes 196640 | tf_op jit(solution)/shard_map/ppermute | solution.py:32
  89.3 0.1 column_last.1
  89.4 0.1 collective-permute-start.27
  89.5 1.1 %collective-permute-start.28 = (bf16[16,3072]{1,0:T(8,128)(2,1)S(1)}, bf16[16,3072]{1,0:T(8,128)(2,1)S(1)}, u32[]{:S(2)}, u32[]{:S(2)}) collective-permute-start(bf16[16,3072]{1,0:T(8,128)(2,1)S(1)} %get-tuple-element.56), channel_id=1, source_target_pairs={{0,24},{1,25},{2,26},{3,27},{4,28},{5,29},{6,30},{7,31},{8,16},{9,... | collective-permute-start | bytes 294920 | tf_op jit(solution)/shard_map/ppermute | solution.py:46
  90.6 5.9 %collective-permute-done.27.p0 = bf16[16,3072]{1,0:T(8,128)(2,1)S(1)} collective-permute-done((bf16[16,3072]{1,0:T(8,128)(2,1)S(1)}, bf16[16,3072]{1,0:T(8,128)(2,1)S(1)}, u32[]{:S(2)}, u32[]{:S(2)}) %collective-permute-start.27) | collective-permute-done | bytes 98336 | tf_op jit(solution)/shard_map/ppermute | solution.py:46
  96.5 1.6 %collective-permute-done.28.p1 = bf16[16,3072]{1,0:T(8,128)(2,1)S(1)} collective-permute-done((bf16[16,3072]{1,0:T(8,128)(2,1)S(1)}, bf16[16,3072]{1,0:T(8,128)(2,1)S(1)}, u32[]{:S(2)}, u32[]{:S(2)}) %collective-permute-start.28) | collective-permute-done | bytes 98336 | tf_op jit(solution)/shard_map/ppermute | solution.py:46
  98.1 0.7 residual_last.1
  (16 shorter events, 0.0 us)
Async XLA Ops:
  0.6 7.5 %collective-permute-start = (bf16[16,3072]{1,0:T(8,128)(2,1)}, bf16[16,3072]{1,0:T(8,128)(2,1)S(1)}, u32[]{:S(2)}, u32[]{:S(2)}) collective-permute-start(bf16[16,3072]{1,0:T(8,128)(2,1)} %bitcast.14), channel_id=1, source_target_pairs={{0,8},{1,9},{2,10},{3,11},{4,12},{5,13},{6,14},{7,15},{8,0},{9,1},... | collective-permute-start | bytes 294920 | tf_op jit(solution)/shard_map/ppermute | solution.py:38
  3.7 0.7 copy-start.1
  4.4 3.7 %copy-start = (bf16[1,16,3072]{2,1,0:T(8,128)(2,1)S(1)}, bf16[1,16,3072]{2,1,0:T(8,128)(2,1)}, u32[]{:S(2)}) copy-start(bf16[1,16,3072]{2,1,0:T(8,128)(2,1)} %param.10) | copy-start | bytes 294916
  8.4 7.5 %collective-permute-start.4 = (bf16[32,3072]{1,0:T(8,128)(2,1)S(1)}, bf16[32,3072]{1,0:T(8,128)(2,1)S(1)}, u32[]{:S(2)}, u32[]{:S(2)}) collective-permute-start(bf16[32,3072]{1,0:T(8,128)(2,1)S(1)} %get-tuple-element.32.n0), channel_id=1, source_target_pairs={{0,2},{1,3},{2,4},{3,5},{4,6},{5,7},{6,0},{7,1},{8,10},{9,11},{10,... | collective-permute-start | bytes 589832 | tf_op jit(solution)/shard_map/ppermute | solution.py:32
  10.1 7.1 %collective-permute-start.3 = (bf16[32,3072]{1,0:T(8,128)(2,1)S(1)}, bf16[32,3072]{1,0:T(8,128)(2,1)S(1)}, u32[]{:S(2)}, u32[]{:S(2)}) collective-permute-start(bf16[32,3072]{1,0:T(8,128)(2,1)S(1)} %get-tuple-element.32.n0), channel_id=1, source_target_pairs={{0,6},{1,7},{2,0},{3,1},{4,2},{5,3},{6,4},{7,5},{8,14},{9,15},{10,... | collective-permute-start | bytes 589832 | tf_op jit(solution)/shard_map/ppermute | solution.py:32
  10.5 10.6 %collective-permute-start.2 = (bf16[32,3072]{1,0:T(8,128)(2,1)S(1)}, bf16[32,3072]{1,0:T(8,128)(2,1)S(1)}, u32[]{:S(2)}, u32[]{:S(2)}) collective-permute-start(bf16[32,3072]{1,0:T(8,128)(2,1)S(1)} %get-tuple-element.32.n0), channel_id=1, source_target_pairs={{0,4},{1,5},{2,6},{3,7},{4,0},{5,1},{6,2},{7,3},{8,12},{9,13},{10,... | collective-permute-start | bytes 589832 | tf_op jit(solution)/shard_map/ppermute | solution.py:32
  12.8 9.1 %collective-permute-start.5 = (bf16[32,3072]{1,0:T(8,128)(2,1)S(1)}, bf16[32,3072]{1,0:T(8,128)(2,1)S(1)}, u32[]{:S(2)}, u32[]{:S(2)}) collective-permute-start(bf16[32,3072]{1,0:T(8,128)(2,1)S(1)} %get-tuple-element.32.n0), channel_id=1, source_target_pairs={{0,1},{1,0},{2,3},{3,2},{4,5},{5,4},{6,7},{7,6},{8,9},{9,8},{10,11... | collective-permute-start | bytes 589832 | tf_op jit(solution)/shard_map/ppermute | solution.py:28
  15.9 6.0 %collective-permute-start.8 = (bf16[32,3072]{1,0:T(8,128)(2,1)S(1)}, bf16[32,3072]{1,0:T(8,128)(2,1)S(1)}, u32[]{:S(2)}, u32[]{:S(2)}) collective-permute-start(bf16[32,3072]{1,0:T(8,128)(2,1)S(1)} %collective-permute-done.4.n3), channel_id=1, source_target_pairs={{0,1},{1,0},{2,3},{3,2},{4,5},{5,4},{6,7},{7,6},{8,9},{9,8},{10,11... | collective-permute-start | bytes 589832 | tf_op jit(solution)/shard_map/ppermute | solution.py:28
  17.2 4.8 %collective-permute-start.7 = (bf16[32,3072]{1,0:T(8,128)(2,1)S(1)}, bf16[32,3072]{1,0:T(8,128)(2,1)S(1)}, u32[]{:S(2)}, u32[]{:S(2)}) collective-permute-start(bf16[32,3072]{1,0:T(8,128)(2,1)S(1)} %collective-permute-done.3.n1), channel_id=1, source_target_pairs={{0,1},{1,0},{2,3},{3,2},{4,5},{5,4},{6,7},{7,6},{8,9},{9,8},{10,11... | collective-permute-start | bytes 589832 | tf_op jit(solution)/shard_map/ppermute | solution.py:28
  21.1 1.4 %collective-permute-start.6 = (bf16[32,3072]{1,0:T(8,128)(2,1)S(1)}, bf16[32,3072]{1,0:T(8,128)(2,1)S(1)}, u32[]{:S(2)}, u32[]{:S(2)}) collective-permute-start(bf16[32,3072]{1,0:T(8,128)(2,1)S(1)} %collective-permute-done.2.n2), channel_id=1, source_target_pairs={{0,1},{1,0},{2,3},{3,2},{4,5},{5,4},{6,7},{7,6},{8,9},{9,8},{10,11... | collective-permute-start | bytes 589832 | tf_op jit(solution)/shard_map/ppermute | solution.py:28
  21.1 1.4 %copy-start.2 = (s32[16]{0:T(128)S(1)}, s32[16]{0:T(128)}, u32[]{:S(2)}) copy-start(s32[16]{0:T(128)} %patches.3) | copy-start | bytes 196
  21.1 1.4 %copy-start.3 = (bf16[1,2,128]{2,1,0:T(2,128)(2,1)S(1)}, bf16[1,2,128]{2,1,0:T(2,128)(2,1)}, u32[]{:S(2)}) copy-start(bf16[1,2,128]{2,1,0:T(2,128)(2,1)} %param.15) | copy-start | bytes 1540
  26.2 2.4 %collective-permute-start.9 = (bf16[128,3072]{1,0:T(8,128)(2,1)S(1)}, bf16[128,3072]{1,0:T(8,128)(2,1)S(1)}, u32[]{:S(2)}, u32[]{:S(2)}) collective-permute-start(bf16[128,3072]{1,0:T(8,128)(2,1)S(1)} %get-tuple-element.39), channel_id=1, source_target_pairs={{0,1},{1,0},{2,3},{3,2},{4,5},{5,4},{6,7},{7,6},{8,9},{9,8},{10,11... | collective-permute-start | bytes 2359304 | tf_op jit(solution)/shard_map/ppermute | solution.py:28
  28.8 7.8 %collective-permute-start.10 = (bf16[32,3072]{1,0:T(8,128)(2,1)S(1)}, bf16[32,3072]{1,0:T(8,128)(2,1)S(1)}, u32[]{:S(2)}, u32[]{:S(2)}) collective-permute-start(bf16[32,3072]{1,0:T(8,128)(2,1)S(1)} %get-tuple-element.41), channel_id=1, source_target_pairs={{0,2},{1,3},{2,4},{3,5},{4,6},{5,7},{6,0},{7,1},{8,10},{9,11},{10,... | collective-permute-start | bytes 589832 | tf_op jit(solution)/shard_map/ppermute | solution.py:32
  29.0 7.6 %collective-permute-start.11 = (bf16[32,3072]{1,0:T(8,128)(2,1)S(1)}, bf16[32,3072]{1,0:T(8,128)(2,1)S(1)}, u32[]{:S(2)}, u32[]{:S(2)}) collective-permute-start(bf16[32,3072]{1,0:T(8,128)(2,1)S(1)} %get-tuple-element.42), channel_id=1, source_target_pairs={{0,6},{1,7},{2,0},{3,1},{4,2},{5,3},{6,4},{7,5},{8,14},{9,15},{10,... | collective-permute-start | bytes 589832 | tf_op jit(solution)/shard_map/ppermute | solution.py:32
  30.9 10.9 %collective-permute-start.12 = (bf16[32,3072]{1,0:T(8,128)(2,1)S(1)}, bf16[32,3072]{1,0:T(8,128)(2,1)S(1)}, u32[]{:S(2)}, u32[]{:S(2)}) collective-permute-start(bf16[32,3072]{1,0:T(8,128)(2,1)S(1)} %get-tuple-element.43), channel_id=1, source_target_pairs={{0,4},{1,5},{2,6},{3,7},{4,0},{5,1},{6,2},{7,3},{8,12},{9,13},{10,... | collective-permute-start | bytes 589832 | tf_op jit(solution)/shard_map/ppermute | solution.py:32
  32.8 11.5 %collective-permute-start.1 = (bf16[32,3072]{1,0:T(8,128)(2,1)S(1)}, bf16[32,3072]{1,0:T(8,128)(2,1)S(1)}, u32[]{:S(2)}, u32[]{:S(2)}) collective-permute-start(bf16[32,3072]{1,0:T(8,128)(2,1)S(1)} %get-tuple-element.31), channel_id=1, source_target_pairs={{0,16},{1,17},{2,18},{3,19},{4,20},{5,21},{6,22},{7,23},{8,24},{9,... | collective-permute-start | bytes 589832 | tf_op jit(solution)/shard_map/ppermute | solution.py:46
  41.8 12.3 %collective-permute-start.14 = (bf16[32,3072]{1,0:T(8,128)(2,1)S(1)}, bf16[32,3072]{1,0:T(8,128)(2,1)S(1)}, u32[]{:S(2)}, u32[]{:S(2)}) collective-permute-start(bf16[32,3072]{1,0:T(8,128)(2,1)S(1)} %column_sum.1), channel_id=1, source_target_pairs={{0,24},{1,25},{2,26},{3,27},{4,28},{5,29},{6,30},{7,31},{8,16},{9,... | collective-permute-start | bytes 589832 | tf_op jit(solution)/shard_map/ppermute | solution.py:46
  43.0 13.1 %collective-permute-start.13 = (bf16[32,3072]{1,0:T(8,128)(2,1)S(1)}, bf16[32,3072]{1,0:T(8,128)(2,1)S(1)}, u32[]{:S(2)}, u32[]{:S(2)}) collective-permute-start(bf16[32,3072]{1,0:T(8,128)(2,1)S(1)} %column_sum.1), channel_id=1, source_target_pairs={{0,16},{1,17},{2,18},{3,19},{4,20},{5,21},{6,22},{7,23},{8,24},{9,... | collective-permute-start | bytes 589832 | tf_op jit(solution)/shard_map/ppermute | solution.py:46
  56.5 7.8 %collective-permute-start.18 = (bf16[32,3072]{1,0:T(8,128)(2,1)S(1)}, bf16[32,3072]{1,0:T(8,128)(2,1)S(1)}, u32[]{:S(2)}, u32[]{:S(2)}) collective-permute-start(bf16[32,3072]{1,0:T(8,128)(2,1)S(1)} %get-tuple-element.46.n0), channel_id=1, source_target_pairs={{0,2},{1,3},{2,4},{3,5},{4,6},{5,7},{6,0},{7,1},{8,10},{9,11},{10,... | collective-permute-start | bytes 589832 | tf_op jit(solution)/shard_map/ppermute | solution.py:32
  56.6 7.7 %collective-permute-start.17 = (bf16[32,3072]{1,0:T(8,128)(2,1)S(1)}, bf16[32,3072]{1,0:T(8,128)(2,1)S(1)}, u32[]{:S(2)}, u32[]{:S(2)}) collective-permute-start(bf16[32,3072]{1,0:T(8,128)(2,1)S(1)} %get-tuple-element.46.n0), channel_id=1, source_target_pairs={{0,6},{1,7},{2,0},{3,1},{4,2},{5,3},{6,4},{7,5},{8,14},{9,15},{10,... | collective-permute-start | bytes 589832 | tf_op jit(solution)/shard_map/ppermute | solution.py:32
  58.6 9.0 %collective-permute-start.16 = (bf16[32,3072]{1,0:T(8,128)(2,1)S(1)}, bf16[32,3072]{1,0:T(8,128)(2,1)S(1)}, u32[]{:S(2)}, u32[]{:S(2)}) collective-permute-start(bf16[32,3072]{1,0:T(8,128)(2,1)S(1)} %get-tuple-element.46.n0), channel_id=1, source_target_pairs={{0,4},{1,5},{2,6},{3,7},{4,0},{5,1},{6,2},{7,3},{8,12},{9,13},{10,... | collective-permute-start | bytes 589832 | tf_op jit(solution)/shard_map/ppermute | solution.py:32
  60.1 8.3 %collective-permute-start.19 = (bf16[32,3072]{1,0:T(8,128)(2,1)S(1)}, bf16[32,3072]{1,0:T(8,128)(2,1)S(1)}, u32[]{:S(2)}, u32[]{:S(2)}) collective-permute-start(bf16[32,3072]{1,0:T(8,128)(2,1)S(1)} %get-tuple-element.46.n0), channel_id=1, source_target_pairs={{0,1},{1,0},{2,3},{3,2},{4,5},{5,4},{6,7},{7,6},{8,9},{9,8},{10,11... | collective-permute-start | bytes 589832 | tf_op jit(solution)/shard_map/ppermute | solution.py:28
  60.1 14.3 %collective-permute-start.15 = (bf16[16,3072]{1,0:T(8,128)(2,1)S(1)}, bf16[16,3072]{1,0:T(8,128)(2,1)S(1)}, u32[]{:S(2)}, u32[]{:S(2)}) collective-permute-start(bf16[16,3072]{1,0:T(8,128)(2,1)S(1)} %get-tuple-element.45), channel_id=1, source_target_pairs={{0,16},{1,17},{2,18},{3,19},{4,20},{5,21},{6,22},{7,23},{8,24},{9,... | collective-permute-start | bytes 294920 | tf_op jit(solution)/shard_map/ppermute | solution.py:46
  64.3 4.2 %collective-permute-start.22 = (bf16[32,3072]{1,0:T(8,128)(2,1)S(1)}, bf16[32,3072]{1,0:T(8,128)(2,1)S(1)}, u32[]{:S(2)}, u32[]{:S(2)}) collective-permute-start(bf16[32,3072]{1,0:T(8,128)(2,1)S(1)} %collective-permute-done.18.n3), channel_id=1, source_target_pairs={{0,1},{1,0},{2,3},{3,2},{4,5},{5,4},{6,7},{7,6},{8,9},{9,8},{10,11... | collective-permute-start | bytes 589832 | tf_op jit(solution)/shard_map/ppermute | solution.py:28
  64.3 4.2 %collective-permute-start.21 = (bf16[32,3072]{1,0:T(8,128)(2,1)S(1)}, bf16[32,3072]{1,0:T(8,128)(2,1)S(1)}, u32[]{:S(2)}, u32[]{:S(2)}) collective-permute-start(bf16[32,3072]{1,0:T(8,128)(2,1)S(1)} %collective-permute-done.17.n1), channel_id=1, source_target_pairs={{0,1},{1,0},{2,3},{3,2},{4,5},{5,4},{6,7},{7,6},{8,9},{9,8},{10,11... | collective-permute-start | bytes 589832 | tf_op jit(solution)/shard_map/ppermute | solution.py:28
  67.6 1.4 %collective-permute-start.20 = (bf16[32,3072]{1,0:T(8,128)(2,1)S(1)}, bf16[32,3072]{1,0:T(8,128)(2,1)S(1)}, u32[]{:S(2)}, u32[]{:S(2)}) collective-permute-start(bf16[32,3072]{1,0:T(8,128)(2,1)S(1)} %collective-permute-done.16.n2), channel_id=1, source_target_pairs={{0,1},{1,0},{2,3},{3,2},{4,5},{5,4},{6,7},{7,6},{8,9},{9,8},{10,11... | collective-permute-start | bytes 589832 | tf_op jit(solution)/shard_map/ppermute | solution.py:28
  72.3 2.6 %collective-permute-start.23 = (bf16[128,3072]{1,0:T(8,128)(2,1)S(1)}, bf16[128,3072]{1,0:T(8,128)(2,1)S(1)}, u32[]{:S(2)}, u32[]{:S(2)}) collective-permute-start(bf16[128,3072]{1,0:T(8,128)(2,1)S(1)} %get-tuple-element.50), channel_id=1, source_target_pairs={{0,1},{1,0},{2,3},{3,2},{4,5},{5,4},{6,7},{7,6},{8,9},{9,8},{10,11... | collective-permute-start | bytes 2359304 | tf_op jit(solution)/shard_map/ppermute | solution.py:28
  75.0 7.8 %collective-permute-start.24 = (bf16[32,3072]{1,0:T(8,128)(2,1)S(1)}, bf16[32,3072]{1,0:T(8,128)(2,1)S(1)}, u32[]{:S(2)}, u32[]{:S(2)}) collective-permute-start(bf16[32,3072]{1,0:T(8,128)(2,1)S(1)} %get-tuple-element.52), channel_id=1, source_target_pairs={{0,2},{1,3},{2,4},{3,5},{4,6},{5,7},{6,0},{7,1},{8,10},{9,11},{10,... | collective-permute-start | bytes 589832 | tf_op jit(solution)/shard_map/ppermute | solution.py:32
  75.4 8.6 %collective-permute-start.25 = (bf16[32,3072]{1,0:T(8,128)(2,1)S(1)}, bf16[32,3072]{1,0:T(8,128)(2,1)S(1)}, u32[]{:S(2)}, u32[]{:S(2)}) collective-permute-start(bf16[32,3072]{1,0:T(8,128)(2,1)S(1)} %get-tuple-element.53), channel_id=1, source_target_pairs={{0,6},{1,7},{2,0},{3,1},{4,2},{5,3},{6,4},{7,5},{8,14},{9,15},{10,... | collective-permute-start | bytes 589832 | tf_op jit(solution)/shard_map/ppermute | solution.py:32
  77.1 12.2 %collective-permute-start.26 = (bf16[32,3072]{1,0:T(8,128)(2,1)S(1)}, bf16[32,3072]{1,0:T(8,128)(2,1)S(1)}, u32[]{:S(2)}, u32[]{:S(2)}) collective-permute-start(bf16[32,3072]{1,0:T(8,128)(2,1)S(1)} %get-tuple-element.54), channel_id=1, source_target_pairs={{0,4},{1,5},{2,6},{3,7},{4,0},{5,1},{6,2},{7,3},{8,12},{9,13},{10,... | collective-permute-start | bytes 589832 | tf_op jit(solution)/shard_map/ppermute | solution.py:32
  89.4 7.0 %collective-permute-start.27 = (bf16[16,3072]{1,0:T(8,128)(2,1)S(1)}, bf16[16,3072]{1,0:T(8,128)(2,1)S(1)}, u32[]{:S(2)}, u32[]{:S(2)}) collective-permute-start(bf16[16,3072]{1,0:T(8,128)(2,1)S(1)} %get-tuple-element.55), channel_id=1, source_target_pairs={{0,16},{1,17},{2,18},{3,19},{4,20},{5,21},{6,22},{7,23},{8,24},{9,... | collective-permute-start | bytes 294920 | tf_op jit(solution)/shard_map/ppermute | solution.py:46
  89.5 8.6 %collective-permute-start.28 = (bf16[16,3072]{1,0:T(8,128)(2,1)S(1)}, bf16[16,3072]{1,0:T(8,128)(2,1)S(1)}, u32[]{:S(2)}, u32[]{:S(2)}) collective-permute-start(bf16[16,3072]{1,0:T(8,128)(2,1)S(1)} %get-tuple-element.56), channel_id=1, source_target_pairs={{0,24},{1,25},{2,26},{3,27},{4,28},{5,29},{6,30},{7,31},{8,16},{9,... | collective-permute-start | bytes 294920 | tf_op jit(solution)/shard_map/ppermute | solution.py:46
